TPU v7x, 128 devices: a whole 4x4x4 slice. The times are simulated.
128 devices in a mesh: section: 8 (over y, core), ep: 16 (over z, x).
Axes of the slice: x: 4, y: 4, z: 4, core: 2. Of those that a mesh axis runs over, the one named last changes fastest.
Arguments:
- rows_in: bfloat16 [4, 128, 7168], P(None, 'ep'), may hold values from -6 to 6
- routes: int32 [8, 4, 128, 2], P('section', None, 'ep'), may hold values from 0 to 7, all different within a row; in each aligned block of 8 rows (0 to 7, 8 to 15, ..., all dimensions but the last counted through in order) at most 4 rows name the same one
- hot_blocks: int32 [8], P('section'), may hold values from 0 to 31
- gains: float32 [8, 7168], P('section'), may hold values from 0.1 to 1.9
- router: bfloat16 [8, 7168, 8], P('section'), may hold values from -0.0625 to 0.0625
- w_gate: bfloat16 [8, 7168, 8192], P('section', None, 'ep'), may hold values from -0.0625 to 0.0625
- w_up: bfloat16 [8, 7168, 8192], P('section', None, 'ep'), may hold values from -0.0625 to 0.0625
- w_down: bfloat16 [8, 8192, 7168], P('section', 'ep'), may hold values from -0.1875 to 0.1875
Outputs:
- section_rows: bfloat16 [8, 4, 128, 7168], P('section', None, 'ep')
- relative_load: float32 [8, 16], P('section', 'ep')
Inputs may be any that keep to these rules, and one draw needn't show every extreme that they name: `routes`: in every layer and micro-batch the 8 rows of one device name each expert at most 4 times.
All inputs are finite; a program needn't handle non-finite values.
Results may differ from a plain program's by a relative error of at most 0.025.
Values may be sent and summed in bfloat16 or wider, within the bound.
No kernel may reach another device: no remote copies, remote signals or barrier semaphores. Data moves between devices by JAX's collectives and lax.ppermute only.
A program may use at most 128 MiB of HBM per device.

v0:
```python
import jax
import jax.numpy as jnp
from jax import lax
from jax.sharding import PartitionSpec as P

FFW = 1024
BLK = 256


def spread(block, axis, source):
    block = jnp.where(lax.axis_index(axis) == source, block, jnp.zeros_like(block))
    return lax.psum(block, axis)


def shifted(block, axis, distance):
    devices = range(lax.axis_size(axis))
    route = [(i - distance, i) for i in devices if i - distance in devices]
    return lax.ppermute(block, axis, route)


def local(rows_in, routes, hot_blocks, gains, router, w_gate, w_up, w_down):
    section_index = lax.axis_index("section")
    ep_index = lax.axis_index("ep")
    section_count = lax.axis_size("section")
    micro_count = rows_in.shape[0]
    tok_rows = rows_in.shape[1]
    model_width = rows_in.shape[2]
    columns = w_gate.shape[2]
    expert_count = router.shape[2]
    top_count = routes.shape[3]
    capacity = tok_rows // 2
    blocks_per_expert = FFW // BLK
    hot_index = hot_blocks[0]
    owner_index = hot_index // 2
    hot_expert = hot_index // blocks_per_expert
    norm_gain = gains[0]
    router_w = router[0]
    gate_w = w_gate[0]
    up_w = w_up[0]
    down_w = w_down[0]
    column_block = 2 * ep_index + lax.iota(jnp.int32, columns) // BLK
    keep_column = (column_block != hot_index)[None, :]
    expert_ids = lax.iota(jnp.int32, expert_count)
    block_start = hot_index % 2 * BLK
    copy_gate, copy_up, copy_down = (
        spread(lax.dynamic_slice_in_dim(gate_w, block_start, BLK, 1), "ep", owner_index),
        spread(lax.dynamic_slice_in_dim(up_w, block_start, BLK, 1), "ep", owner_index),
        spread(lax.dynamic_slice_in_dim(down_w, block_start, BLK, 0), "ep", owner_index),
    )

    def expert_rows(flat_rows):
        gate_value = jnp.dot(flat_rows, gate_w, preferred_element_type=jnp.float32)
        up_value = jnp.dot(flat_rows, up_w, preferred_element_type=jnp.float32)
        activation = (jax.nn.silu(gate_value) * up_value).astype(jnp.bfloat16)
        home_act = jnp.where(keep_column, activation, jnp.zeros_like(activation))
        return jnp.dot(home_act, down_w, preferred_element_type=jnp.float32).astype(jnp.bfloat16)

    def work_both(recv_parts):
        recv_rows, recv_flags = recv_parts
        sources = recv_rows.shape[0]
        item_count = recv_rows.shape[1]
        home_part = expert_rows(recv_rows.reshape(sources * item_count, model_width))
        home_part = home_part.reshape(sources, item_count, model_width)
        returned = lax.all_to_all(home_part, "ep", split_axis=0, concat_axis=0, tiled=True)
        filled = jnp.sum(recv_flags.astype(jnp.float32), axis=0, keepdims=True)
        return (returned, filled)

    def apply_layer(layer_input, route_ids):
        rows_float = layer_input.astype(jnp.float32)
        mean_square = jnp.mean(rows_float * rows_float, axis=-1, keepdims=True)
        normed = (rows_float * lax.rsqrt(mean_square + 1e-06) * norm_gain).astype(jnp.bfloat16)
        scores = jax.nn.sigmoid(jnp.dot(normed, router_w, preferred_element_type=jnp.float32))
        member = (route_ids[:, :, None] == expert_ids[None, None, :]).astype(jnp.float32)
        chosen = jnp.sum(member * scores[:, None, :], axis=2)
        gate_weights = 2.5 * chosen / jnp.sum(chosen, axis=1, keepdims=True)
        token_gate = jnp.sum(member * gate_weights[:, :, None], axis=1)
        routed = jnp.sum(member, axis=1)
        slot_rank = jnp.cumsum(routed, axis=0) - routed
        slot_ids = lax.iota(jnp.float32, capacity)
        placement = routed.T[:, None, :] * (
            slot_rank.T[:, None, :] == slot_ids[None, :, None]
        ).astype(jnp.float32)
        packed = jnp.einsum(
            "ect,tf->ecf",
            placement.astype(jnp.bfloat16),
            normed,
            preferred_element_type=jnp.float32,
        ).astype(jnp.bfloat16)
        slot_flags = jnp.sum(placement, axis=2).astype(jnp.bfloat16)
        send_rows = jnp.repeat(packed, 2, axis=0)
        send_flags = jnp.repeat(slot_flags, 2, axis=0)
        home_back, filled = work_both(
            (
                lax.all_to_all(send_rows, "ep", split_axis=0, concat_axis=0, tiled=True),
                lax.all_to_all(send_flags, "ep", split_axis=0, concat_axis=0, tiled=True),
            )
        )
        combined = home_back.astype(jnp.float32).reshape(expert_count, 2, capacity, model_width)
        pair_sum = combined[:, 0] + combined[:, 1]
        weighting = placement * token_gate.T[:, None, :]
        routed_sum = jnp.einsum("ect,ecf->tf", weighting, pair_sum, precision=lax.Precision.HIGHEST)
        local_gate = jnp.dot(normed, copy_gate, preferred_element_type=jnp.float32)
        local_up = jnp.dot(normed, copy_up, preferred_element_type=jnp.float32)
        local_act = (jax.nn.silu(local_gate) * local_up).astype(jnp.bfloat16)
        local_part = (
            jnp.dot(local_act, copy_down, preferred_element_type=jnp.float32)
            .astype(jnp.bfloat16)
            .astype(jnp.float32)
        )
        hot_gate = jnp.sum(jnp.where((expert_ids == hot_expert)[None, :], token_gate, 0.0), axis=1)
        routed_sum = routed_sum + hot_gate[:, None] * local_part
        own_hot = jnp.sum(jnp.where((expert_ids == hot_expert)[None, :], routed, 0.0))
        return ((rows_float + routed_sum).astype(jnp.bfloat16), jnp.sum(filled), own_hot)

    def run_tick(tick_index, loop_state):
        incoming, outputs, home_total, hot_total = loop_state
        micro_index = tick_index - section_index
        is_live = (micro_index >= 0) & (micro_index < micro_count)
        clipped = jnp.clip(micro_index, 0, micro_count - 1)
        fresh_rows = lax.dynamic_index_in_dim(rows_in, clipped, 0, keepdims=False)
        layer_input = jnp.where(section_index == 0, fresh_rows, incoming)
        route_ids = lax.dynamic_index_in_dim(routes[0], clipped, 0, keepdims=False)
        next_rows, home_rows, hot_rows = apply_layer(layer_input, route_ids)
        updated = lax.dynamic_update_index_in_dim(outputs, next_rows, clipped, 0)
        outputs = jnp.where(is_live, updated, outputs)
        home_total = home_total + jnp.where(is_live, home_rows, 0.0)
        hot_total = hot_total + jnp.where(is_live, hot_rows, 0.0)
        incoming = shifted(next_rows, "section", 1)
        return (incoming, outputs, home_total, hot_total)

    tick_count = micro_count + section_count - 1
    start_state = (
        jnp.zeros((tok_rows, model_width), jnp.bfloat16),
        jnp.zeros(rows_in.shape, jnp.bfloat16),
        jnp.float32(0.0),
        jnp.float32(0.0),
    )
    final_state = lax.fori_loop(0, tick_count, run_tick, start_state)
    outputs = final_state[1]
    unit_count = (
        final_state[2] * (2.0 - (owner_index == ep_index).astype(jnp.float32)) + final_state[3]
    )
    relative = unit_count / float(micro_count * tok_rows * top_count * blocks_per_expert)
    return (outputs[None], relative.reshape(1, 1))


def solution(mesh):
    return jax.shard_map(
        local,
        mesh=mesh,
        in_specs=(
            P(None, "ep", None),
            P("section", None, "ep", None),
            P("section"),
            P("section", None),
            P("section", None, None),
            P("section", None, "ep"),
            P("section", None, "ep"),
            P("section", "ep", None),
        ),
        out_specs=(P("section", None, "ep", None), P("section", "ep")),
        check_vma=False,
    )
```

profile of v0, /device:TPU:0, one launch (start us, length us, event | category | flops | bytes accessed | tf_op | source)
XLA Modules:
  0.0 965.8 jit_solution(9492379663822661273)
XLA Ops:
  12.7 6.3 select_bitcast_fusion.1
  19.1 167.6 %all-reduce.3.cloned.1.call-done = (bf16[7168,256]{1,0:T(8,128)(2,1)}, bf16[7168,256]{1,0:T(8,128)(2,1)}, bf16[256,7168]{1,0:T(8,128)(2,1)}) async-done(((bf16[7168,256]{1,0:T(8,128)(2,1)}, bf16[7168,256]{1,0:T(8,128)(2,1)}, bf16[256,7168]{1,0:T(8,128)(2,1)}), (bf16[7168,256]{1,0:T(8,128)(2,1)}, bf16[7168,256]{1,0:T(8,128)(2,1)}, bf16[256,7168]{1,0:T(8,128)(2,1)})) %all-reduce.3.cloned.1.call-update) | async-done | bytes 11010064 | tf_op jit(solution)/shard_map/psum | solution.py:12
  186.8 770.2 %while.22 = (s32[]{:T(128)}, bf16[8,7168]{1,0:T(8,128)(2,1)S(1)}, bf16[4,8,7168]{2,1,0:T(8,128)(2,1)S(1)}, f32[]{:T(128)}, f32[]{:T(128)}, /*index=5*/pred[]{:T(...) while((s32[]{:T(128)}, bf16[8,7168]{1,0:T(8,128)(2,1)S(1)}, ...), condition=%wide.region_14.15_spmd.clone.clone, body=%wide.region_3.14_spmd.clone.clone.sunk | while | flops 1527207040 | bytes 56855520 | solution.py:138
  191.0 5.3 all-to-all-start
  197.1 15.3 %all-to-all-done = bf16[16,4,7168]{2,1,0:T(4,128)(2,1)S(1)} async-done(((bf16[16,4,7168]{2,1,0:T(4,128)(2,1)}), bf16[16,4,7168]{2,1,0:T(4,128)(2,1)S(1)}, u32[]{:S(2)}, u32[]{:S(2)}) %all-to-all-start) | async-done | bytes 917536 | tf_op jit(solution)/shard_map/while/body/eval_jaxpr/all_to_all | solution.py:94
  217.1 7.9 convolution_convert_fusion.6
  233.3 5.3 fusion.107
  238.6 6.2 all-to-all-done.1
  253.4 6.8 all-to-all-done.2
  270.1 18.4 %all-to-all-done = bf16[16,4,7168]{2,1,0:T(4,128)(2,1)S(1)} async-done(((bf16[16,4,7168]{2,1,0:T(4,128)(2,1)}), bf16[16,4,7168]{2,1,0:T(4,128)(2,1)S(1)}, u32[]{:S(2)}, u32[]{:S(2)}) %all-to-all-start) | async-done | bytes 917536 | tf_op jit(solution)/shard_map/while/body/eval_jaxpr/all_to_all | solution.py:94
  293.1 7.9 convolution_convert_fusion.6
  309.3 5.3 fusion.107
  314.6 7.8 all-to-all-done.1
  331.2 6.9 all-to-all-done.2
  348.0 15.1 %all-to-all-done = bf16[16,4,7168]{2,1,0:T(4,128)(2,1)S(1)} async-done(((bf16[16,4,7168]{2,1,0:T(4,128)(2,1)}), bf16[16,4,7168]{2,1,0:T(4,128)(2,1)S(1)}, u32[]{:S(2)}, u32[]{:S(2)}) %all-to-all-start) | async-done | bytes 917536 | tf_op jit(solution)/shard_map/while/body/eval_jaxpr/all_to_all | solution.py:94
  367.8 7.9 convolution_convert_fusion.6
  383.9 5.3 fusion.107
  389.2 6.0 all-to-all-done.1
  403.8 6.8 all-to-all-done.2
  420.5 15.3 %all-to-all-done = bf16[16,4,7168]{2,1,0:T(4,128)(2,1)S(1)} async-done(((bf16[16,4,7168]{2,1,0:T(4,128)(2,1)}), bf16[16,4,7168]{2,1,0:T(4,128)(2,1)S(1)}, u32[]{:S(2)}, u32[]{:S(2)}) %all-to-all-start) | async-done | bytes 917536 | tf_op jit(solution)/shard_map/while/body/eval_jaxpr/all_to_all | solution.py:94
  440.6 7.9 convolution_convert_fusion.6
  456.8 5.3 fusion.107
  462.0 6.2 all-to-all-done.1
  476.8 6.8 all-to-all-done.2
  493.5 12.9 %all-to-all-done = bf16[16,4,7168]{2,1,0:T(4,128)(2,1)S(1)} async-done(((bf16[16,4,7168]{2,1,0:T(4,128)(2,1)}), bf16[16,4,7168]{2,1,0:T(4,128)(2,1)S(1)}, u32[]{:S(2)}, u32[]{:S(2)}) %all-to-all-start) | async-done | bytes 917536 | tf_op jit(solution)/shard_map/while/body/eval_jaxpr/all_to_all | solution.py:94
  511.1 7.9 convolution_convert_fusion.6
  527.3 5.3 fusion.107
  545.5 6.8 all-to-all-done.2
  562.2 11.6 %all-to-all-done = bf16[16,4,7168]{2,1,0:T(4,128)(2,1)S(1)} async-done(((bf16[16,4,7168]{2,1,0:T(4,128)(2,1)}), bf16[16,4,7168]{2,1,0:T(4,128)(2,1)S(1)}, u32[]{:S(2)}, u32[]{:S(2)}) %all-to-all-start) | async-done | bytes 917536 | tf_op jit(solution)/shard_map/while/body/eval_jaxpr/all_to_all | solution.py:94
  578.5 7.9 convolution_convert_fusion.6
  612.4 6.8 all-to-all-done.2
  629.1 11.4 %all-to-all-done = bf16[16,4,7168]{2,1,0:T(4,128)(2,1)S(1)} async-done(((bf16[16,4,7168]{2,1,0:T(4,128)(2,1)}), bf16[16,4,7168]{2,1,0:T(4,128)(2,1)S(1)}, u32[]{:S(2)}, u32[]{:S(2)}) %all-to-all-start) | async-done | bytes 917536 | tf_op jit(solution)/shard_map/while/body/eval_jaxpr/all_to_all | solution.py:94
  645.1 7.9 convolution_convert_fusion.6
  679.0 6.8 all-to-all-done.2
  695.7 12.3 %all-to-all-done = bf16[16,4,7168]{2,1,0:T(4,128)(2,1)S(1)} async-done(((bf16[16,4,7168]{2,1,0:T(4,128)(2,1)}), bf16[16,4,7168]{2,1,0:T(4,128)(2,1)S(1)}, u32[]{:S(2)}, u32[]{:S(2)}) %all-to-all-start) | async-done | bytes 917536 | tf_op jit(solution)/shard_map/while/body/eval_jaxpr/all_to_all | solution.py:94
  712.6 7.9 convolution_convert_fusion.6
  728.8 5.3 fusion.107
  746.4 6.9 all-to-all-done.2
  763.2 12.3 %all-to-all-done = bf16[16,4,7168]{2,1,0:T(4,128)(2,1)S(1)} async-done(((bf16[16,4,7168]{2,1,0:T(4,128)(2,1)}), bf16[16,4,7168]{2,1,0:T(4,128)(2,1)S(1)}, u32[]{:S(2)}, u32[]{:S(2)}) %all-to-all-start) | async-done | bytes 917536 | tf_op jit(solution)/shard_map/while/body/eval_jaxpr/all_to_all | solution.py:94
  780.1 7.9 convolution_convert_fusion.6
  796.3 5.3 fusion.107
  813.9 6.9 all-to-all-done.2
  830.7 12.3 %all-to-all-done = bf16[16,4,7168]{2,1,0:T(4,128)(2,1)S(1)} async-done(((bf16[16,4,7168]{2,1,0:T(4,128)(2,1)}), bf16[16,4,7168]{2,1,0:T(4,128)(2,1)S(1)}, u32[]{:S(2)}, u32[]{:S(2)}) %all-to-all-start) | async-done | bytes 917536 | tf_op jit(solution)/shard_map/while/body/eval_jaxpr/all_to_all | solution.py:94
  847.6 7.9 convolution_convert_fusion.6
  881.4 6.9 all-to-all-done.2
  898.2 12.3 %all-to-all-done = bf16[16,4,7168]{2,1,0:T(4,128)(2,1)S(1)} async-done(((bf16[16,4,7168]{2,1,0:T(4,128)(2,1)}), bf16[16,4,7168]{2,1,0:T(4,128)(2,1)S(1)}, u32[]{:S(2)}, u32[]{:S(2)}) %all-to-all-start) | async-done | bytes 917536 | tf_op jit(solution)/shard_map/while/body/eval_jaxpr/all_to_all | solution.py:94
  915.1 7.9 convolution_convert_fusion.6
  948.9 6.9 all-to-all-done.2
  (375 shorter events, 380.3 us)
Async XLA Ops:
  7.2 179.6 %all-reduce.3.cloned.1.call-start = ((), (), s32[]{:S(2)}) async-start(), calls=%async_computation.3 | async-start | bytes 22020096 | tf_op jit(solution)/shard_map/psum | solution.py:12
  7.9 4.8 copy-start
  19.0 167.7 %copy-start.1 = (f32[1,7168]{1,0:T(1,128)S(1)}, f32[1,7168]{1,0:T(1,128)}, u32[]{:S(2)}) copy-start(f32[1,7168]{1,0:T(1,128)} %param.13) | copy-start | bytes 86020
  19.0 167.8 %copy-start.3 = (bf16[1,7168,8]{1,2,0:T(8,128)(2,1)S(1)}, bf16[1,7168,8]{1,2,0:T(8,128)(2,1)}, u32[]{:S(2)}) copy-start(bf16[1,7168,8]{1,2,0:T(8,128)(2,1)} %param.14) | copy-start | bytes 344068
  191.0 21.4 %all-to-all-start = ((bf16[16,4,7168]{2,1,0:T(4,128)(2,1)}), bf16[16,4,7168]{2,1,0:T(4,128)(2,1)S(1)}, u32[]{:S(2)}, u32[]{:S(2)}) async-start(bf16[16,4,7168]{2,1,0:T(4,128)(2,1)} %bitcast.92), calls=%async_computation | async-start | bytes 1835008 | tf_op jit(solution)/shard_map/while/body/eval_jaxpr/all_to_all | solution.py:94
  226.3 18.5 %all-to-all-start.1 = ((bf16[16,4,7168]{2,1,0:T(4,128)(2,1)}), bf16[16,4,7168]{2,1,0:T(4,128)(2,1)S(1)}, u32[]{:S(2)}, u32[]{:S(2)}) async-start(bf16[16,4,7168]{2,1,0:T(4,128)(2,1)} %reshape.177), calls=%async_computation.1 | async-start | bytes 1835008 | tf_op jit(solution)/shard_map/while/body/eval_jaxpr/all_to_all | solution.py:64
  247.2 14.2 %collective-permute-start = (bf16[8,7168]{1,0:T(8,128)(2,1)S(1)}, bf16[8,7168]{1,0:T(8,128)(2,1)S(1)}, u32[]{:S(2)}, u32[]{:S(2)}) collective-permute-start(bf16[8,7168]{1,0:T(8,128)(2,1)S(1)} %get-tuple-element.674), channel_id=1, source_target_pairs={{0,16},{16,32},{32,48},{48,64},{64,80},{80,96},{96,112},{1,17},{17... | collective-permute-start | bytes 344072 | tf_op jit(solution)/shard_map/while/body/eval_jaxpr/ppermute | solution.py:18
  249.3 10.9 %all-to-all-start.2 = ((bf16[16,1,4]{2,1,0:T(2,128)(2,1)}), bf16[16,1,4]{2,1,0:T(2,128)(2,1)S(1)}, u32[]{:S(2)}, u32[]{:S(2)}) async-start(bf16[16,1,4]{2,1,0:T(2,128)(2,1)} %copy.40), calls=%async_computation.2 | async-start | bytes 16384 | tf_op jit(solution)/shard_map/while/body/eval_jaxpr/all_to_all | solution.py:95
  265.6 22.8 %all-to-all-start = ((bf16[16,4,7168]{2,1,0:T(4,128)(2,1)}), bf16[16,4,7168]{2,1,0:T(4,128)(2,1)S(1)}, u32[]{:S(2)}, u32[]{:S(2)}) async-start(bf16[16,4,7168]{2,1,0:T(4,128)(2,1)} %bitcast.92), calls=%async_computation | async-start | bytes 1835008 | tf_op jit(solution)/shard_map/while/body/eval_jaxpr/all_to_all | solution.py:94
  302.3 20.1 %all-to-all-start.1 = ((bf16[16,4,7168]{2,1,0:T(4,128)(2,1)}), bf16[16,4,7168]{2,1,0:T(4,128)(2,1)S(1)}, u32[]{:S(2)}, u32[]{:S(2)}) async-start(bf16[16,4,7168]{2,1,0:T(4,128)(2,1)} %reshape.177), calls=%async_computation.1 | async-start | bytes 1835008 | tf_op jit(solution)/shard_map/while/body/eval_jaxpr/all_to_all | solution.py:64
  324.8 14.5 %collective-permute-start = (bf16[8,7168]{1,0:T(8,128)(2,1)S(1)}, bf16[8,7168]{1,0:T(8,128)(2,1)S(1)}, u32[]{:S(2)}, u32[]{:S(2)}) collective-permute-start(bf16[8,7168]{1,0:T(8,128)(2,1)S(1)} %get-tuple-element.674), channel_id=1, source_target_pairs={{0,16},{16,32},{32,48},{48,64},{64,80},{80,96},{96,112},{1,17},{17... | collective-permute-start | bytes 344072 | tf_op jit(solution)/shard_map/while/body/eval_jaxpr/ppermute | solution.py:18
  326.9 11.2 %all-to-all-start.2 = ((bf16[16,1,4]{2,1,0:T(2,128)(2,1)}), bf16[16,1,4]{2,1,0:T(2,128)(2,1)S(1)}, u32[]{:S(2)}, u32[]{:S(2)}) async-start(bf16[16,1,4]{2,1,0:T(2,128)(2,1)} %copy.40), calls=%async_computation.2 | async-start | bytes 16384 | tf_op jit(solution)/shard_map/while/body/eval_jaxpr/all_to_all | solution.py:95
  343.5 19.5 %all-to-all-start = ((bf16[16,4,7168]{2,1,0:T(4,128)(2,1)}), bf16[16,4,7168]{2,1,0:T(4,128)(2,1)S(1)}, u32[]{:S(2)}, u32[]{:S(2)}) async-start(bf16[16,4,7168]{2,1,0:T(4,128)(2,1)} %bitcast.92), calls=%async_computation | async-start | bytes 1835008 | tf_op jit(solution)/shard_map/while/body/eval_jaxpr/all_to_all | solution.py:94
  376.9 18.3 %all-to-all-start.1 = ((bf16[16,4,7168]{2,1,0:T(4,128)(2,1)}), bf16[16,4,7168]{2,1,0:T(4,128)(2,1)S(1)}, u32[]{:S(2)}, u32[]{:S(2)}) async-start(bf16[16,4,7168]{2,1,0:T(4,128)(2,1)} %reshape.177), calls=%async_computation.1 | async-start | bytes 1835008 | tf_op jit(solution)/shard_map/while/body/eval_jaxpr/all_to_all | solution.py:64
  397.7 14.2 %collective-permute-start = (bf16[8,7168]{1,0:T(8,128)(2,1)S(1)}, bf16[8,7168]{1,0:T(8,128)(2,1)S(1)}, u32[]{:S(2)}, u32[]{:S(2)}) collective-permute-start(bf16[8,7168]{1,0:T(8,128)(2,1)S(1)} %get-tuple-element.674), channel_id=1, source_target_pairs={{0,16},{16,32},{32,48},{48,64},{64,80},{80,96},{96,112},{1,17},{17... | collective-permute-start | bytes 344072 | tf_op jit(solution)/shard_map/while/body/eval_jaxpr/ppermute | solution.py:18
  399.7 10.9 %all-to-all-start.2 = ((bf16[16,1,4]{2,1,0:T(2,128)(2,1)}), bf16[16,1,4]{2,1,0:T(2,128)(2,1)S(1)}, u32[]{:S(2)}, u32[]{:S(2)}) async-start(bf16[16,1,4]{2,1,0:T(2,128)(2,1)} %copy.40), calls=%async_computation.2 | async-start | bytes 16384 | tf_op jit(solution)/shard_map/while/body/eval_jaxpr/all_to_all | solution.py:95
  416.1 19.8 %all-to-all-start = ((bf16[16,4,7168]{2,1,0:T(4,128)(2,1)}), bf16[16,4,7168]{2,1,0:T(4,128)(2,1)S(1)}, u32[]{:S(2)}, u32[]{:S(2)}) async-start(bf16[16,4,7168]{2,1,0:T(4,128)(2,1)} %bitcast.92), calls=%async_computation | async-start | bytes 1835008 | tf_op jit(solution)/shard_map/while/body/eval_jaxpr/all_to_all | solution.py:94
  449.7 18.5 %all-to-all-start.1 = ((bf16[16,4,7168]{2,1,0:T(4,128)(2,1)}), bf16[16,4,7168]{2,1,0:T(4,128)(2,1)S(1)}, u32[]{:S(2)}, u32[]{:S(2)}) async-start(bf16[16,4,7168]{2,1,0:T(4,128)(2,1)} %reshape.177), calls=%async_computation.1 | async-start | bytes 1835008 | tf_op jit(solution)/shard_map/while/body/eval_jaxpr/all_to_all | solution.py:64
  470.7 14.2 %collective-permute-start = (bf16[8,7168]{1,0:T(8,128)(2,1)S(1)}, bf16[8,7168]{1,0:T(8,128)(2,1)S(1)}, u32[]{:S(2)}, u32[]{:S(2)}) collective-permute-start(bf16[8,7168]{1,0:T(8,128)(2,1)S(1)} %get-tuple-element.674), channel_id=1, source_target_pairs={{0,16},{16,32},{32,48},{48,64},{64,80},{80,96},{96,112},{1,17},{17... | collective-permute-start | bytes 344072 | tf_op jit(solution)/shard_map/while/body/eval_jaxpr/ppermute | solution.py:18
  472.7 10.9 %all-to-all-start.2 = ((bf16[16,1,4]{2,1,0:T(2,128)(2,1)}), bf16[16,1,4]{2,1,0:T(2,128)(2,1)S(1)}, u32[]{:S(2)}, u32[]{:S(2)}) async-start(bf16[16,1,4]{2,1,0:T(2,128)(2,1)} %copy.40), calls=%async_computation.2 | async-start | bytes 16384 | tf_op jit(solution)/shard_map/while/body/eval_jaxpr/all_to_all | solution.py:95
  489.1 17.4 %all-to-all-start = ((bf16[16,4,7168]{2,1,0:T(4,128)(2,1)}), bf16[16,4,7168]{2,1,0:T(4,128)(2,1)S(1)}, u32[]{:S(2)}, u32[]{:S(2)}) async-start(bf16[16,4,7168]{2,1,0:T(4,128)(2,1)} %bitcast.92), calls=%async_computation | async-start | bytes 1835008 | tf_op jit(solution)/shard_map/while/body/eval_jaxpr/all_to_all | solution.py:94
  520.3 16.6 %all-to-all-start.1 = ((bf16[16,4,7168]{2,1,0:T(4,128)(2,1)}), bf16[16,4,7168]{2,1,0:T(4,128)(2,1)S(1)}, u32[]{:S(2)}, u32[]{:S(2)}) async-start(bf16[16,4,7168]{2,1,0:T(4,128)(2,1)} %reshape.177), calls=%async_computation.1 | async-start | bytes 1835008 | tf_op jit(solution)/shard_map/while/body/eval_jaxpr/all_to_all | solution.py:64
  539.4 14.2 %collective-permute-start = (bf16[8,7168]{1,0:T(8,128)(2,1)S(1)}, bf16[8,7168]{1,0:T(8,128)(2,1)S(1)}, u32[]{:S(2)}, u32[]{:S(2)}) collective-permute-start(bf16[8,7168]{1,0:T(8,128)(2,1)S(1)} %get-tuple-element.674), channel_id=1, source_target_pairs={{0,16},{16,32},{32,48},{48,64},{64,80},{80,96},{96,112},{1,17},{17... | collective-permute-start | bytes 344072 | tf_op jit(solution)/shard_map/while/body/eval_jaxpr/ppermute | solution.py:18
  541.4 10.9 %all-to-all-start.2 = ((bf16[16,1,4]{2,1,0:T(2,128)(2,1)}), bf16[16,1,4]{2,1,0:T(2,128)(2,1)S(1)}, u32[]{:S(2)}, u32[]{:S(2)}) async-start(bf16[16,1,4]{2,1,0:T(2,128)(2,1)} %copy.40), calls=%async_computation.2 | async-start | bytes 16384 | tf_op jit(solution)/shard_map/while/body/eval_jaxpr/all_to_all | solution.py:95
  557.8 16.1 %all-to-all-start = ((bf16[16,4,7168]{2,1,0:T(4,128)(2,1)}), bf16[16,4,7168]{2,1,0:T(4,128)(2,1)S(1)}, u32[]{:S(2)}, u32[]{:S(2)}) async-start(bf16[16,4,7168]{2,1,0:T(4,128)(2,1)} %bitcast.92), calls=%async_computation | async-start | bytes 1835008 | tf_op jit(solution)/shard_map/while/body/eval_jaxpr/all_to_all | solution.py:94
  587.7 16.1 %all-to-all-start.1 = ((bf16[16,4,7168]{2,1,0:T(4,128)(2,1)}), bf16[16,4,7168]{2,1,0:T(4,128)(2,1)S(1)}, u32[]{:S(2)}, u32[]{:S(2)}) async-start(bf16[16,4,7168]{2,1,0:T(4,128)(2,1)} %reshape.177), calls=%async_computation.1 | async-start | bytes 1835008 | tf_op jit(solution)/shard_map/while/body/eval_jaxpr/all_to_all | solution.py:64
  606.2 14.2 %collective-permute-start = (bf16[8,7168]{1,0:T(8,128)(2,1)S(1)}, bf16[8,7168]{1,0:T(8,128)(2,1)S(1)}, u32[]{:S(2)}, u32[]{:S(2)}) collective-permute-start(bf16[8,7168]{1,0:T(8,128)(2,1)S(1)} %get-tuple-element.674), channel_id=1, source_target_pairs={{0,16},{16,32},{32,48},{48,64},{64,80},{80,96},{96,112},{1,17},{17... | collective-permute-start | bytes 344072 | tf_op jit(solution)/shard_map/while/body/eval_jaxpr/ppermute | solution.py:18
  608.3 10.9 %all-to-all-start.2 = ((bf16[16,1,4]{2,1,0:T(2,128)(2,1)}), bf16[16,1,4]{2,1,0:T(2,128)(2,1)S(1)}, u32[]{:S(2)}, u32[]{:S(2)}) async-start(bf16[16,1,4]{2,1,0:T(2,128)(2,1)} %copy.40), calls=%async_computation.2 | async-start | bytes 16384 | tf_op jit(solution)/shard_map/while/body/eval_jaxpr/all_to_all | solution.py:95
  624.7 15.8 %all-to-all-start = ((bf16[16,4,7168]{2,1,0:T(4,128)(2,1)}), bf16[16,4,7168]{2,1,0:T(4,128)(2,1)S(1)}, u32[]{:S(2)}, u32[]{:S(2)}) async-start(bf16[16,4,7168]{2,1,0:T(4,128)(2,1)} %bitcast.92), calls=%async_computation | async-start | bytes 1835008 | tf_op jit(solution)/shard_map/while/body/eval_jaxpr/all_to_all | solution.py:94
  654.3 16.1 %all-to-all-start.1 = ((bf16[16,4,7168]{2,1,0:T(4,128)(2,1)}), bf16[16,4,7168]{2,1,0:T(4,128)(2,1)S(1)}, u32[]{:S(2)}, u32[]{:S(2)}) async-start(bf16[16,4,7168]{2,1,0:T(4,128)(2,1)} %reshape.177), calls=%async_computation.1 | async-start | bytes 1835008 | tf_op jit(solution)/shard_map/while/body/eval_jaxpr/all_to_all | solution.py:64
  672.8 14.2 %collective-permute-start = (bf16[8,7168]{1,0:T(8,128)(2,1)S(1)}, bf16[8,7168]{1,0:T(8,128)(2,1)S(1)}, u32[]{:S(2)}, u32[]{:S(2)}) collective-permute-start(bf16[8,7168]{1,0:T(8,128)(2,1)S(1)} %get-tuple-element.674), channel_id=1, source_target_pairs={{0,16},{16,32},{32,48},{48,64},{64,80},{80,96},{96,112},{1,17},{17... | collective-permute-start | bytes 344072 | tf_op jit(solution)/shard_map/while/body/eval_jaxpr/ppermute | solution.py:18
  674.9 10.9 %all-to-all-start.2 = ((bf16[16,1,4]{2,1,0:T(2,128)(2,1)}), bf16[16,1,4]{2,1,0:T(2,128)(2,1)S(1)}, u32[]{:S(2)}, u32[]{:S(2)}) async-start(bf16[16,1,4]{2,1,0:T(2,128)(2,1)} %copy.40), calls=%async_computation.2 | async-start | bytes 16384 | tf_op jit(solution)/shard_map/while/body/eval_jaxpr/all_to_all | solution.py:95
  691.3 16.7 %all-to-all-start = ((bf16[16,4,7168]{2,1,0:T(4,128)(2,1)}), bf16[16,4,7168]{2,1,0:T(4,128)(2,1)S(1)}, u32[]{:S(2)}, u32[]{:S(2)}) async-start(bf16[16,4,7168]{2,1,0:T(4,128)(2,1)} %bitcast.92), calls=%async_computation | async-start | bytes 1835008 | tf_op jit(solution)/shard_map/while/body/eval_jaxpr/all_to_all | solution.py:94
  721.8 15.8 %all-to-all-start.1 = ((bf16[16,4,7168]{2,1,0:T(4,128)(2,1)}), bf16[16,4,7168]{2,1,0:T(4,128)(2,1)S(1)}, u32[]{:S(2)}, u32[]{:S(2)}) async-start(bf16[16,4,7168]{2,1,0:T(4,128)(2,1)} %reshape.177), calls=%async_computation.1 | async-start | bytes 1835008 | tf_op jit(solution)/shard_map/while/body/eval_jaxpr/all_to_all | solution.py:64
  740.1 14.4 %collective-permute-start = (bf16[8,7168]{1,0:T(8,128)(2,1)S(1)}, bf16[8,7168]{1,0:T(8,128)(2,1)S(1)}, u32[]{:S(2)}, u32[]{:S(2)}) collective-permute-start(bf16[8,7168]{1,0:T(8,128)(2,1)S(1)} %get-tuple-element.674), channel_id=1, source_target_pairs={{0,16},{16,32},{32,48},{48,64},{64,80},{80,96},{96,112},{1,17},{17... | collective-permute-start | bytes 344072 | tf_op jit(solution)/shard_map/while/body/eval_jaxpr/ppermute | solution.py:18
  742.1 11.1 %all-to-all-start.2 = ((bf16[16,1,4]{2,1,0:T(2,128)(2,1)}), bf16[16,1,4]{2,1,0:T(2,128)(2,1)S(1)}, u32[]{:S(2)}, u32[]{:S(2)}) async-start(bf16[16,1,4]{2,1,0:T(2,128)(2,1)} %copy.40), calls=%async_computation.2 | async-start | bytes 16384 | tf_op jit(solution)/shard_map/while/body/eval_jaxpr/all_to_all | solution.py:95
  758.7 16.7 %all-to-all-start = ((bf16[16,4,7168]{2,1,0:T(4,128)(2,1)}), bf16[16,4,7168]{2,1,0:T(4,128)(2,1)S(1)}, u32[]{:S(2)}, u32[]{:S(2)}) async-start(bf16[16,4,7168]{2,1,0:T(4,128)(2,1)} %bitcast.92), calls=%async_computation | async-start | bytes 1835008 | tf_op jit(solution)/shard_map/while/body/eval_jaxpr/all_to_all | solution.py:94
  789.3 15.8 %all-to-all-start.1 = ((bf16[16,4,7168]{2,1,0:T(4,128)(2,1)}), bf16[16,4,7168]{2,1,0:T(4,128)(2,1)S(1)}, u32[]{:S(2)}, u32[]{:S(2)}) async-start(bf16[16,4,7168]{2,1,0:T(4,128)(2,1)} %reshape.177), calls=%async_computation.1 | async-start | bytes 1835008 | tf_op jit(solution)/shard_map/while/body/eval_jaxpr/all_to_all | solution.py:64
  807.6 14.4 %collective-permute-start = (bf16[8,7168]{1,0:T(8,128)(2,1)S(1)}, bf16[8,7168]{1,0:T(8,128)(2,1)S(1)}, u32[]{:S(2)}, u32[]{:S(2)}) collective-permute-start(bf16[8,7168]{1,0:T(8,128)(2,1)S(1)} %get-tuple-element.674), channel_id=1, source_target_pairs={{0,16},{16,32},{32,48},{48,64},{64,80},{80,96},{96,112},{1,17},{17... | collective-permute-start | bytes 344072 | tf_op jit(solution)/shard_map/while/body/eval_jaxpr/ppermute | solution.py:18
  809.6 11.1 %all-to-all-start.2 = ((bf16[16,1,4]{2,1,0:T(2,128)(2,1)}), bf16[16,1,4]{2,1,0:T(2,128)(2,1)S(1)}, u32[]{:S(2)}, u32[]{:S(2)}) async-start(bf16[16,1,4]{2,1,0:T(2,128)(2,1)} %copy.40), calls=%async_computation.2 | async-start | bytes 16384 | tf_op jit(solution)/shard_map/while/body/eval_jaxpr/all_to_all | solution.py:95
  826.2 16.7 %all-to-all-start = ((bf16[16,4,7168]{2,1,0:T(4,128)(2,1)}), bf16[16,4,7168]{2,1,0:T(4,128)(2,1)S(1)}, u32[]{:S(2)}, u32[]{:S(2)}) async-start(bf16[16,4,7168]{2,1,0:T(4,128)(2,1)} %bitcast.92), calls=%async_computation | async-start | bytes 1835008 | tf_op jit(solution)/shard_map/while/body/eval_jaxpr/all_to_all | solution.py:94
  856.8 15.8 %all-to-all-start.1 = ((bf16[16,4,7168]{2,1,0:T(4,128)(2,1)}), bf16[16,4,7168]{2,1,0:T(4,128)(2,1)S(1)}, u32[]{:S(2)}, u32[]{:S(2)}) async-start(bf16[16,4,7168]{2,1,0:T(4,128)(2,1)} %reshape.177), calls=%async_computation.1 | async-start | bytes 1835008 | tf_op jit(solution)/shard_map/while/body/eval_jaxpr/all_to_all | solution.py:64
  875.1 14.4 %collective-permute-start = (bf16[8,7168]{1,0:T(8,128)(2,1)S(1)}, bf16[8,7168]{1,0:T(8,128)(2,1)S(1)}, u32[]{:S(2)}, u32[]{:S(2)}) collective-permute-start(bf16[8,7168]{1,0:T(8,128)(2,1)S(1)} %get-tuple-element.674), channel_id=1, source_target_pairs={{0,16},{16,32},{32,48},{48,64},{64,80},{80,96},{96,112},{1,17},{17... | collective-permute-start | bytes 344072 | tf_op jit(solution)/shard_map/while/body/eval_jaxpr/ppermute | solution.py:18
  877.1 11.1 %all-to-all-start.2 = ((bf16[16,1,4]{2,1,0:T(2,128)(2,1)}), bf16[16,1,4]{2,1,0:T(2,128)(2,1)S(1)}, u32[]{:S(2)}, u32[]{:S(2)}) async-start(bf16[16,1,4]{2,1,0:T(2,128)(2,1)} %copy.40), calls=%async_computation.2 | async-start | bytes 16384 | tf_op jit(solution)/shard_map/while/body/eval_jaxpr/all_to_all | solution.py:95
  893.7 16.7 %all-to-all-start = ((bf16[16,4,7168]{2,1,0:T(4,128)(2,1)}), bf16[16,4,7168]{2,1,0:T(4,128)(2,1)S(1)}, u32[]{:S(2)}, u32[]{:S(2)}) async-start(bf16[16,4,7168]{2,1,0:T(4,128)(2,1)} %bitcast.92), calls=%async_computation | async-start | bytes 1835008 | tf_op jit(solution)/shard_map/while/body/eval_jaxpr/all_to_all | solution.py:94
  924.3 15.8 %all-to-all-start.1 = ((bf16[16,4,7168]{2,1,0:T(4,128)(2,1)}), bf16[16,4,7168]{2,1,0:T(4,128)(2,1)S(1)}, u32[]{:S(2)}, u32[]{:S(2)}) async-start(bf16[16,4,7168]{2,1,0:T(4,128)(2,1)} %reshape.177), calls=%async_computation.1 | async-start | bytes 1835008 | tf_op jit(solution)/shard_map/while/body/eval_jaxpr/all_to_all | solution.py:64
  942.6 14.4 %collective-permute-start = (bf16[8,7168]{1,0:T(8,128)(2,1)S(1)}, bf16[8,7168]{1,0:T(8,128)(2,1)S(1)}, u32[]{:S(2)}, u32[]{:S(2)}) collective-permute-start(bf16[8,7168]{1,0:T(8,128)(2,1)S(1)} %get-tuple-element.674), channel_id=1, source_target_pairs={{0,16},{16,32},{32,48},{48,64},{64,80},{80,96},{96,112},{1,17},{17... | collective-permute-start | bytes 344072 | tf_op jit(solution)/shard_map/while/body/eval_jaxpr/ppermute | solution.py:18
  944.6 11.1 %all-to-all-start.2 = ((bf16[16,1,4]{2,1,0:T(2,128)(2,1)}), bf16[16,1,4]{2,1,0:T(2,128)(2,1)S(1)}, u32[]{:S(2)}, u32[]{:S(2)}) async-start(bf16[16,1,4]{2,1,0:T(2,128)(2,1)} %copy.40), calls=%async_computation.2 | async-start | bytes 16384 | tf_op jit(solution)/shard_map/while/body/eval_jaxpr/all_to_all | solution.py:95
  (1 other events, 0.8 us)
Sparse Core Ops, SparseCore 0:
  19.2 167.4 all-reduce.2
where the time goes:
time: 970 us; the launch traced here: 966 us
  waiting for transfers between devices  444 us (46%)
  matrix products  252 us (26%)
  starting transfers between devices  135 us (14%)
  other arithmetic  53.5 us (6%)
  local copies, waits for them, and re-layouts  49.6 us (5%)
  loops' own time  15.9 us (2%)
  between operations  15.9 us (2%)
    psum x1, waiting for transfers between devices, spread(): return lax.psum(block, axis)  168 us
    all_to_all x11, waiting for transfers between devices, apply_layer(): lax.all_to_all(send_rows, 'ep', split_axis=0, concat_axis=0, tiled=True)  149 us
    dot_general x11, matrix products, expert_rows(): jnp.dot(home_act, down_w, preferred_element_type=jnp.float32)  87 us
    all_to_all x11, waiting for transfers between devices, apply_layer(): lax.all_to_all(send_flags, 'ep', split_axis=0, concat_axis=0, tiled=True)  75 us
    dot_general x11, matrix products, apply_layer(): jnp.dot(local_act, copy_down, preferred_element_type=jnp.float32)  58 us
    all_to_all x11, waiting for transfers between devices, work_both(): lax.all_to_all(home_part, 'ep', split_axis=0, concat_axis=0, tiled=True)  52.2 us
    dot_general x11, matrix products, expert_rows(): gate_value = jnp.dot(flat_rows, gate_w, preferred_element_type=jnp.float32)  49 us
    all_to_all x11, starting transfers between devices, apply_layer(): lax.all_to_all(send_rows, 'ep', split_axis=0, concat_axis=0, tiled=True)  41.7 us
  transfers between devices with their start and end apart: 45, of which 34 were waited for; matrix products, arithmetic and copies ran while one was open for 12% of the time, Pallas kernels for 0%

commit v1 on v0

v1 whole, which is shorter than its diff:
```python
import jax
import jax.numpy as jnp
from jax import lax
from jax.sharding import PartitionSpec as P

FFW = 1024
BLK = 256


def shifted(block, axis, distance):
    devices = range(lax.axis_size(axis))
    route = [(i - distance, i) for i in devices if i - distance in devices]
    return lax.ppermute(block, axis, route)


def local(rows_in, routes, hot_blocks, gains, router, w_gate, w_up, w_down):
    section_index = lax.axis_index("section")
    ep_index = lax.axis_index("ep")
    section_count = lax.axis_size("section")
    micro_count, tok_rows, model_width = rows_in.shape
    expert_count = router.shape[2]
    top_count = routes.shape[3]
    capacity = tok_rows // 2
    blocks_per_expert = FFW // BLK
    hot_index = hot_blocks[0]
    owner_index = hot_index // 2
    hot_expert = hot_index // blocks_per_expert
    expert_ids = lax.iota(jnp.int32, expert_count)

    member = (routes[0][:, :, :, None] == expert_ids).astype(jnp.float32)
    routed = jnp.sum(member, axis=2)
    before = (
        lax.broadcasted_iota(jnp.int32, (tok_rows, tok_rows), 0)
        > lax.broadcasted_iota(jnp.int32, (tok_rows, tok_rows), 1)
    ).astype(jnp.float32)
    slot_rank = jnp.einsum("ts,mse->mte", before, routed)
    slot_ids = lax.iota(jnp.float32, capacity)
    placement = routed.transpose(0, 2, 1)[:, :, None, :] * (
        slot_rank.transpose(0, 2, 1)[:, :, None, :] == slot_ids[None, None, :, None]
    ).astype(jnp.float32)
    placement = jnp.repeat(placement, 2, axis=1).reshape(
        micro_count, expert_count * 2 * capacity, tok_rows
    )

    expert_load = jnp.sum(routed, axis=(0, 1))
    expert_total = lax.psum(expert_load, "ep")
    mine = (expert_ids == ep_index // 2).astype(jnp.float32)
    hot_one = (expert_ids == hot_expert).astype(jnp.float32)
    unit_count = jnp.sum(expert_total * mine) * (
        2.0 - (owner_index == ep_index).astype(jnp.float32)
    ) + jnp.sum(expert_load * hot_one)
    relative = unit_count / float(micro_count * tok_rows * top_count * blocks_per_expert)

    norm_gain = gains[0]
    router_w = router[0]
    gate_w = w_gate[0]
    up_w = w_up[0]
    down_w = w_down[0]

    def apply_layer(layer_input, member_m, place_m):
        rows_float = layer_input.astype(jnp.float32)
        mean_square = jnp.mean(rows_float * rows_float, axis=-1, keepdims=True)
        normed = (rows_float * lax.rsqrt(mean_square + 1e-06) * norm_gain).astype(jnp.bfloat16)
        send = jnp.dot(
            place_m.astype(jnp.bfloat16), normed, preferred_element_type=jnp.float32
        ).astype(jnp.bfloat16)
        recv = lax.all_to_all(send, "ep", split_axis=0, concat_axis=0, tiled=True)
        scores = jax.nn.sigmoid(jnp.dot(normed, router_w, preferred_element_type=jnp.float32))
        chosen = jnp.sum(member_m * scores[:, None, :], axis=2)
        gate_weights = 2.5 * chosen / jnp.sum(chosen, axis=1, keepdims=True)
        token_gate = jnp.sum(member_m * gate_weights[:, :, None], axis=1)
        wide_gate = jnp.repeat(token_gate.T, 2 * capacity, axis=0)
        weighting = (place_m * wide_gate).T
        gate_value = jnp.dot(recv, gate_w, preferred_element_type=jnp.float32)
        up_value = jnp.dot(recv, up_w, preferred_element_type=jnp.float32)
        activation = (jax.nn.silu(gate_value) * up_value).astype(jnp.bfloat16)
        part = jnp.dot(activation, down_w, preferred_element_type=jnp.float32).astype(jnp.bfloat16)
        back = lax.all_to_all(part, "ep", split_axis=0, concat_axis=0, tiled=True)
        high = weighting.astype(jnp.bfloat16)
        low = (weighting - high.astype(jnp.float32)).astype(jnp.bfloat16)
        both = jnp.dot(
            jnp.concatenate([high, low]), back, preferred_element_type=jnp.float32
        )
        routed_sum = both[:tok_rows] + both[tok_rows:]
        return (rows_float + routed_sum).astype(jnp.bfloat16)

    incoming = jnp.zeros((tok_rows, model_width), jnp.bfloat16)
    ticks = []
    for tick_index in range(micro_count + section_count - 1):
        micro_index = jnp.clip(tick_index - section_index, 0, micro_count - 1)
        if tick_index < micro_count:
            layer_input = jnp.where(section_index == 0, rows_in[tick_index], incoming)
        else:
            layer_input = incoming
        member_m = lax.dynamic_index_in_dim(member, micro_index, 0, keepdims=False)
        place_m = lax.dynamic_index_in_dim(placement, micro_index, 0, keepdims=False)
        next_rows = apply_layer(layer_input, member_m, place_m)
        ticks.append(next_rows)
        if tick_index < micro_count + section_count - 2:
            incoming = shifted(next_rows, "section", 1)
    outputs = lax.dynamic_slice_in_dim(jnp.stack(ticks), section_index, micro_count, 0)
    return (outputs[None], relative.reshape(1, 1))


def solution(mesh):
    return jax.shard_map(
        local,
        mesh=mesh,
        in_specs=(
            P(None, "ep", None),
            P("section", None, "ep", None),
            P("section"),
            P("section", None),
            P("section", None, None),
            P("section", None, "ep"),
            P("section", None, "ep"),
            P("section", "ep", None),
        ),
        out_specs=(P("section", None, "ep", None), P("section", "ep")),
        check_vma=False,
    )
```

time: 970 us -> 706 us (0.73)
  waiting for transfers between devices: 444 us -> 339 us
  matrix products: 252 us -> 152 us
  blocking collectives: 0 us -> 44.9 us
  other arithmetic: 53.5 us -> 16.2 us
  starting transfers between devices: 135 us -> 101 us
  loops' own time: 15.9 us -> 0 us
  local copies, waits for them, and re-layouts: 49.6 us -> 36.6 us
  between operations: 15.9 us -> 5.38 us
    psum x1 -> x0, waiting for transfers between devices: 168 us -> none  [spread(): return lax.psum(block, axis)]
    dot_general x66 -> x45, matrix products: 249 us -> 145 us  [the longest x11 87.2 us: apply_layer(): jnp.dot(activation, down_w, preferred_element_type=jnp.float32)]
    all_to_all x33 -> x22, waiting for transfers between devices: 276 us -> 330 us  [the longest x11 168 us: apply_layer(): back = lax.all_to_all(part, 'ep', split_axis=0, concat_axis=0, tiled=True)]
    psum x0 -> x1, blocking collectives: none -> 44.9 us  [local(): expert_total = lax.psum(expert_load, 'ep')]
    all_to_all x33 -> x22, starting transfers between devices: 121 us -> 86.9 us  [the longest x11 45.5 us: apply_layer(): recv = lax.all_to_all(send, 'ep', split_axis=0, concat_axis=0, tiled=True)]
    all_to_all x11 -> x44, local copies, waits for them, and re-layouts: 6.68 us -> 32.5 us  [the longest x22 16.3 us: apply_layer(): recv = lax.all_to_all(send, 'ep', split_axis=0, concat_axis=0, tiled=True)]
    another operation x1 -> x0, loops' own time: 15.9 us -> none  [local(): final_state = lax.fori_loop(0, tick_count, run_tick, start_state)]
    reshape x22 -> x11, local copies, waits for them, and re-layouts: 16.2 us -> 0.94 us  [apply_layer(): wide_gate = jnp.repeat(token_gate.T, 2 * capacity, axis=0)]
  transfers between devices with their start and end apart: 45 -> 32, of which waited for: 34 -> 31; matrix products, arithmetic and copies ran while one was open for 12% -> 3% of each run, Pallas kernels for 0% -> 0%
where the time goes in v1:
time: 706 us; the launch traced here: 695 us
  waiting for transfers between devices  339 us (48%)
  matrix products  152 us (22%)
  starting transfers between devices  101 us (14%)
  blocking collectives  44.9 us (6%)
  local copies, waits for them, and re-layouts  36.6 us (5%)
  other arithmetic  16.2 us (2%)
    all_to_all x11, waiting for transfers between devices, apply_layer(): back = lax.all_to_all(part, 'ep', split_axis=0, concat_axis=0, tiled=True)  168 us
    all_to_all x11, waiting for transfers between devices, apply_layer(): recv = lax.all_to_all(send, 'ep', split_axis=0, concat_axis=0, tiled=True)  162 us
    dot_general x11, matrix products, apply_layer(): jnp.dot(activation, down_w, preferred_element_type=jnp.float32)  87.2 us
    dot_general x11, matrix products, apply_layer(): gate_value = jnp.dot(recv, gate_w, preferred_element_type=jnp.float32)  49 us
    all_to_all x11, starting transfers between devices, apply_layer(): recv = lax.all_to_all(send, 'ep', split_axis=0, concat_axis=0, tiled=True)  45.5 us
    psum x1, blocking collectives, local(): expert_total = lax.psum(expert_load, 'ep')  44.9 us
    all_to_all x11, starting transfers between devices, apply_layer(): back = lax.all_to_all(part, 'ep', split_axis=0, concat_axis=0, tiled=True)  41.4 us
    all_to_all x22, local copies, waits for them, and re-layouts, apply_layer(): recv = lax.all_to_all(send, 'ep', split_axis=0, concat_axis=0, tiled=True)  16.3 us
  transfers between devices with their start and end apart: 32, of which 31 were waited for; matrix products, arithmetic and copies ran while one was open for 3% of the time, Pallas kernels for 0%

profile of v1, /device:TPU:0, one launch (start us, length us, event | category | flops | bytes accessed | tf_op | source)
XLA Modules:
  0.0 694.9 jit_solution(2647751796080765288)
XLA Ops:
  6.7 8.0 %all-to-all-start = ((bf16[16,4,7168]{2,1,0:T(4,128)(2,1)}), bf16[16,4,7168]{2,1,0:T(4,128)(2,1)S(1)}, u32[]{:S(2)}, u32[]{:S(2)}) async-start(bf16[16,4,7168]{2,1,0:T(4,128)(2,1)} %all_to_all.176), calls=%async_computation | async-start | bytes 1835008 | tf_op jit(solution)/shard_map/all_to_all | solution.py:67
  16.7 14.1 %all-to-all-done = bf16[16,4,7168]{2,1,0:T(4,128)(2,1)S(1)} async-done(((bf16[16,4,7168]{2,1,0:T(4,128)(2,1)}), bf16[16,4,7168]{2,1,0:T(4,128)(2,1)S(1)}, u32[]{:S(2)}, u32[]{:S(2)}) %all-to-all-start) | async-done | bytes 917536 | tf_op jit(solution)/shard_map/all_to_all | solution.py:67
  31.0 4.5 fusion.53
  35.4 8.0 %convolution_convert_fusion.10 = bf16[64,7168]{1,0:T(8,128)(2,1)S(1)} fusion(bf16[1,512,7168]{2,1,0:T(8,128)(2,1)} %param.15, bf16[64,7168]{1,0:T(8,128)(2,1)S(1)} %all_to_all.178, bf16[1,7168,512]{2,1,0:T(8,128)(2,1)} %param.14, f32[64,512]{1,0:T(8,128)S(1)} %fusion.53), kind=kOutput, calls=%fused_computation.10 | convolution fusion | flops 940179456 | bytes 16646144 | tf_op jit(solution)/shard_map/dot_general | solution.py:77
  48.7 14.4 %all-to-all-done.1 = bf16[16,4,7168]{2,1,0:T(4,128)(2,1)S(1)} async-done(((bf16[16,4,7168]{2,1,0:T(4,128)(2,1)}), bf16[16,4,7168]{2,1,0:T(4,128)(2,1)S(1)}, u32[]{:S(2)}, u32[]{:S(2)}) %all-to-all-start.1) | async-done | bytes 917536 | tf_op jit(solution)/shard_map/all_to_all | solution.py:78
  72.4 14.8 %all-to-all-done.2 = bf16[16,4,7168]{2,1,0:T(4,128)(2,1)S(1)} async-done(((bf16[16,4,7168]{2,1,0:T(4,128)(2,1)}), bf16[16,4,7168]{2,1,0:T(4,128)(2,1)S(1)}, u32[]{:S(2)}, u32[]{:S(2)}) %all-to-all-start.2) | async-done | bytes 917536 | tf_op jit(solution)/shard_map/all_to_all | solution.py:67
  87.4 4.5 fusion.51
  91.9 7.9 %convolution_convert_fusion.9 = bf16[64,7168]{1,0:T(8,128)(2,1)S(1)} fusion(bf16[1,512,7168]{2,1,0:T(8,128)(2,1)} %param.15, bf16[64,7168]{1,0:T(8,128)(2,1)S(1)} %all_to_all.184, bf16[1,7168,512]{2,1,0:T(8,128)(2,1)} %param.14, f32[64,512]{1,0:T(8,128)S(1)} %fusion.51), kind=kOutput, calls=%fused_computation.9 | convolution fusion | flops 940179456 | bytes 16646144 | tf_op jit(solution)/shard_map/dot_general | solution.py:77
  101.1 4.8 all-to-all-start.3
  106.3 18.6 %all-to-all-done.3 = bf16[16,4,7168]{2,1,0:T(4,128)(2,1)S(1)} async-done(((bf16[16,4,7168]{2,1,0:T(4,128)(2,1)}), bf16[16,4,7168]{2,1,0:T(4,128)(2,1)S(1)}, u32[]{:S(2)}, u32[]{:S(2)}) %all-to-all-start.3) | async-done | bytes 917536 | tf_op jit(solution)/shard_map/all_to_all | solution.py:78
  130.7 4.2 all-to-all-start.4
  135.1 16.5 %all-to-all-done.4 = bf16[16,4,7168]{2,1,0:T(4,128)(2,1)S(1)} async-done(((bf16[16,4,7168]{2,1,0:T(4,128)(2,1)}), bf16[16,4,7168]{2,1,0:T(4,128)(2,1)S(1)}, u32[]{:S(2)}, u32[]{:S(2)}) %all-to-all-start.4) | async-done | bytes 917536 | tf_op jit(solution)/shard_map/all_to_all | solution.py:67
  151.8 4.5 fusion.49
  156.3 7.9 %convolution_convert_fusion.8 = bf16[64,7168]{1,0:T(8,128)(2,1)S(1)} fusion(bf16[1,512,7168]{2,1,0:T(8,128)(2,1)} %param.15, bf16[64,7168]{1,0:T(8,128)(2,1)S(1)} %all_to_all.190, bf16[1,7168,512]{2,1,0:T(8,128)(2,1)} %param.14, f32[64,512]{1,0:T(8,128)S(1)} %fusion.49), kind=kOutput, calls=%fused_computation.8 | convolution fusion | flops 940179456 | bytes 16646144 | tf_op jit(solution)/shard_map/dot_general | solution.py:77
  169.7 16.8 %all-to-all-done.5 = bf16[16,4,7168]{2,1,0:T(4,128)(2,1)S(1)} async-done(((bf16[16,4,7168]{2,1,0:T(4,128)(2,1)}), bf16[16,4,7168]{2,1,0:T(4,128)(2,1)S(1)}, u32[]{:S(2)}, u32[]{:S(2)}) %all-to-all-start.5) | async-done | bytes 917536 | tf_op jit(solution)/shard_map/all_to_all | solution.py:78
  195.8 16.4 %all-to-all-done.6 = bf16[16,4,7168]{2,1,0:T(4,128)(2,1)S(1)} async-done(((bf16[16,4,7168]{2,1,0:T(4,128)(2,1)}), bf16[16,4,7168]{2,1,0:T(4,128)(2,1)S(1)}, u32[]{:S(2)}, u32[]{:S(2)}) %all-to-all-start.6) | async-done | bytes 917536 | tf_op jit(solution)/shard_map/all_to_all | solution.py:67
  212.4 4.5 fusion.47
  216.9 7.9 %convolution_convert_fusion.7 = bf16[64,7168]{1,0:T(8,128)(2,1)S(1)} fusion(bf16[1,512,7168]{2,1,0:T(8,128)(2,1)} %param.15, bf16[64,7168]{1,0:T(8,128)(2,1)S(1)} %all_to_all.196, bf16[1,7168,512]{2,1,0:T(8,128)(2,1)} %param.14, f32[64,512]{1,0:T(8,128)S(1)} %fusion.47), kind=kOutput, calls=%fused_computation.7 | convolution fusion | flops 940179456 | bytes 16646144 | tf_op jit(solution)/shard_map/dot_general | solution.py:77
  230.4 16.7 %all-to-all-done.7 = bf16[16,4,7168]{2,1,0:T(4,128)(2,1)S(1)} async-done(((bf16[16,4,7168]{2,1,0:T(4,128)(2,1)}), bf16[16,4,7168]{2,1,0:T(4,128)(2,1)S(1)}, u32[]{:S(2)}, u32[]{:S(2)}) %all-to-all-start.7) | async-done | bytes 917536 | tf_op jit(solution)/shard_map/all_to_all | solution.py:78
  257.3 18.3 %all-to-all-done.8 = bf16[16,4,7168]{2,1,0:T(4,128)(2,1)S(1)} async-done(((bf16[16,4,7168]{2,1,0:T(4,128)(2,1)}), bf16[16,4,7168]{2,1,0:T(4,128)(2,1)S(1)}, u32[]{:S(2)}, u32[]{:S(2)}) %all-to-all-start.8) | async-done | bytes 917536 | tf_op jit(solution)/shard_map/all_to_all | solution.py:67
  275.8 4.5 fusion.45
  280.3 8.0 %convolution_convert_fusion.6 = bf16[64,7168]{1,0:T(8,128)(2,1)S(1)} fusion(bf16[1,512,7168]{2,1,0:T(8,128)(2,1)} %param.15, bf16[64,7168]{1,0:T(8,128)(2,1)S(1)} %all_to_all.202, bf16[1,7168,512]{2,1,0:T(8,128)(2,1)} %param.14, f32[64,512]{1,0:T(8,128)S(1)} %fusion.45), kind=kOutput, calls=%fused_computation.6 | convolution fusion | flops 940179456 | bytes 16646144 | tf_op jit(solution)/shard_map/dot_general | solution.py:77
  294.4 15.1 %all-to-all-done.9 = bf16[16,4,7168]{2,1,0:T(4,128)(2,1)S(1)} async-done(((bf16[16,4,7168]{2,1,0:T(4,128)(2,1)}), bf16[16,4,7168]{2,1,0:T(4,128)(2,1)S(1)}, u32[]{:S(2)}, u32[]{:S(2)}) %all-to-all-start.9) | async-done | bytes 917536 | tf_op jit(solution)/shard_map/all_to_all | solution.py:78
  318.6 17.0 %all-to-all-done.10 = bf16[16,4,7168]{2,1,0:T(4,128)(2,1)S(1)} async-done(((bf16[16,4,7168]{2,1,0:T(4,128)(2,1)}), bf16[16,4,7168]{2,1,0:T(4,128)(2,1)S(1)}, u32[]{:S(2)}, u32[]{:S(2)}) %all-to-all-start.10) | async-done | bytes 917536 | tf_op jit(solution)/shard_map/all_to_all | solution.py:67
  335.8 4.5 fusion.43
  340.3 7.9 %convolution_convert_fusion.5 = bf16[64,7168]{1,0:T(8,128)(2,1)S(1)} fusion(bf16[1,512,7168]{2,1,0:T(8,128)(2,1)} %param.15, bf16[64,7168]{1,0:T(8,128)(2,1)S(1)} %all_to_all.208, bf16[1,7168,512]{2,1,0:T(8,128)(2,1)} %param.14, f32[64,512]{1,0:T(8,128)S(1)} %fusion.43), kind=kOutput, calls=%fused_computation.5 | convolution fusion | flops 940179456 | bytes 16646144 | tf_op jit(solution)/shard_map/dot_general | solution.py:77
  354.3 15.0 %all-to-all-done.11 = bf16[16,4,7168]{2,1,0:T(4,128)(2,1)S(1)} async-done(((bf16[16,4,7168]{2,1,0:T(4,128)(2,1)}), bf16[16,4,7168]{2,1,0:T(4,128)(2,1)S(1)}, u32[]{:S(2)}, u32[]{:S(2)}) %all-to-all-start.11) | async-done | bytes 917536 | tf_op jit(solution)/shard_map/all_to_all | solution.py:78
  378.7 16.2 %all-to-all-done.12 = bf16[16,4,7168]{2,1,0:T(4,128)(2,1)S(1)} async-done(((bf16[16,4,7168]{2,1,0:T(4,128)(2,1)}), bf16[16,4,7168]{2,1,0:T(4,128)(2,1)S(1)}, u32[]{:S(2)}, u32[]{:S(2)}) %all-to-all-start.12) | async-done | bytes 917536 | tf_op jit(solution)/shard_map/all_to_all | solution.py:67
  395.1 4.5 fusion.41
  399.5 7.9 %convolution_convert_fusion.4 = bf16[64,7168]{1,0:T(8,128)(2,1)S(1)} fusion(bf16[1,512,7168]{2,1,0:T(8,128)(2,1)} %param.15, bf16[64,7168]{1,0:T(8,128)(2,1)S(1)} %all_to_all.214, bf16[1,7168,512]{2,1,0:T(8,128)(2,1)} %param.14, f32[64,512]{1,0:T(8,128)S(1)} %fusion.41), kind=kOutput, calls=%fused_computation.4 | convolution fusion | flops 940179456 | bytes 16646144 | tf_op jit(solution)/shard_map/dot_general | solution.py:77
  413.5 14.9 %all-to-all-done.13 = bf16[16,4,7168]{2,1,0:T(4,128)(2,1)S(1)} async-done(((bf16[16,4,7168]{2,1,0:T(4,128)(2,1)}), bf16[16,4,7168]{2,1,0:T(4,128)(2,1)S(1)}, u32[]{:S(2)}, u32[]{:S(2)}) %all-to-all-start.13) | async-done | bytes 917536 | tf_op jit(solution)/shard_map/all_to_all | solution.py:78
  437.5 16.2 %all-to-all-done.14 = bf16[16,4,7168]{2,1,0:T(4,128)(2,1)S(1)} async-done(((bf16[16,4,7168]{2,1,0:T(4,128)(2,1)}), bf16[16,4,7168]{2,1,0:T(4,128)(2,1)S(1)}, u32[]{:S(2)}, u32[]{:S(2)}) %all-to-all-start.14) | async-done | bytes 917536 | tf_op jit(solution)/shard_map/all_to_all | solution.py:67
  454.0 4.5 fusion.39
  458.4 7.9 %convolution_convert_fusion.3 = bf16[64,7168]{1,0:T(8,128)(2,1)S(1)} fusion(bf16[1,512,7168]{2,1,0:T(8,128)(2,1)} %param.15, bf16[64,7168]{1,0:T(8,128)(2,1)S(1)} %all_to_all.220, bf16[1,7168,512]{2,1,0:T(8,128)(2,1)} %param.14, f32[64,512]{1,0:T(8,128)S(1)} %fusion.39), kind=kOutput, calls=%fused_computation.3 | convolution fusion | flops 940179456 | bytes 16646144 | tf_op jit(solution)/shard_map/dot_general | solution.py:77
  472.4 14.9 %all-to-all-done.15 = bf16[16,4,7168]{2,1,0:T(4,128)(2,1)S(1)} async-done(((bf16[16,4,7168]{2,1,0:T(4,128)(2,1)}), bf16[16,4,7168]{2,1,0:T(4,128)(2,1)S(1)}, u32[]{:S(2)}, u32[]{:S(2)}) %all-to-all-start.15) | async-done | bytes 917536 | tf_op jit(solution)/shard_map/all_to_all | solution.py:78
  491.9 3.9 all-to-all-start.16
  496.7 16.2 %all-to-all-done.16 = bf16[16,4,7168]{2,1,0:T(4,128)(2,1)S(1)} async-done(((bf16[16,4,7168]{2,1,0:T(4,128)(2,1)}), bf16[16,4,7168]{2,1,0:T(4,128)(2,1)S(1)}, u32[]{:S(2)}, u32[]{:S(2)}) %all-to-all-start.16) | async-done | bytes 917536 | tf_op jit(solution)/shard_map/all_to_all | solution.py:67
  513.1 4.5 fusion.37
  517.5 7.9 %convolution_convert_fusion.2 = bf16[64,7168]{1,0:T(8,128)(2,1)S(1)} fusion(bf16[1,512,7168]{2,1,0:T(8,128)(2,1)} %param.15, bf16[64,7168]{1,0:T(8,128)(2,1)S(1)} %all_to_all.226, bf16[1,7168,512]{2,1,0:T(8,128)(2,1)} %param.14, f32[64,512]{1,0:T(8,128)S(1)} %fusion.37), kind=kOutput, calls=%fused_computation.2 | convolution fusion | flops 940179456 | bytes 16646144 | tf_op jit(solution)/shard_map/dot_general | solution.py:77
  531.5 14.9 %all-to-all-done.17 = bf16[16,4,7168]{2,1,0:T(4,128)(2,1)S(1)} async-done(((bf16[16,4,7168]{2,1,0:T(4,128)(2,1)}), bf16[16,4,7168]{2,1,0:T(4,128)(2,1)S(1)}, u32[]{:S(2)}, u32[]{:S(2)}) %all-to-all-start.17) | async-done | bytes 917536 | tf_op jit(solution)/shard_map/all_to_all | solution.py:78
  555.5 16.2 %all-to-all-done.18 = bf16[16,4,7168]{2,1,0:T(4,128)(2,1)S(1)} async-done(((bf16[16,4,7168]{2,1,0:T(4,128)(2,1)}), bf16[16,4,7168]{2,1,0:T(4,128)(2,1)S(1)}, u32[]{:S(2)}, u32[]{:S(2)}) %all-to-all-start.18) | async-done | bytes 917536 | tf_op jit(solution)/shard_map/all_to_all | solution.py:67
  572.0 4.5 fusion.35
  576.4 7.9 %convolution_convert_fusion.1 = bf16[64,7168]{1,0:T(8,128)(2,1)S(1)} fusion(bf16[1,512,7168]{2,1,0:T(8,128)(2,1)} %param.15, bf16[64,7168]{1,0:T(8,128)(2,1)S(1)} %all_to_all.232, bf16[1,7168,512]{2,1,0:T(8,128)(2,1)} %param.14, f32[64,512]{1,0:T(8,128)S(1)} %fusion.35), kind=kOutput, calls=%fused_computation.1 | convolution fusion | flops 940179456 | bytes 16646144 | tf_op jit(solution)/shard_map/dot_general | solution.py:77
  590.4 14.9 %all-to-all-done.19 = bf16[16,4,7168]{2,1,0:T(4,128)(2,1)S(1)} async-done(((bf16[16,4,7168]{2,1,0:T(4,128)(2,1)}), bf16[16,4,7168]{2,1,0:T(4,128)(2,1)S(1)}, u32[]{:S(2)}, u32[]{:S(2)}) %all-to-all-start.19) | async-done | bytes 917536 | tf_op jit(solution)/shard_map/all_to_all | solution.py:78
  613.6 44.9 %psum.7 = f32[8]{0:T(128)S(1)} all-reduce(f32[8]{0:T(128)S(1)} %copy-done.9), channel_id=1, replica_groups=mesh['section'=8,'ep'=16] {'ep'}, use_global_device_ids=true, to_apply=%region_46.47 | all-reduce | flops 8 | bytes 64 | tf_op jit(solution)/shard_map/psum | solution.py:46
  662.2 4.5 fusion.33
  666.7 7.9 %convolution_convert_fusion = bf16[64,7168]{1,0:T(8,128)(2,1)S(1)} fusion(bf16[1,512,7168]{2,1,0:T(8,128)(2,1)} %param.15, bf16[64,7168]{1,0:T(8,128)(2,1)S(1)} %all_to_all.238, bf16[1,7168,512]{2,1,0:T(8,128)(2,1)} %param.14, f32[64,512]{1,0:T(8,128)S(1)} %fusion.33), kind=kOutput, calls=%fused_computation | convolution fusion | flops 940179456 | bytes 16646144 | tf_op jit(solution)/shard_map/dot_general | solution.py:77
  679.9 12.0 %all-to-all-done.21 = bf16[16,4,7168]{2,1,0:T(4,128)(2,1)S(1)} async-done(((bf16[16,4,7168]{2,1,0:T(4,128)(2,1)}), bf16[16,4,7168]{2,1,0:T(4,128)(2,1)S(1)}, u32[]{:S(2)}, u32[]{:S(2)}) %all-to-all-start.21) | async-done | bytes 917536 | tf_op jit(solution)/shard_map/all_to_all | solution.py:78
  (267 shorter events, 157.6 us)
Async XLA Ops:
  0.6 14.9 %copy-start = (bf16[1,7168,8]{1,2,0:T(8,128)(2,1)S(1)}, bf16[1,7168,8]{1,2,0:T(8,128)(2,1)}, u32[]{:S(2)}) copy-start(bf16[1,7168,8]{1,2,0:T(8,128)(2,1)} %param.12) | copy-start | bytes 344068
  6.7 24.0 %all-to-all-start = ((bf16[16,4,7168]{2,1,0:T(4,128)(2,1)}), bf16[16,4,7168]{2,1,0:T(4,128)(2,1)S(1)}, u32[]{:S(2)}, u32[]{:S(2)}) async-start(bf16[16,4,7168]{2,1,0:T(4,128)(2,1)} %all_to_all.176), calls=%async_computation | async-start | bytes 1835008 | tf_op jit(solution)/shard_map/all_to_all | solution.py:67
  35.4 28.2 %copy-start.2 = (bf16[4,8,7168]{2,1,0:T(8,128)(2,1)S(1)}, bf16[4,8,7168]{2,1,0:T(8,128)(2,1)}, u32[]{:S(2)}) copy-start(bf16[4,8,7168]{2,1,0:T(8,128)(2,1)} %param.8) | copy-start | bytes 1376260
  43.4 23.3 %copy-start.1 = (f32[1,7168]{1,0:T(1,128)S(1)}, f32[1,7168]{1,0:T(1,128)}, u32[]{:S(2)}) copy-start(f32[1,7168]{1,0:T(1,128)} %param.11) | copy-start | bytes 86020
  44.7 18.5 %all-to-all-start.1 = ((bf16[16,4,7168]{2,1,0:T(4,128)(2,1)}), bf16[16,4,7168]{2,1,0:T(4,128)(2,1)S(1)}, u32[]{:S(2)}, u32[]{:S(2)}) async-start(bf16[16,4,7168]{2,1,0:T(4,128)(2,1)} %all_to_all.179), calls=%async_computation.1 | async-start | bytes 1835008 | tf_op jit(solution)/shard_map/all_to_all | solution.py:78
  64.3 2.2 collective-permute-start
  68.5 18.7 %all-to-all-start.2 = ((bf16[16,4,7168]{2,1,0:T(4,128)(2,1)}), bf16[16,4,7168]{2,1,0:T(4,128)(2,1)S(1)}, u32[]{:S(2)}, u32[]{:S(2)}) async-start(bf16[16,4,7168]{2,1,0:T(4,128)(2,1)} %all_to_all.182), calls=%async_computation.2 | async-start | bytes 1835008 | tf_op jit(solution)/shard_map/all_to_all | solution.py:67
  101.1 23.8 %all-to-all-start.3 = ((bf16[16,4,7168]{2,1,0:T(4,128)(2,1)}), bf16[16,4,7168]{2,1,0:T(4,128)(2,1)S(1)}, u32[]{:S(2)}, u32[]{:S(2)}) async-start(bf16[16,4,7168]{2,1,0:T(4,128)(2,1)} %all_to_all.185), calls=%async_computation.3 | async-start | bytes 1835008 | tf_op jit(solution)/shard_map/all_to_all | solution.py:78
  126.0 2.8 collective-permute-start.1
  130.7 20.9 %all-to-all-start.4 = ((bf16[16,4,7168]{2,1,0:T(4,128)(2,1)}), bf16[16,4,7168]{2,1,0:T(4,128)(2,1)S(1)}, u32[]{:S(2)}, u32[]{:S(2)}) async-start(bf16[16,4,7168]{2,1,0:T(4,128)(2,1)} %all_to_all.188), calls=%async_computation.4 | async-start | bytes 1835008 | tf_op jit(solution)/shard_map/all_to_all | solution.py:67
  165.5 21.0 %all-to-all-start.5 = ((bf16[16,4,7168]{2,1,0:T(4,128)(2,1)}), bf16[16,4,7168]{2,1,0:T(4,128)(2,1)S(1)}, u32[]{:S(2)}, u32[]{:S(2)}) async-start(bf16[16,4,7168]{2,1,0:T(4,128)(2,1)} %all_to_all.191), calls=%async_computation.5 | async-start | bytes 1835008 | tf_op jit(solution)/shard_map/all_to_all | solution.py:78
  187.6 2.4 collective-permute-start.2
  191.9 20.3 %all-to-all-start.6 = ((bf16[16,4,7168]{2,1,0:T(4,128)(2,1)}), bf16[16,4,7168]{2,1,0:T(4,128)(2,1)S(1)}, u32[]{:S(2)}, u32[]{:S(2)}) async-start(bf16[16,4,7168]{2,1,0:T(4,128)(2,1)} %all_to_all.194), calls=%async_computation.6 | async-start | bytes 1835008 | tf_op jit(solution)/shard_map/all_to_all | solution.py:67
  226.1 21.0 %all-to-all-start.7 = ((bf16[16,4,7168]{2,1,0:T(4,128)(2,1)}), bf16[16,4,7168]{2,1,0:T(4,128)(2,1)S(1)}, u32[]{:S(2)}, u32[]{:S(2)}) async-start(bf16[16,4,7168]{2,1,0:T(4,128)(2,1)} %all_to_all.197), calls=%async_computation.7 | async-start | bytes 1835008 | tf_op jit(solution)/shard_map/all_to_all | solution.py:78
  248.3 2.4 collective-permute-start.3
  252.6 23.0 %all-to-all-start.8 = ((bf16[16,4,7168]{2,1,0:T(4,128)(2,1)}), bf16[16,4,7168]{2,1,0:T(4,128)(2,1)S(1)}, u32[]{:S(2)}, u32[]{:S(2)}) async-start(bf16[16,4,7168]{2,1,0:T(4,128)(2,1)} %all_to_all.200), calls=%async_computation.8 | async-start | bytes 1835008 | tf_op jit(solution)/shard_map/all_to_all | solution.py:67
  280.3 29.6 %copy-start.3 = (bf16[11,8,7168]{2,1,0:T(8,128)(2,1)S(1)}, bf16[11,8,7168]{2,1,0:T(8,128)(2,1)}, u32[]{:S(2)}) copy-start(bf16[11,8,7168]{2,1,0:T(8,128)(2,1)} %get-tuple-element.38) | copy-start | bytes 3784708
  288.3 23.0 %copy-start.8 = (f32[1,64,8]{2,1,0:T(8,128)S(1)}, f32[1,64,8]{2,1,0:T(8,128)}, u32[]{:S(2)}) copy-start(f32[1,64,8]{2,1,0:T(8,128)} %get-tuple-element.57) | copy-start | bytes 6148
  289.6 19.9 %all-to-all-start.9 = ((bf16[16,4,7168]{2,1,0:T(4,128)(2,1)}), bf16[16,4,7168]{2,1,0:T(4,128)(2,1)S(1)}, u32[]{:S(2)}, u32[]{:S(2)}) async-start(bf16[16,4,7168]{2,1,0:T(4,128)(2,1)} %all_to_all.203), calls=%async_computation.9 | async-start | bytes 1835008 | tf_op jit(solution)/shard_map/all_to_all | solution.py:78
  310.0 2.2 collective-permute-start.4
  314.1 21.5 %all-to-all-start.10 = ((bf16[16,4,7168]{2,1,0:T(4,128)(2,1)}), bf16[16,4,7168]{2,1,0:T(4,128)(2,1)S(1)}, u32[]{:S(2)}, u32[]{:S(2)}) async-start(bf16[16,4,7168]{2,1,0:T(4,128)(2,1)} %all_to_all.206), calls=%async_computation.10 | async-start | bytes 1835008 | tf_op jit(solution)/shard_map/all_to_all | solution.py:67
  348.2 22.9 %copy-start.7 = (f32[1,64,8]{2,1,0:T(8,128)S(1)}, f32[1,64,8]{2,1,0:T(8,128)}, u32[]{:S(2)}) copy-start(f32[1,64,8]{2,1,0:T(8,128)} %get-tuple-element.56) | copy-start | bytes 6148
  349.5 19.8 %all-to-all-start.11 = ((bf16[16,4,7168]{2,1,0:T(4,128)(2,1)}), bf16[16,4,7168]{2,1,0:T(4,128)(2,1)S(1)}, u32[]{:S(2)}, u32[]{:S(2)}) async-start(bf16[16,4,7168]{2,1,0:T(4,128)(2,1)} %all_to_all.209), calls=%async_computation.11 | async-start | bytes 1835008 | tf_op jit(solution)/shard_map/all_to_all | solution.py:78
  369.8 2.2 collective-permute-start.5
  374.0 20.9 %all-to-all-start.12 = ((bf16[16,4,7168]{2,1,0:T(4,128)(2,1)}), bf16[16,4,7168]{2,1,0:T(4,128)(2,1)S(1)}, u32[]{:S(2)}, u32[]{:S(2)}) async-start(bf16[16,4,7168]{2,1,0:T(4,128)(2,1)} %all_to_all.212), calls=%async_computation.12 | async-start | bytes 1835008 | tf_op jit(solution)/shard_map/all_to_all | solution.py:67
  407.5 22.7 %copy-start.6 = (f32[1,64,8]{2,1,0:T(8,128)S(1)}, f32[1,64,8]{2,1,0:T(8,128)}, u32[]{:S(2)}) copy-start(f32[1,64,8]{2,1,0:T(8,128)} %get-tuple-element.55) | copy-start | bytes 6148
  408.7 19.7 %all-to-all-start.13 = ((bf16[16,4,7168]{2,1,0:T(4,128)(2,1)}), bf16[16,4,7168]{2,1,0:T(4,128)(2,1)S(1)}, u32[]{:S(2)}, u32[]{:S(2)}) async-start(bf16[16,4,7168]{2,1,0:T(4,128)(2,1)} %all_to_all.215), calls=%async_computation.13 | async-start | bytes 1835008 | tf_op jit(solution)/shard_map/all_to_all | solution.py:78
  428.9 2.2 collective-permute-start.6
  433.0 20.7 %all-to-all-start.14 = ((bf16[16,4,7168]{2,1,0:T(4,128)(2,1)}), bf16[16,4,7168]{2,1,0:T(4,128)(2,1)S(1)}, u32[]{:S(2)}, u32[]{:S(2)}) async-start(bf16[16,4,7168]{2,1,0:T(4,128)(2,1)} %all_to_all.218), calls=%async_computation.14 | async-start | bytes 1835008 | tf_op jit(solution)/shard_map/all_to_all | solution.py:67
  466.3 22.7 %copy-start.5 = (f32[1,64,8]{2,1,0:T(8,128)S(1)}, f32[1,64,8]{2,1,0:T(8,128)}, u32[]{:S(2)}) copy-start(f32[1,64,8]{2,1,0:T(8,128)} %get-tuple-element.54) | copy-start | bytes 6148
  467.6 19.7 %all-to-all-start.15 = ((bf16[16,4,7168]{2,1,0:T(4,128)(2,1)}), bf16[16,4,7168]{2,1,0:T(4,128)(2,1)S(1)}, u32[]{:S(2)}, u32[]{:S(2)}) async-start(bf16[16,4,7168]{2,1,0:T(4,128)(2,1)} %all_to_all.221), calls=%async_computation.15 | async-start | bytes 1835008 | tf_op jit(solution)/shard_map/all_to_all | solution.py:78
  487.8 2.2 collective-permute-start.7
  491.9 20.9 %all-to-all-start.16 = ((bf16[16,4,7168]{2,1,0:T(4,128)(2,1)}), bf16[16,4,7168]{2,1,0:T(4,128)(2,1)S(1)}, u32[]{:S(2)}, u32[]{:S(2)}) async-start(bf16[16,4,7168]{2,1,0:T(4,128)(2,1)} %all_to_all.224), calls=%async_computation.16 | async-start | bytes 1835008 | tf_op jit(solution)/shard_map/all_to_all | solution.py:67
  525.4 22.7 %copy-start.4 = (f32[1,64,8]{2,1,0:T(8,128)S(1)}, f32[1,64,8]{2,1,0:T(8,128)}, u32[]{:S(2)}) copy-start(f32[1,64,8]{2,1,0:T(8,128)} %get-tuple-element.53) | copy-start | bytes 6148
  526.7 19.7 %all-to-all-start.17 = ((bf16[16,4,7168]{2,1,0:T(4,128)(2,1)}), bf16[16,4,7168]{2,1,0:T(4,128)(2,1)S(1)}, u32[]{:S(2)}, u32[]{:S(2)}) async-start(bf16[16,4,7168]{2,1,0:T(4,128)(2,1)} %all_to_all.227), calls=%async_computation.17 | async-start | bytes 1835008 | tf_op jit(solution)/shard_map/all_to_all | solution.py:78
  546.9 2.2 collective-permute-start.8
  551.0 20.7 %all-to-all-start.18 = ((bf16[16,4,7168]{2,1,0:T(4,128)(2,1)}), bf16[16,4,7168]{2,1,0:T(4,128)(2,1)S(1)}, u32[]{:S(2)}, u32[]{:S(2)}) async-start(bf16[16,4,7168]{2,1,0:T(4,128)(2,1)} %all_to_all.230), calls=%async_computation.18 | async-start | bytes 1835008 | tf_op jit(solution)/shard_map/all_to_all | solution.py:67
  584.4 29.2 %copy-start.9 = (f32[8]{0:T(128)S(1)}, f32[8]{0:T(128)}, u32[]{:S(2)}) copy-start(f32[8]{0:T(128)} %get-tuple-element.24) | copy-start | bytes 100
  585.6 19.7 %all-to-all-start.19 = ((bf16[16,4,7168]{2,1,0:T(4,128)(2,1)}), bf16[16,4,7168]{2,1,0:T(4,128)(2,1)S(1)}, u32[]{:S(2)}, u32[]{:S(2)}) async-start(bf16[16,4,7168]{2,1,0:T(4,128)(2,1)} %all_to_all.233), calls=%async_computation.19 | async-start | bytes 1835008 | tf_op jit(solution)/shard_map/all_to_all | solution.py:78
  605.8 2.2 collective-permute-start.9
  609.9 52.0 %all-to-all-start.20 = ((bf16[16,4,7168]{2,1,0:T(4,128)(2,1)}), bf16[16,4,7168]{2,1,0:T(4,128)(2,1)S(1)}, u32[]{:S(2)}, u32[]{:S(2)}) async-start(bf16[16,4,7168]{2,1,0:T(4,128)(2,1)} %all_to_all.236), calls=%async_computation.20 | async-start | bytes 1835008 | tf_op jit(solution)/shard_map/all_to_all | solution.py:67
  675.9 16.1 %all-to-all-start.21 = ((bf16[16,4,7168]{2,1,0:T(4,128)(2,1)}), bf16[16,4,7168]{2,1,0:T(4,128)(2,1)S(1)}, u32[]{:S(2)}, u32[]{:S(2)}) async-start(bf16[16,4,7168]{2,1,0:T(4,128)(2,1)} %all_to_all.239), calls=%async_computation.21 | async-start | bytes 1835008 | tf_op jit(solution)/shard_map/all_to_all | solution.py:78

commit v2 on v1

v2 whole, which is shorter than its diff:
```python
import functools

import jax
import jax.numpy as jnp
from jax import lax
from jax.experimental import pallas as pl
from jax.experimental.pallas import tpu as pltpu
from jax.sharding import PartitionSpec as P

FFW = 1024
BLK = 256
VM = pl.BlockSpec(memory_space=pltpu.VMEM)
SM = pl.BlockSpec(memory_space=pltpu.SMEM)
F32 = jnp.float32
BF16 = jnp.bfloat16


def shifted(block, axis, distance):
    devices = range(lax.axis_size(axis))
    route = [(i - distance, i) for i in devices if i - distance in devices]
    return lax.ppermute(block, axis, route)


def pre_kernel(tick, place_ref, rows_ref, came_ref, gain_ref, router_ref, pack_ref, unpack_ref, routed_ref, extra_ref,
               send_ref, mix_ref, input_ref):
    micro_count = pack_ref.shape[0]
    section = place_ref[0]
    m = jnp.clip(tick - section, 0, micro_count - 1)
    half = rows_ref.shape[2] // 2
    if tick == 0:
        x = rows_ref[0]
        send_ref[:, half:] = extra_ref[...]
    elif tick < micro_count:
        x = jnp.where(section == 0, rows_ref[tick].astype(F32), came_ref[...].astype(F32)).astype(BF16)
    else:
        x = came_ref[...]
    input_ref[...] = x
    x = x.astype(F32)
    mean_square = jnp.mean(x * x, axis=-1, keepdims=True)
    normed = x * lax.rsqrt(mean_square + 1e-06) * gain_ref[...]
    halves = jnp.concatenate([normed[:, :half], normed[:, half:]], axis=0).astype(BF16)
    send_ref[:, :half] = jnp.dot(pack_ref[m], halves, preferred_element_type=F32).astype(BF16)
    logits = lax.dot_general(
        normed.astype(BF16), router_ref[...], (((1,), (1,)), ((), ())), preferred_element_type=F32
    )
    scores = routed_ref[m] / (1.0 + jnp.exp(-logits))
    gates = 2.5 * scores / jnp.sum(scores, axis=1, keepdims=True)
    experts = gates.shape[1]
    rows = send_ref.shape[0]
    owner = lax.broadcasted_iota(jnp.int32, (gates.shape[0], rows), 1) // (rows // experts)
    wide = jnp.zeros(owner.shape, F32)
    for e in range(experts):
        wide = jnp.where(owner == e, gates[:, e : e + 1], wide)
    mix = jnp.concatenate([wide, wide], axis=0) * unpack_ref[m]
    high = mix.astype(BF16)
    mix_ref[: mix.shape[0]] = high
    mix_ref[mix.shape[0] :] = (mix - high.astype(F32)).astype(BF16)


def expert_kernel(rows_ref, gate_ref, up_ref, down_ref, *rest):
    if len(rest) == 4:
        load_ref, out_ref, total_ref, act_ref = rest
        units = jnp.sum(rows_ref[:, out_ref.shape[1] :].astype(F32), axis=0, keepdims=True) * 0.125
        total_ref[...] = units * load_ref[0:1] + load_ref[1:2]
    else:
        out_ref, act_ref = rest
    count, half = out_ref.shape
    hidden = gate_ref.shape[1]
    left = rows_ref[:, :half]
    keep = lax.broadcasted_iota(jnp.int32, (count, 256), 0) % 8 < 4

    def joined(w_ref, cols):
        a = jnp.dot(left, w_ref[:half, cols], preferred_element_type=F32)
        b = jnp.dot(left, w_ref[half:, cols], preferred_element_type=F32)
        return a + pltpu.roll(b, count - 4, 0)

    for n in range(hidden // 256):
        cols = slice(n * 256, n * 256 + 256)
        g = joined(gate_ref, cols)
        u = joined(up_ref, cols)
        act = g / (1.0 + jnp.exp(-g)) * u
        act = jnp.where(keep, act, 0.0)
        act_ref[:, cols] = act.astype(BF16)
        act_ref[:, n * 256 + hidden : n * 256 + hidden + 256] = pltpu.roll(act, 4, 0).astype(BF16)
    first = act_ref[:, :hidden]
    second = act_ref[:, hidden:]
    wide = half // 2
    for n in range(2):
        cols = slice(n * wide, n * wide + wide)
        rest = slice(half + n * wide, half + n * wide + wide)
        out = jnp.dot(first, down_ref[:, cols], preferred_element_type=F32) + jnp.dot(
            second, down_ref[:, rest], preferred_element_type=F32
        )
        out_ref[:, cols] = out.astype(BF16)


def post_kernel(tick, place_ref, x_ref, back_ref, mix_ref, sofar_ref, out_ref, kept_ref):
    half = back_ref.shape[1]
    tokens = x_ref.shape[0]
    both = jnp.dot(mix_ref[...], back_ref[...], preferred_element_type=F32)
    total = both[: 2 * tokens] + both[2 * tokens :]
    x = x_ref[...].astype(F32)
    left = (x[:, :half] + total[:tokens]).astype(BF16)
    right = (x[:, half:] + total[tokens:]).astype(BF16)
    out_ref[:, :half] = left
    out_ref[:, half:] = right
    m = tick - place_ref[0]

    @pl.when((m >= 0) & (m < kept_ref.shape[0]))
    def _():
        kept_ref[m, :, :half] = left
        kept_ref[m, :, half:] = right


def local(rows_in, routes, hot_blocks, gains, router, w_gate, w_up, w_down):
    section_index = lax.axis_index("section")
    ep_index = lax.axis_index("ep")
    section_count = lax.axis_size("section")
    ep_count = lax.axis_size("ep")
    micro_count, tok_rows, model_width = rows_in.shape
    expert_count = router.shape[2]
    top_count = routes.shape[3]
    capacity = tok_rows // 2
    half = model_width // 2
    count = ep_count * 2 * capacity
    hidden = w_gate.shape[2]
    blocks_per_expert = FFW // BLK
    hot_index = hot_blocks[0]
    owner_index = hot_index // 2
    hot_expert = hot_index // blocks_per_expert
    expert_ids = lax.iota(jnp.int32, expert_count)

    member = (routes[0][:, :, :, None] == expert_ids).astype(F32)
    routed = jnp.sum(member, axis=2)
    before = (
        lax.broadcasted_iota(jnp.int32, (tok_rows, tok_rows), 0)
        > lax.broadcasted_iota(jnp.int32, (tok_rows, tok_rows), 1)
    ).astype(F32)
    slot_rank = jnp.einsum("ts,mse->mte", before, routed)
    slot_ids = lax.iota(F32, capacity)
    placement = routed[..., None] * (slot_rank[..., None] == slot_ids).astype(F32)
    halves = jnp.eye(2, dtype=F32)
    unpack = (
        placement[:, None, :, :, None, None, :]
        * halves[None, :, None, None, None, :, None]
        * jnp.ones((1, 1, 1, 1, 2, 1, 1), F32)
    ).reshape(micro_count, 2 * tok_rows, count)
    pack = unpack.transpose(0, 2, 1).astype(BF16)

    expert_load = jnp.sum(routed, axis=(0, 1))
    extra = jnp.broadcast_to(
        jnp.repeat(expert_load, 4 * capacity)[:, None], (count, 128)
    ).astype(BF16)
    hot_one = (expert_ids == hot_expert).astype(F32)
    mean_units = float(micro_count * tok_rows * top_count * blocks_per_expert)
    load_info = jnp.broadcast_to(
        jnp.stack(
            [2.0 - (owner_index == ep_index).astype(F32), jnp.sum(expert_load * hot_one)]
        )[:, None] / mean_units,
        (2, 128),
    )

    pack, unpack, routed, extra, load_info = lax.optimization_barrier(
        (pack, unpack, routed, extra, load_info)
    )
    router_t = router[0].T
    place = section_index.reshape(1)
    resident = functools.partial(pltpu.with_memory_space_constraint, memory_space=pltpu.VMEM)
    gate_w, up_w, down_w = resident(w_gate[0]), resident(w_up[0]), resident(w_down[0])
    row_shape = jax.ShapeDtypeStruct((tok_rows, model_width), BF16)

    def pre(tick, came):
        return pl.pallas_call(
            functools.partial(pre_kernel, tick),
            out_shape=(
                jax.ShapeDtypeStruct((count, half + (128 if tick == 0 else 0)), BF16),
                jax.ShapeDtypeStruct((4 * tok_rows, count), BF16),
                row_shape,
            ),
            in_specs=[SM] + [VM] * 8,
            out_specs=(VM, VM, VM),
            compiler_params=pltpu.CompilerParams(vmem_limit_bytes=8 << 20),
            name="pre",
        )(place, rows_in, came, gains, router_t, pack, unpack, routed, extra)

    def experts(rows, *load):
        out_shape = [jax.ShapeDtypeStruct((count, half), BF16)]
        out_shape += [jax.ShapeDtypeStruct((1, 128), F32) for _ in load]
        return pl.pallas_call(
            expert_kernel,
            out_shape=out_shape,
            in_specs=[VM] * (4 + len(load)),
            out_specs=[VM] * len(out_shape),
            scratch_shapes=[pltpu.VMEM((count, 2 * hidden), BF16)],
            compiler_params=pltpu.CompilerParams(vmem_limit_bytes=12 << 20),
            name="experts",
        )(rows, gate_w, up_w, down_w, *load)

    def post(tick, x, back, mix, kept):
        return pl.pallas_call(
            functools.partial(post_kernel, tick),
            out_shape=(row_shape, jax.ShapeDtypeStruct(kept.shape, kept.dtype)),
            in_specs=[SM] + [VM] * 4,
            out_specs=(VM, VM),
            input_output_aliases={4: 1},
            compiler_params=pltpu.CompilerParams(vmem_limit_bytes=8 << 20),
            name="post",
        )(place, x, back, mix, resident(kept))

    def exchange(block):
        return lax.all_to_all(block, "ep", split_axis=0, concat_axis=0, tiled=True)

    incoming = jnp.zeros((tok_rows, model_width), BF16)
    kept = jnp.zeros(rows_in.shape, BF16)
    last = micro_count + section_count - 2
    for tick in range(last + 1):
        send, mix, layer_input = pre(tick, incoming)
        received = exchange(send)
        if tick == 0:
            part, relative = experts(received, load_info)
        else:
            (part,) = experts(received)
        next_rows, kept = post(tick, layer_input, exchange(part), mix, kept)
        if tick < last:
            incoming = shifted(next_rows, "section", 1)
    return (kept[None], relative[:, :1])


def solution(mesh):
    return jax.shard_map(
        local,
        mesh=mesh,
        in_specs=(
            P(None, "ep", None),
            P("section", None, "ep", None),
            P("section"),
            P("section", None),
            P("section", None, None),
            P("section", None, "ep"),
            P("section", None, "ep"),
            P("section", "ep", None),
        ),
        out_specs=(P("section", None, "ep", None), P("section", "ep")),
        check_vma=False,
    )
```

time: 706 us -> 523 us (0.74)
  blocking collectives: 44.9 us -> 417 us
  waiting for transfers between devices: 339 us -> 9.41 us
  matrix products: 152 us -> 0.19 us
  starting transfers between devices: 101 us -> 16.9 us
  Pallas kernels: 0 us -> 47.7 us
  local copies, waits for them, and re-layouts: 36.6 us -> 17.2 us
  other arithmetic: 16.2 us -> 3.24 us
    all_to_all x0 -> x22, blocking collectives: none -> 417 us  [exchange(): return lax.all_to_all(block, 'ep', split_axis=0, concat_axis=0, tiled=True)]
    all_to_all x22 -> x0, waiting for transfers between devices: 330 us -> none  [the longest x11 168 us: apply_layer(): back = lax.all_to_all(part, 'ep', split_axis=0, concat_axis=0, tiled=True)]
    dot_general x55 -> x0, matrix products: 152 us -> none  [the longest x11 87.2 us: apply_layer(): jnp.dot(activation, down_w, preferred_element_type=jnp.float32)]
    all_to_all x22 -> x0, starting transfers between devices: 86.9 us -> none  [the longest x11 45.5 us: apply_layer(): recv = lax.all_to_all(send, 'ep', split_axis=0, concat_axis=0, tiled=True)]
    pallas_call x0 -> x33, Pallas kernels: none -> 47.7 us  [the longest x11 35.1 us: experts(): pl.pallas_call(expert_kernel, out_shape=out_shape, in_specs=[VM] * (4 + l...]
    psum x1 -> x0, blocking collectives: 44.9 us -> none  [local(): expert_total = lax.psum(expert_load, 'ep')]
    all_to_all x44 -> x0, local copies, waits for them, and re-layouts: 32.5 us -> none  [the longest x22 16.3 us: apply_layer(): recv = lax.all_to_all(send, 'ep', split_axis=0, concat_axis=0, tiled=True)]
    unnamed x20 -> x27, local copies, waits for them, and re-layouts: 0.06 us -> 12.7 us
  transfers between devices with their start and end apart: 32 -> 10, of which waited for: 31 -> 10; matrix products, arithmetic and copies ran while one was open for 3% -> 0% of each run, Pallas kernels for 0% -> 0%
where the time goes in v2:
time: 523 us; the launch traced here: 514 us
  blocking collectives  417 us (80%)
  Pallas kernels  47.7 us (9%)
  local copies, waits for them, and re-layouts  17.2 us (3%)
  starting transfers between devices  16.9 us (3%)
  waiting for transfers between devices  9.41 us (2%)
    all_to_all x22, blocking collectives, exchange(): return lax.all_to_all(block, 'ep', split_axis=0, concat_axis=0, tiled=True)  417 us
    pallas_call x11, Pallas kernels, experts(): pl.pallas_call(expert_kernel, out_shape=out_shape, in_specs=[VM] * (4 + l...  35.1 us
    ppermute x10, starting transfers between devices, shifted(): return lax.ppermute(block, axis, route)  16.9 us
    unnamed x27, local copies, waits for them, and re-layouts  12.7 us
  transfers between devices with their start and end apart: 10, of which 10 were waited for; matrix products, arithmetic and copies ran while one was open for 0% of the time, Pallas kernels for 0%

profile of v2, /device:TPU:0, one launch (start us, length us, event | category | flops | bytes accessed | tf_op | source)
XLA Modules:
  0.0 514.1 jit_solution(9154016007295811152)
XLA Ops:
  4.2 2.1 reshape.97
  8.2 1.0 copy.55.unpack_ref
  12.7 23.9 %all_to_all.242 = bf16[16,8,3712]{2,1,0:T(8,128)(2,1)S(1)} all-to-all(bf16[16,8,3712]{2,1,0:T(8,128)(2,1)S(1)} %bitcast.150), channel_id=1, replica_groups=mesh['section'=8,'ep'=16] {'ep'}, dimensions={0} | all-to-all | bytes 1900544 | tf_op jit(solution)/shard_map/all_to_all | solution.py:211
  36.6 3.1 copy-done
  39.7 3.1 copy-done.1
  42.8 3.1 copy-done.3
  45.9 3.6 experts.11
  49.5 18.4 %all_to_all.243 = bf16[16,8,3584]{2,1,0:T(8,128)(2,1)S(1)} all-to-all(bf16[16,8,3584]{2,1,0:T(8,128)(2,1)S(1)} %bitcast.152), channel_id=1, replica_groups=mesh['section'=8,'ep'=16] {'ep'}, dimensions={0} | all-to-all | bytes 1835008 | tf_op jit(solution)/shard_map/all_to_all | solution.py:211
  68.1 1.3 collective-permute-start
  71.3 18.2 %all_to_all.244 = bf16[16,8,3584]{2,1,0:T(8,128)(2,1)S(1)} all-to-all(bf16[16,8,3584]{2,1,0:T(8,128)(2,1)S(1)} %bitcast.153), channel_id=1, replica_groups=mesh['section'=8,'ep'=16] {'ep'}, dimensions={0} | all-to-all | bytes 1835008 | tf_op jit(solution)/shard_map/all_to_all | solution.py:211
  89.5 3.2 experts.12
  92.7 19.3 %all_to_all.245 = bf16[16,8,3584]{2,1,0:T(8,128)(2,1)S(1)} all-to-all(bf16[16,8,3584]{2,1,0:T(8,128)(2,1)S(1)} %bitcast.131), channel_id=1, replica_groups=mesh['section'=8,'ep'=16] {'ep'}, dimensions={0} | all-to-all | bytes 1835008 | tf_op jit(solution)/shard_map/all_to_all | solution.py:211
  112.2 2.3 collective-permute-start.1
  116.3 17.6 %all_to_all.246 = bf16[16,8,3584]{2,1,0:T(8,128)(2,1)S(1)} all-to-all(bf16[16,8,3584]{2,1,0:T(8,128)(2,1)S(1)} %bitcast.154), channel_id=1, replica_groups=mesh['section'=8,'ep'=16] {'ep'}, dimensions={0} | all-to-all | bytes 1835008 | tf_op jit(solution)/shard_map/all_to_all | solution.py:211
  133.9 3.2 experts.13
  137.0 19.2 %all_to_all.247 = bf16[16,8,3584]{2,1,0:T(8,128)(2,1)S(1)} all-to-all(bf16[16,8,3584]{2,1,0:T(8,128)(2,1)S(1)} %bitcast.133), channel_id=1, replica_groups=mesh['section'=8,'ep'=16] {'ep'}, dimensions={0} | all-to-all | bytes 1835008 | tf_op jit(solution)/shard_map/all_to_all | solution.py:211
  156.5 2.9 collective-permute-start.2
  161.3 17.8 %all_to_all.248 = bf16[16,8,3584]{2,1,0:T(8,128)(2,1)S(1)} all-to-all(bf16[16,8,3584]{2,1,0:T(8,128)(2,1)S(1)} %bitcast.155), channel_id=1, replica_groups=mesh['section'=8,'ep'=16] {'ep'}, dimensions={0} | all-to-all | bytes 1835008 | tf_op jit(solution)/shard_map/all_to_all | solution.py:211
  179.0 3.2 experts.14
  182.2 19.3 %all_to_all.249 = bf16[16,8,3584]{2,1,0:T(8,128)(2,1)S(1)} all-to-all(bf16[16,8,3584]{2,1,0:T(8,128)(2,1)S(1)} %bitcast.135), channel_id=1, replica_groups=mesh['section'=8,'ep'=16] {'ep'}, dimensions={0} | all-to-all | bytes 1835008 | tf_op jit(solution)/shard_map/all_to_all | solution.py:211
  201.7 2.6 collective-permute-start.3
  206.1 19.7 %all_to_all.250 = bf16[16,8,3584]{2,1,0:T(8,128)(2,1)S(1)} all-to-all(bf16[16,8,3584]{2,1,0:T(8,128)(2,1)S(1)} %bitcast.156), channel_id=1, replica_groups=mesh['section'=8,'ep'=16] {'ep'}, dimensions={0} | all-to-all | bytes 1835008 | tf_op jit(solution)/shard_map/all_to_all | solution.py:211
  225.8 3.2 experts.15
  228.9 18.8 %all_to_all.251 = bf16[16,8,3584]{2,1,0:T(8,128)(2,1)S(1)} all-to-all(bf16[16,8,3584]{2,1,0:T(8,128)(2,1)S(1)} %bitcast.137), channel_id=1, replica_groups=mesh['section'=8,'ep'=16] {'ep'}, dimensions={0} | all-to-all | bytes 1835008 | tf_op jit(solution)/shard_map/all_to_all | solution.py:211
  248.0 1.3 collective-permute-start.4
  251.1 19.2 %all_to_all.252 = bf16[16,8,3584]{2,1,0:T(8,128)(2,1)S(1)} all-to-all(bf16[16,8,3584]{2,1,0:T(8,128)(2,1)S(1)} %bitcast.157), channel_id=1, replica_groups=mesh['section'=8,'ep'=16] {'ep'}, dimensions={0} | all-to-all | bytes 1835008 | tf_op jit(solution)/shard_map/all_to_all | solution.py:211
  270.2 3.2 experts.16
  273.4 18.3 %all_to_all.253 = bf16[16,8,3584]{2,1,0:T(8,128)(2,1)S(1)} all-to-all(bf16[16,8,3584]{2,1,0:T(8,128)(2,1)S(1)} %bitcast.139), channel_id=1, replica_groups=mesh['section'=8,'ep'=16] {'ep'}, dimensions={0} | all-to-all | bytes 1835008 | tf_op jit(solution)/shard_map/all_to_all | solution.py:211
  292.0 1.3 collective-permute-start.5
  295.1 19.2 %all_to_all.254 = bf16[16,8,3584]{2,1,0:T(8,128)(2,1)S(1)} all-to-all(bf16[16,8,3584]{2,1,0:T(8,128)(2,1)S(1)} %bitcast.158), channel_id=1, replica_groups=mesh['section'=8,'ep'=16] {'ep'}, dimensions={0} | all-to-all | bytes 1835008 | tf_op jit(solution)/shard_map/all_to_all | solution.py:211
  314.2 3.2 experts.17
  317.4 18.3 %all_to_all.255 = bf16[16,8,3584]{2,1,0:T(8,128)(2,1)S(1)} all-to-all(bf16[16,8,3584]{2,1,0:T(8,128)(2,1)S(1)} %bitcast.141), channel_id=1, replica_groups=mesh['section'=8,'ep'=16] {'ep'}, dimensions={0} | all-to-all | bytes 1835008 | tf_op jit(solution)/shard_map/all_to_all | solution.py:211
  335.9 1.3 collective-permute-start.6
  339.0 19.4 %all_to_all.256 = bf16[16,8,3584]{2,1,0:T(8,128)(2,1)S(1)} all-to-all(bf16[16,8,3584]{2,1,0:T(8,128)(2,1)S(1)} %bitcast.159), channel_id=1, replica_groups=mesh['section'=8,'ep'=16] {'ep'}, dimensions={0} | all-to-all | bytes 1835008 | tf_op jit(solution)/shard_map/all_to_all | solution.py:211
  358.4 3.2 experts.18
  361.6 18.3 %all_to_all.257 = bf16[16,8,3584]{2,1,0:T(8,128)(2,1)S(1)} all-to-all(bf16[16,8,3584]{2,1,0:T(8,128)(2,1)S(1)} %bitcast.143), channel_id=1, replica_groups=mesh['section'=8,'ep'=16] {'ep'}, dimensions={0} | all-to-all | bytes 1835008 | tf_op jit(solution)/shard_map/all_to_all | solution.py:211
  380.1 1.3 collective-permute-start.7
  383.2 19.2 %all_to_all.258 = bf16[16,8,3584]{2,1,0:T(8,128)(2,1)S(1)} all-to-all(bf16[16,8,3584]{2,1,0:T(8,128)(2,1)S(1)} %bitcast.160), channel_id=1, replica_groups=mesh['section'=8,'ep'=16] {'ep'}, dimensions={0} | all-to-all | bytes 1835008 | tf_op jit(solution)/shard_map/all_to_all | solution.py:211
  402.4 3.2 experts.19
  405.5 18.3 %all_to_all.259 = bf16[16,8,3584]{2,1,0:T(8,128)(2,1)S(1)} all-to-all(bf16[16,8,3584]{2,1,0:T(8,128)(2,1)S(1)} %bitcast.145), channel_id=1, replica_groups=mesh['section'=8,'ep'=16] {'ep'}, dimensions={0} | all-to-all | bytes 1835008 | tf_op jit(solution)/shard_map/all_to_all | solution.py:211
  424.1 1.3 collective-permute-start.8
  427.2 19.2 %all_to_all.260 = bf16[16,8,3584]{2,1,0:T(8,128)(2,1)S(1)} all-to-all(bf16[16,8,3584]{2,1,0:T(8,128)(2,1)S(1)} %bitcast.161), channel_id=1, replica_groups=mesh['section'=8,'ep'=16] {'ep'}, dimensions={0} | all-to-all | bytes 1835008 | tf_op jit(solution)/shard_map/all_to_all | solution.py:211
  446.3 3.2 experts.20
  449.5 18.6 %all_to_all.261 = bf16[16,8,3584]{2,1,0:T(8,128)(2,1)S(1)} all-to-all(bf16[16,8,3584]{2,1,0:T(8,128)(2,1)S(1)} %bitcast.147), channel_id=1, replica_groups=mesh['section'=8,'ep'=16] {'ep'}, dimensions={0} | all-to-all | bytes 1835008 | tf_op jit(solution)/shard_map/all_to_all | solution.py:211
  468.3 1.3 collective-permute-start.9
  471.4 19.2 %all_to_all.262 = bf16[16,8,3584]{2,1,0:T(8,128)(2,1)S(1)} all-to-all(bf16[16,8,3584]{2,1,0:T(8,128)(2,1)S(1)} %bitcast.151), channel_id=1, replica_groups=mesh['section'=8,'ep'=16] {'ep'}, dimensions={0} | all-to-all | bytes 1835008 | tf_op jit(solution)/shard_map/all_to_all | solution.py:211
  490.6 3.2 experts.21
  493.7 18.3 %all_to_all.263 = bf16[16,8,3584]{2,1,0:T(8,128)(2,1)S(1)} all-to-all(bf16[16,8,3584]{2,1,0:T(8,128)(2,1)S(1)} %bitcast.149), channel_id=1, replica_groups=mesh['section'=8,'ep'=16] {'ep'}, dimensions={0} | all-to-all | bytes 1835008 | tf_op jit(solution)/shard_map/all_to_all | solution.py:211
  (73 shorter events, 30.3 us)
Async XLA Ops:
  3.1 86.4 %slice-start = ((s8[7340032]{0:T(1024)(128)(4,1)}), s8[3145728]{0:T(1024)(128)(4,1)S(1)}, s32[]{:S(2)}) async-start(s8[7340032]{0:T(1024)(128)(4,1)} %bitcast.73), calls=%async_computation.22 | async-start | bytes 6291456
  9.2 1.0 copy-start.5
  10.3 0.9 copy-start.7
  11.2 0.7 copy-start.9
  36.6 3.1 copy-start
  39.7 3.1 copy-start.1
  42.8 3.1 copy-start.3
  45.8 24.6 %copy-start.6 = (bf16[4,8,7168]{2,1,0:T(8,128)(2,1)S(1)}, bf16[4,8,7168]{2,1,0:T(8,128)(2,1)}, u32[]{:S(2)}) copy-start(bf16[4,8,7168]{2,1,0:T(8,128)(2,1)} %rows_ref.21) | copy-start | bytes 1376260
  45.9 24.6 %copy-start.8 = (bf16[1,7168,8]{1,2,0:T(8,128)(2,1)S(1)}, bf16[1,7168,8]{1,2,0:T(8,128)(2,1)}, u32[]{:S(2)}) copy-start(bf16[1,7168,8]{1,2,0:T(8,128)(2,1)} %param.12) | copy-start | bytes 344068
  45.9 24.6 %copy-start.10 = (f32[1,7168]{1,0:T(1,128)S(1)}, f32[1,7168]{1,0:T(1,128)}, u32[]{:S(2)}) copy-start(f32[1,7168]{1,0:T(1,128)} %gain_ref.21) | copy-start | bytes 86020
  45.9 43.7 %slice-start.1 = ((s8[7340032]{0:T(1024)(128)(4,1)}), s8[4194304]{0:T(1024)(128)(4,1)S(1)}, s32[]{:S(2)}) async-start(s8[7340032]{0:T(1024)(128)(4,1)} %bitcast.73), calls=%async_computation.23 | async-start | bytes 8388608
  45.9 43.6 %copy-start.2 = (bf16[1,7168,512]{2,1,0:T(8,128)(2,1)S(1)}, bf16[1,7168,512]{2,1,0:T(8,128)(2,1)}, u32[]{:S(2)}) copy-start(bf16[1,7168,512]{2,1,0:T(8,128)(2,1)} %param.14) | copy-start | bytes 22020100
  45.9 43.6 %copy-start.4 = (bf16[1,512,7168]{2,1,0:T(8,128)(2,1)S(1)}, bf16[1,512,7168]{2,1,0:T(8,128)(2,1)}, u32[]{:S(2)}) copy-start(bf16[1,512,7168]{2,1,0:T(8,128)(2,1)} %param.15) | copy-start | bytes 22020100
  68.1 2.2 collective-permute-start
  112.2 3.2 collective-permute-start.1
  156.5 3.9 collective-permute-start.2
  201.7 3.5 collective-permute-start.3
  248.0 2.2 collective-permute-start.4
  292.0 2.2 collective-permute-start.5
  335.9 2.2 collective-permute-start.6
  380.1 2.2 collective-permute-start.7
  424.1 2.2 collective-permute-start.8
  468.3 2.2 collective-permute-start.9

commit v3 on v2

v3 whole, which is shorter than its diff:
```python
import functools

import jax
import jax.numpy as jnp
from jax import lax
from jax.experimental import pallas as pl
from jax.experimental.pallas import tpu as pltpu
from jax.sharding import PartitionSpec as P

FFW = 1024
BLK = 256
VM = pl.BlockSpec(memory_space=pltpu.VMEM)
SM = pl.BlockSpec(memory_space=pltpu.SMEM)
F32 = jnp.float32
BF16 = jnp.bfloat16


def live_hop(block, axis, tick, micro_count):
    last = lax.axis_size(axis) - 1
    route = [(s, s + 1) for s in range(last) if 0 <= tick - s < micro_count]
    return lax.ppermute(block, axis, route)


def row_ids(rows, lanes, experts, capacity):
    row = lax.broadcasted_iota(jnp.int32, (rows, lanes), 1)
    return row // (lanes // experts), row // capacity % 2, row % capacity


def column(routes, k):
    tokens = routes.shape[1]
    shape = (tokens, tokens)
    same = lax.broadcasted_iota(jnp.int32, shape, 0) == lax.broadcasted_iota(jnp.int32, shape, 1)
    spread = jnp.broadcast_to(routes[k : k + 1].astype(F32), shape)
    return jnp.sum(jnp.where(same, spread, 0.0), axis=1, keepdims=True)


def plan(hot_ref, routes_ref, unpack_ref, info_ref):
    micro_count, top_count, tokens = routes_ref.shape
    lanes = unpack_ref.shape[2]
    expert, half_id, slot = row_ids(tokens, lanes, 8, tokens // 2)
    before = (
        lax.broadcasted_iota(jnp.int32, (tokens, tokens), 0)
        > lax.broadcasted_iota(jnp.int32, (tokens, tokens), 1)
    ).astype(BF16)
    counts = jnp.zeros((tokens, lanes), F32)
    for m in range(micro_count):
        ids = routes_ref[m]
        hit = jnp.zeros((tokens, lanes), F32)
        for k in range(top_count):
            hit = hit + (column(ids, k) == expert.astype(F32)).astype(F32)
        rank = jnp.dot(before, hit.astype(BF16), preferred_element_type=F32)
        placed = jnp.where(rank == slot.astype(F32), hit, 0.0)
        unpack_ref[m, :tokens] = jnp.where(half_id == 0, placed, 0.0)
        unpack_ref[m, tokens:] = jnp.where(half_id == 1, placed, 0.0)
        counts = counts + hit
    counts = jnp.sum(counts, axis=0, keepdims=True)
    hot = hot_ref[0]
    device = lax.axis_index("ep")
    lane = lax.broadcasted_iota(jnp.int32, counts.shape, 1)
    per = lanes // 8
    homes = 2.0 - (hot // 2 == device).astype(F32)
    info_ref[0:1] = jnp.where(lane == device // 2 * per, homes, 0.0)
    info_ref[1:2] = jnp.where(lane == hot // (FFW // BLK) * per, counts, 0.0)
    return counts


def pre_kernel(tick, *refs):
    if tick == 0:
        hot_ref, *sources, send_ref, mix_ref, input_ref, unpack_ref, info_ref = refs[:10]
        rows_ref, gain_ref, router_ref, routes_ref, sems = refs[10:]
        copies = [
            pltpu.make_async_copy(source, held, sems.at[i])
            for i, (source, held) in enumerate(zip(sources, refs[10:14]))
        ]
        for copy in copies:
            copy.start()
        for copy in copies:
            copy.wait()
    else:
        rows_ref, gain_ref, router_ref, routes_ref, unpack_ref, came_ref, send_ref, mix_ref, input_ref = refs
    micro_count, tokens, width = rows_ref.shape
    half = width // 2
    section = lax.axis_index("section")
    m = jnp.clip(tick - section, 0, micro_count - 1)
    if tick == 0:
        counts = plan(hot_ref, routes_ref, unpack_ref, info_ref)
        send_ref[:, half:] = jnp.broadcast_to(
            counts, (send_ref.shape[0], counts.shape[1])
        ).astype(BF16)
        x = rows_ref[0]
    else:
        x = came_ref[...]
        if tick < micro_count:
            x = jnp.where(section == 0, rows_ref[tick].astype(F32), x.astype(F32)).astype(BF16)
    input_ref[...] = x
    x = x.astype(F32)
    mean_square = jnp.mean(x * x, axis=-1, keepdims=True)
    normed = x * lax.rsqrt(mean_square + 1e-06) * gain_ref[...]
    halves = jnp.concatenate([normed[:, :half], normed[:, half:]], axis=0).astype(BF16)
    unpack = unpack_ref[m]
    send_ref[:, :half] = lax.dot_general(
        unpack.astype(BF16), halves, (((0,), (0,)), ((), ())), preferred_element_type=F32
    ).astype(BF16)
    logits = lax.dot_general(
        normed.astype(BF16), router_ref[...], (((1,), (1,)), ((), ())), preferred_element_type=F32
    )
    experts = router_ref.shape[0]
    ids = routes_ref[m]
    expert = lax.broadcasted_iota(jnp.int32, (tokens, experts), 1)
    routed = jnp.zeros((tokens, experts), F32)
    for k in range(ids.shape[0]):
        routed = routed + (column(ids, k) == expert.astype(F32)).astype(F32)
    scores = routed / (1.0 + jnp.exp(-logits))
    gates = 2.5 * scores / jnp.sum(scores, axis=1, keepdims=True)
    owner = row_ids(tokens, unpack.shape[1], experts, tokens // 2)[0]
    wide = jnp.zeros(owner.shape, F32)
    for e in range(experts):
        wide = jnp.where(owner == e, gates[:, e : e + 1], wide)
    mix = jnp.concatenate([wide, wide], axis=0) * unpack
    high = mix.astype(BF16)
    mix_ref[: mix.shape[0]] = high
    mix_ref[mix.shape[0] :] = (mix - high.astype(F32)).astype(BF16)


def product(rows_ref, gate_ref, up_ref, down_ref, out_ref, act_ref, arrived):
    count, half = out_ref.shape
    hidden = gate_ref.shape[1]
    left = rows_ref[:, :half]
    keep = lax.broadcasted_iota(jnp.int32, (count, 256), 0) % 8 < 4

    def joined(w_ref, cols):
        a = jnp.dot(left, w_ref[:half, cols], preferred_element_type=F32)
        b = jnp.dot(left, w_ref[half:, cols], preferred_element_type=F32)
        return a + pltpu.roll(b, count - 4, 0)

    for n in range(hidden // 256):
        cols = slice(n * 256, n * 256 + 256)
        arrived(2 * n)
        g = joined(gate_ref, cols)
        arrived(2 * n + 1)
        u = joined(up_ref, cols)
        act = g / (1.0 + jnp.exp(-g)) * u
        act = jnp.where(keep, act, 0.0)
        act_ref[:, cols] = act.astype(BF16)
        act_ref[:, n * 256 + hidden : n * 256 + hidden + 256] = pltpu.roll(act, 4, 0).astype(BF16)
    first = act_ref[:, :hidden]
    second = act_ref[:, hidden:]
    wide = half // 2
    for n in range(2):
        cols = slice(n * wide, n * wide + wide)
        rest = slice(half + n * wide, half + n * wide + wide)
        arrived(hidden // 128 + n)
        out = jnp.dot(first, down_ref[:, cols], preferred_element_type=F32) + jnp.dot(
            second, down_ref[:, rest], preferred_element_type=F32
        )
        out_ref[:, cols] = out.astype(BF16)


def expert_kernel(rows_ref, gate_ref, up_ref, down_ref, out_ref, act_ref):
    product(rows_ref, gate_ref, up_ref, down_ref, out_ref, act_ref, lambda step: None)


def first_kernel(info_ref, rows_ref, gate_hbm, up_hbm, down_hbm,
                 out_ref, load_ref, gate_ref, up_ref, down_ref, act_ref, sems):
    half = out_ref.shape[1]
    hidden = gate_ref.shape[1]
    wide = half // 2
    steps = []
    for n in range(hidden // 256):
        cols = slice(n * 256, n * 256 + 256)
        steps.append([(gate_hbm, gate_ref, cols)])
        steps.append([(up_hbm, up_ref, cols)])
    for n in range(2):
        steps.append(
            [(down_hbm, down_ref, slice(c + n * wide, c + n * wide + wide)) for c in (0, half)]
        )
    copies = []
    for step in steps:
        started = []
        for src, dst, cols in step:
            index = sum(map(len, copies)) + len(started)
            copy = pltpu.make_async_copy(src.at[:, cols], dst.at[:, cols], sems.at[index])
            copy.start()
            started.append(copy)
        copies.append(started)

    units = jnp.sum(rows_ref[:, half:].astype(F32), axis=0, keepdims=True) * 0.125
    load_ref[...] = jnp.broadcast_to(
        jnp.sum(units * info_ref[0:1] + info_ref[1:2], axis=1, keepdims=True) / 256.0, load_ref.shape
    )

    def arrived(step):
        for copy in copies[step]:
            copy.wait()

    product(rows_ref, gate_ref, up_ref, down_ref, out_ref, act_ref, arrived)


def post_kernel(tick, x_ref, back_ref, mix_ref, *rest):
    out_ref, kept_ref = rest[-2:]
    half = back_ref.shape[1]
    tokens = x_ref.shape[0]
    both = jnp.dot(mix_ref[...], back_ref[...], preferred_element_type=F32)
    total = both[: 2 * tokens] + both[2 * tokens :]
    x = x_ref[...].astype(F32)
    left = (x[:, :half] + total[:tokens]).astype(BF16)
    right = (x[:, half:] + total[tokens:]).astype(BF16)
    out_ref[:, :half] = left
    out_ref[:, half:] = right
    m = tick - lax.axis_index("section")

    @pl.when((m >= 0) & (m < kept_ref.shape[0]))
    def _():
        kept_ref[m, :, :half] = left
        kept_ref[m, :, half:] = right


def local(rows_in, routes, hot_blocks, gains, router, w_gate, w_up, w_down):
    section_count = lax.axis_size("section")
    ep_count = lax.axis_size("ep")
    micro_count, tok_rows, model_width = rows_in.shape
    half = model_width // 2
    count = ep_count * tok_rows
    hidden = w_gate.shape[2]
    resident = functools.partial(pltpu.with_memory_space_constraint, memory_space=pltpu.VMEM)
    outside = functools.partial(pltpu.with_memory_space_constraint, memory_space=pltpu.HBM)
    HB = pl.BlockSpec(memory_space=pltpu.HBM)
    router_t = router[0].T
    routes_t = routes[0].transpose(0, 2, 1)
    row_shape = jax.ShapeDtypeStruct((tok_rows, model_width), BF16)

    def params(mib):
        return pltpu.CompilerParams(vmem_limit_bytes=mib << 20)

    def pre(tick, *more):
        out_shape = [
            jax.ShapeDtypeStruct((count, half + (count if tick == 0 else 0)), BF16),
            jax.ShapeDtypeStruct((4 * tok_rows, count), BF16),
            row_shape,
        ]
        if tick == 0:
            out_shape += [
                jax.ShapeDtypeStruct((micro_count, 2 * tok_rows, count), F32),
                jax.ShapeDtypeStruct((2, count), F32),
            ]
        values = (rows_in, gains, router_t, routes_t)
        if tick == 0:
            values = (hot_blocks, *map(outside, values))
            specs = [SM] + [HB] * 4
            scratch = [pltpu.VMEM(v.shape, v.dtype) for v in values[1:]]
            scratch += [pltpu.SemaphoreType.DMA((4,))]
        else:
            values += more
            specs = [VM] * len(values)
            scratch = []
        return pl.pallas_call(
            functools.partial(pre_kernel, tick),
            out_shape=out_shape,
            in_specs=specs,
            out_specs=[VM] * len(out_shape),
            scratch_shapes=scratch,
            compiler_params=params(8),
            name="pre",
        )(*values)

    part_shape = jax.ShapeDtypeStruct((count, half), BF16)
    act_shape = pltpu.VMEM((count, 2 * hidden), BF16)
    weights = (w_gate[0], w_up[0], w_down[0])

    def first(rows, info):
        return pl.pallas_call(
            first_kernel,
            out_shape=[part_shape, jax.ShapeDtypeStruct((1, 128), F32)]
            + [pltpu.VMEM(w.shape, w.dtype) for w in weights],
            in_specs=[VM, VM] + [HB] * 3,
            out_specs=[VM] * 5,
            scratch_shapes=[act_shape, pltpu.SemaphoreType.DMA((8,))],
            compiler_params=params(12),
            name="first",
        )(info, rows, *map(outside, weights))

    def experts(rows, held):
        return pl.pallas_call(
            expert_kernel,
            out_shape=part_shape,
            in_specs=[VM] * 4,
            out_specs=VM,
            scratch_shapes=[act_shape],
            compiler_params=params(12),
            name="experts",
        )(rows, *map(resident, held))

    def post(tick, x, back, mix, *kept):
        return pl.pallas_call(
            functools.partial(post_kernel, tick),
            out_shape=(row_shape, pltpu.VMEM(rows_in.shape, BF16)),
            in_specs=[VM] * (3 + len(kept)),
            out_specs=(VM, VM),
            input_output_aliases={3: 1} if kept else {},
            compiler_params=params(8),
            name="post",
        )(x, back, mix, *map(resident, kept))

    def exchange(block):
        return lax.all_to_all(block, "ep", split_axis=0, concat_axis=0, tiled=True)

    kept = ()
    last = micro_count + section_count - 2
    for tick in range(last + 1):
        if tick == 0:
            send, mix, layer_input, unpack, info = pre(tick)
            part, relative, *held = first(exchange(send), info)
        else:
            send, mix, layer_input = pre(tick, unpack, incoming)
            part = experts(exchange(send), held)
        next_rows, *kept = post(tick, layer_input, exchange(part), mix, *kept)
        if tick < last:
            incoming = live_hop(next_rows, "section", tick, micro_count)
    return (kept[0][None], relative[:, :1])


def solution(mesh):
    return jax.shard_map(
        local,
        mesh=mesh,
        in_specs=(
            P(None, "ep", None),
            P("section", None, "ep", None),
            P("section"),
            P("section", None),
            P("section", None, None),
            P("section", None, "ep"),
            P("section", None, "ep"),
            P("section", "ep", None),
        ),
        out_specs=(P("section", None, "ep", None), P("section", "ep")),
        check_vma=False,
    )
```

time: 523 us -> 489 us (0.935)
  the two profiles are of different devices: /device:TPU:0 before, /device:TPU:16 now
where the time goes in v3:
time: 489 us; the launch traced here: 481 us
  blocking collectives  372 us (76%)
  Pallas kernels  53.7 us (11%)
  waiting for transfers between devices  41.2 us (8%)
  starting transfers between devices  11.7 us (2%)
    all_to_all x22, blocking collectives, exchange(): return lax.all_to_all(block, 'ep', split_axis=0, concat_axis=0, tiled=True)  372 us
    ppermute x10, waiting for transfers between devices, live_hop(): return lax.ppermute(block, axis, route)  41.2 us
    pallas_call x10, Pallas kernels, experts(): pl.pallas_call(expert_kernel, out_shape=part_shape, in_specs=[VM] * 4, ou...  31.7 us
    ppermute x10, starting transfers between devices, live_hop(): return lax.ppermute(block, axis, route)  11.7 us
    pallas_call x11, Pallas kernels, pre(): pl.pallas_call(functools.partial(pre_kernel, tick), out_shape=out_shape,...  10.4 us
  transfers between devices with their start and end apart: 10, of which 5 were waited for; matrix products, arithmetic and copies ran while one was open for 0% of the time, Pallas kernels for 0%

profile of v3, /device:TPU:16, one launch (start us, length us, event | category | flops | bytes accessed | tf_op | source)
XLA Modules:
  0.0 481.3 jit_solution(1436395549492327962)
XLA Ops:
  1.3 2.0 pre.11
  3.3 23.8 %all_to_all.242 = bf16[16,8,3712]{2,1,0:T(8,128)(2,1)S(1)} all-to-all(bf16[16,8,3712]{2,1,0:T(8,128)(2,1)S(1)} %bitcast.99), channel_id=1, replica_groups=mesh['section'=8,'ep'=16] {'ep'}, dimensions={0} | all-to-all | bytes 1900544 | tf_op jit(solution)/shard_map/all_to_all | solution.py:305
  27.1 8.2 %first.1 = (bf16[128,3584]{1,0:T(8,128)(2,1)S(1)}, f32[1,128]{1,0:T(1,128)}, bf16[7168,512]{1,0:T(8,128)(2,1)S(1)}, bf16[7168,512]{1,0:T(8,128)(2,1)S(1)}, bf16[512,7168]{1,0:T(8,128)(2,1)S(1)}) custom-call(f32[2,128]{1,0:T(2,128)S(1)} %get-tuple-element.65.info_ref, bf16[128,3712]{1,0:T(8,128)(2,1)S(1)} %bitcast.67, bf16[7168,512]{1,0:T(8,128)(2,1)} %bitcast.122, ...), custom_call_target="tpu_custom_call" | custom-call | tf_op jit(solution)/shard_map/first/pallas_call | solution.py:271
  35.3 18.2 %all_to_all.243 = bf16[16,8,3584]{2,1,0:T(8,128)(2,1)S(1)} all-to-all(bf16[16,8,3584]{2,1,0:T(8,128)(2,1)S(1)} %bitcast.100), channel_id=1, replica_groups=mesh['section'=8,'ep'=16] {'ep'}, dimensions={0} | all-to-all | bytes 1835008 | tf_op jit(solution)/shard_map/all_to_all | solution.py:305
  54.5 0.9 pre.12
  55.4 16.8 %all_to_all.244 = bf16[16,8,3584]{2,1,0:T(8,128)(2,1)S(1)} all-to-all(bf16[16,8,3584]{2,1,0:T(8,128)(2,1)S(1)} %bitcast.102), channel_id=1, replica_groups=mesh['section'=8,'ep'=16] {'ep'}, dimensions={0} | all-to-all | bytes 1835008 | tf_op jit(solution)/shard_map/all_to_all | solution.py:305
  72.2 3.2 experts.10
  75.3 15.7 %all_to_all.245 = bf16[16,8,3584]{2,1,0:T(8,128)(2,1)S(1)} all-to-all(bf16[16,8,3584]{2,1,0:T(8,128)(2,1)S(1)} %bitcast.82), channel_id=1, replica_groups=mesh['section'=8,'ep'=16] {'ep'}, dimensions={0} | all-to-all | bytes 1835008 | tf_op jit(solution)/shard_map/all_to_all | solution.py:305
  92.0 0.9 pre.13
  92.8 15.3 %all_to_all.246 = bf16[16,8,3584]{2,1,0:T(8,128)(2,1)S(1)} all-to-all(bf16[16,8,3584]{2,1,0:T(8,128)(2,1)S(1)} %bitcast.103), channel_id=1, replica_groups=mesh['section'=8,'ep'=16] {'ep'}, dimensions={0} | all-to-all | bytes 1835008 | tf_op jit(solution)/shard_map/all_to_all | solution.py:305
  108.2 3.2 experts.11
  111.3 15.1 %all_to_all.247 = bf16[16,8,3584]{2,1,0:T(8,128)(2,1)S(1)} all-to-all(bf16[16,8,3584]{2,1,0:T(8,128)(2,1)S(1)} %bitcast.84), channel_id=1, replica_groups=mesh['section'=8,'ep'=16] {'ep'}, dimensions={0} | all-to-all | bytes 1835008 | tf_op jit(solution)/shard_map/all_to_all | solution.py:305
  127.4 0.9 pre.14
  128.3 15.1 %all_to_all.248 = bf16[16,8,3584]{2,1,0:T(8,128)(2,1)S(1)} all-to-all(bf16[16,8,3584]{2,1,0:T(8,128)(2,1)S(1)} %bitcast.104), channel_id=1, replica_groups=mesh['section'=8,'ep'=16] {'ep'}, dimensions={0} | all-to-all | bytes 1835008 | tf_op jit(solution)/shard_map/all_to_all | solution.py:305
  143.4 3.2 experts.12
  146.6 15.2 %all_to_all.249 = bf16[16,8,3584]{2,1,0:T(8,128)(2,1)S(1)} all-to-all(bf16[16,8,3584]{2,1,0:T(8,128)(2,1)S(1)} %bitcast.86), channel_id=1, replica_groups=mesh['section'=8,'ep'=16] {'ep'}, dimensions={0} | all-to-all | bytes 1835008 | tf_op jit(solution)/shard_map/all_to_all | solution.py:305
  162.1 1.3 collective-permute-start.3
  163.4 14.6 %collective-permute-done.3.refs_5_ = bf16[8,7168]{1,0:T(8,128)(2,1)S(1)} collective-permute-done((bf16[8,7168]{1,0:T(8,128)(2,1)S(1)}, bf16[8,7168]{1,0:T(8,128)(2,1)S(1)}, u32[]{:S(2)}, u32[]{:S(2)}) %collective-permute-start.3) | collective-permute-done | bytes 114720 | tf_op jit(solution)/shard_map/ppermute | solution.py:21
  178.9 15.2 %all_to_all.250 = bf16[16,8,3584]{2,1,0:T(8,128)(2,1)S(1)} all-to-all(bf16[16,8,3584]{2,1,0:T(8,128)(2,1)S(1)} %bitcast.105), channel_id=1, replica_groups=mesh['section'=8,'ep'=16] {'ep'}, dimensions={0} | all-to-all | bytes 1835008 | tf_op jit(solution)/shard_map/all_to_all | solution.py:305
  194.1 3.2 experts.13
  197.3 15.6 %all_to_all.251 = bf16[16,8,3584]{2,1,0:T(8,128)(2,1)S(1)} all-to-all(bf16[16,8,3584]{2,1,0:T(8,128)(2,1)S(1)} %bitcast.88), channel_id=1, replica_groups=mesh['section'=8,'ep'=16] {'ep'}, dimensions={0} | all-to-all | bytes 1835008 | tf_op jit(solution)/shard_map/all_to_all | solution.py:305
  213.2 1.9 collective-permute-start.4
  215.1 4.7 collective-permute-done.4.refs_5_
  220.6 15.5 %all_to_all.252 = bf16[16,8,3584]{2,1,0:T(8,128)(2,1)S(1)} all-to-all(bf16[16,8,3584]{2,1,0:T(8,128)(2,1)S(1)} %bitcast.106), channel_id=1, replica_groups=mesh['section'=8,'ep'=16] {'ep'}, dimensions={0} | all-to-all | bytes 1835008 | tf_op jit(solution)/shard_map/all_to_all | solution.py:305
  236.1 3.2 experts.14
  239.3 15.0 %all_to_all.253 = bf16[16,8,3584]{2,1,0:T(8,128)(2,1)S(1)} all-to-all(bf16[16,8,3584]{2,1,0:T(8,128)(2,1)S(1)} %bitcast.90), channel_id=1, replica_groups=mesh['section'=8,'ep'=16] {'ep'}, dimensions={0} | all-to-all | bytes 1835008 | tf_op jit(solution)/shard_map/all_to_all | solution.py:305
  254.6 1.9 collective-permute-start.5
  256.5 7.4 %collective-permute-done.5.refs_5_ = bf16[8,7168]{1,0:T(8,128)(2,1)S(1)} collective-permute-done((bf16[8,7168]{1,0:T(8,128)(2,1)S(1)}, bf16[8,7168]{1,0:T(8,128)(2,1)S(1)}, u32[]{:S(2)}, u32[]{:S(2)}) %collective-permute-start.5) | collective-permute-done | bytes 114720 | tf_op jit(solution)/shard_map/ppermute | solution.py:21
  264.7 15.1 %all_to_all.254 = bf16[16,8,3584]{2,1,0:T(8,128)(2,1)S(1)} all-to-all(bf16[16,8,3584]{2,1,0:T(8,128)(2,1)S(1)} %bitcast.107), channel_id=1, replica_groups=mesh['section'=8,'ep'=16] {'ep'}, dimensions={0} | all-to-all | bytes 1835008 | tf_op jit(solution)/shard_map/all_to_all | solution.py:305
  279.8 3.2 experts.15
  283.0 15.1 %all_to_all.255 = bf16[16,8,3584]{2,1,0:T(8,128)(2,1)S(1)} all-to-all(bf16[16,8,3584]{2,1,0:T(8,128)(2,1)S(1)} %bitcast.92), channel_id=1, replica_groups=mesh['section'=8,'ep'=16] {'ep'}, dimensions={0} | all-to-all | bytes 1835008 | tf_op jit(solution)/shard_map/all_to_all | solution.py:305
  298.3 1.9 collective-permute-start.6
  300.3 13.6 %collective-permute-done.6.refs_5_ = bf16[8,7168]{1,0:T(8,128)(2,1)S(1)} collective-permute-done((bf16[8,7168]{1,0:T(8,128)(2,1)S(1)}, bf16[8,7168]{1,0:T(8,128)(2,1)S(1)}, u32[]{:S(2)}, u32[]{:S(2)}) %collective-permute-start.6) | collective-permute-done | bytes 114720 | tf_op jit(solution)/shard_map/ppermute | solution.py:21
  314.7 17.5 %all_to_all.256 = bf16[16,8,3584]{2,1,0:T(8,128)(2,1)S(1)} all-to-all(bf16[16,8,3584]{2,1,0:T(8,128)(2,1)S(1)} %bitcast.108), channel_id=1, replica_groups=mesh['section'=8,'ep'=16] {'ep'}, dimensions={0} | all-to-all | bytes 1835008 | tf_op jit(solution)/shard_map/all_to_all | solution.py:305
  332.2 3.2 experts.16
  335.4 15.6 %all_to_all.257 = bf16[16,8,3584]{2,1,0:T(8,128)(2,1)S(1)} all-to-all(bf16[16,8,3584]{2,1,0:T(8,128)(2,1)S(1)} %bitcast.94), channel_id=1, replica_groups=mesh['section'=8,'ep'=16] {'ep'}, dimensions={0} | all-to-all | bytes 1835008 | tf_op jit(solution)/shard_map/all_to_all | solution.py:305
  351.3 1.3 collective-permute-start.7
  352.6 0.9 collective-permute-done.7.refs_5_
  354.3 19.2 %all_to_all.258 = bf16[16,8,3584]{2,1,0:T(8,128)(2,1)S(1)} all-to-all(bf16[16,8,3584]{2,1,0:T(8,128)(2,1)S(1)} %bitcast.109), channel_id=1, replica_groups=mesh['section'=8,'ep'=16] {'ep'}, dimensions={0} | all-to-all | bytes 1835008 | tf_op jit(solution)/shard_map/all_to_all | solution.py:305
  373.5 3.2 experts.17
  376.7 18.3 %all_to_all.259 = bf16[16,8,3584]{2,1,0:T(8,128)(2,1)S(1)} all-to-all(bf16[16,8,3584]{2,1,0:T(8,128)(2,1)S(1)} %bitcast.96), channel_id=1, replica_groups=mesh['section'=8,'ep'=16] {'ep'}, dimensions={0} | all-to-all | bytes 1835008 | tf_op jit(solution)/shard_map/all_to_all | solution.py:305
  396.8 20.4 %all_to_all.260 = bf16[16,8,3584]{2,1,0:T(8,128)(2,1)S(1)} all-to-all(bf16[16,8,3584]{2,1,0:T(8,128)(2,1)S(1)} %bitcast.110), channel_id=1, replica_groups=mesh['section'=8,'ep'=16] {'ep'}, dimensions={0} | all-to-all | bytes 1835008 | tf_op jit(solution)/shard_map/all_to_all | solution.py:305
  417.2 3.2 experts.18
  420.4 19.1 %all_to_all.261 = bf16[16,8,3584]{2,1,0:T(8,128)(2,1)S(1)} all-to-all(bf16[16,8,3584]{2,1,0:T(8,128)(2,1)S(1)} %bitcast.98), channel_id=1, replica_groups=mesh['section'=8,'ep'=16] {'ep'}, dimensions={0} | all-to-all | bytes 1835008 | tf_op jit(solution)/shard_map/all_to_all | solution.py:305
  441.2 18.1 %all_to_all.262 = bf16[16,8,3584]{2,1,0:T(8,128)(2,1)S(1)} all-to-all(bf16[16,8,3584]{2,1,0:T(8,128)(2,1)S(1)} %bitcast.101), channel_id=1, replica_groups=mesh['section'=8,'ep'=16] {'ep'}, dimensions={0} | all-to-all | bytes 1835008 | tf_op jit(solution)/shard_map/all_to_all | solution.py:305
  459.3 3.2 experts.19
  462.5 16.8 %all_to_all.263 = bf16[16,8,3584]{2,1,0:T(8,128)(2,1)S(1)} all-to-all(bf16[16,8,3584]{2,1,0:T(8,128)(2,1)S(1)} %bitcast.80), channel_id=1, replica_groups=mesh['section'=8,'ep'=16] {'ep'}, dimensions={0} | all-to-all | bytes 1835008 | tf_op jit(solution)/shard_map/all_to_all | solution.py:305
  479.3 0.9 post.21
  (36 shorter events, 12.4 us)
Async XLA Ops:
  27.1 27.3 %copy-start = (bf16[4,8,7168]{2,1,0:T(8,128)(2,1)S(1)}, bf16[4,8,7168]{2,1,0:T(8,128)(2,1)}, u32[]{:S(2)}) copy-start(bf16[4,8,7168]{2,1,0:T(8,128)(2,1)} %refs_0_.20) | copy-start | bytes 1376260
  27.1 27.3 %copy-start.1 = (bf16[1,7168,8]{1,2,0:T(8,128)(2,1)S(1)}, bf16[1,7168,8]{1,2,0:T(8,128)(2,1)}, u32[]{:S(2)}) copy-start(bf16[1,7168,8]{1,2,0:T(8,128)(2,1)} %param.12) | copy-start | bytes 344068
  27.1 27.3 %copy-start.2 = (f32[1,7168]{1,0:T(1,128)S(1)}, f32[1,7168]{1,0:T(1,128)}, u32[]{:S(2)}) copy-start(f32[1,7168]{1,0:T(1,128)} %refs_1_.21) | copy-start | bytes 86020
  27.1 27.3 %copy-start.3 = (s32[1,4,8,2]{2,3,1,0:T(2,128)S(1)}, s32[1,4,8,2]{2,3,1,0:T(2,128)}, u32[]{:S(2)}) copy-start(s32[1,4,8,2]{2,3,1,0:T(2,128)} %param.9) | copy-start | bytes 772
  53.7 0.7 collective-permute-start
  91.3 0.7 collective-permute-start.1
  126.7 0.7 collective-permute-start.2
  162.1 15.9 %collective-permute-start.3 = (bf16[8,7168]{1,0:T(8,128)(2,1)S(1)}, bf16[8,7168]{1,0:T(8,128)(2,1)S(1)}, u32[]{:S(2)}, u32[]{:S(2)}) collective-permute-start(bf16[8,7168]{1,0:T(8,128)(2,1)S(1)} %get-tuple-element.87), channel_id=1, source_target_pairs={{0,16},{16,32},{32,48},{48,64},{1,17},{17,33},{33,49},{49,65},{2,1... | collective-permute-start | bytes 344072 | tf_op jit(solution)/shard_map/ppermute | solution.py:21
  213.2 6.6 %collective-permute-start.4 = (bf16[8,7168]{1,0:T(8,128)(2,1)S(1)}, bf16[8,7168]{1,0:T(8,128)(2,1)S(1)}, u32[]{:S(2)}, u32[]{:S(2)}) collective-permute-start(bf16[8,7168]{1,0:T(8,128)(2,1)S(1)} %get-tuple-element.92), channel_id=1, source_target_pairs={{16,32},{32,48},{48,64},{64,80},{17,33},{33,49},{49,65},{65,81},{1... | collective-permute-start | bytes 344072 | tf_op jit(solution)/shard_map/ppermute | solution.py:21
  254.6 9.3 %collective-permute-start.5 = (bf16[8,7168]{1,0:T(8,128)(2,1)S(1)}, bf16[8,7168]{1,0:T(8,128)(2,1)S(1)}, u32[]{:S(2)}, u32[]{:S(2)}) collective-permute-start(bf16[8,7168]{1,0:T(8,128)(2,1)S(1)} %get-tuple-element.97), channel_id=1, source_target_pairs={{32,48},{48,64},{64,80},{80,96},{33,49},{49,65},{65,81},{81,97},{3... | collective-permute-start | bytes 344072 | tf_op jit(solution)/shard_map/ppermute | solution.py:21
  298.3 15.5 %collective-permute-start.6 = (bf16[8,7168]{1,0:T(8,128)(2,1)S(1)}, bf16[8,7168]{1,0:T(8,128)(2,1)S(1)}, u32[]{:S(2)}, u32[]{:S(2)}) collective-permute-start(bf16[8,7168]{1,0:T(8,128)(2,1)S(1)} %get-tuple-element.102), channel_id=1, source_target_pairs={{48,64},{64,80},{80,96},{96,112},{49,65},{65,81},{81,97},{97,113},... | collective-permute-start | bytes 344072 | tf_op jit(solution)/shard_map/ppermute | solution.py:21
  351.3 2.2 collective-permute-start.7
  395.3 0.7 collective-permute-start.8
  439.7 0.7 collective-permute-start.9

commit v4 on v3

--- a/solution.py
+++ b/solution.py
@@ -19,6 +19,20 @@
     last = lax.axis_size(axis) - 1
     route = [(s, s + 1) for s in range(last) if 0 <= tick - s < micro_count]
     return lax.ppermute(block, axis, route)
+
+
+PACE = 1
+
+
+def pacing(token, tick, micro_count):
+    last = lax.axis_size("section") - 1
+    done = tick + 1 - micro_count
+    sections = [0] if tick + 1 < micro_count else [done] if done % 2 == 0 and done < last else []
+    n = lax.axis_size("ep")
+    pairs = [(s * n + p, s * n + (p ^ 1)) for s in sections for p in range(n)]
+    for _ in range(PACE if pairs else 0):
+        token = lax.ppermute(token, ("section", "ep"), pairs)
+    return (token,) if pairs else ()
 
 
 def row_ids(rows, lanes, experts, capacity):
@@ -77,7 +91,7 @@
         for copy in copies:
             copy.wait()
     else:
-        rows_ref, gain_ref, router_ref, routes_ref, unpack_ref, came_ref, send_ref, mix_ref, input_ref = refs
+        rows_ref, gain_ref, router_ref, routes_ref, unpack_ref, came_ref, *_, send_ref, mix_ref, input_ref = refs
     micro_count, tokens, width = rows_ref.shape
     half = width // 2
     section = lax.axis_index("section")
@@ -156,8 +170,15 @@
         out_ref[:, cols] = out.astype(BF16)
 
 
-def expert_kernel(rows_ref, gate_ref, up_ref, down_ref, out_ref, act_ref):
-    product(rows_ref, gate_ref, up_ref, down_ref, out_ref, act_ref, lambda step: None)
+def busy(tick, micro_count):
+    m = tick - lax.axis_index("section")
+    return (m >= 0) & (m <= micro_count)
+
+
+def expert_kernel(tick, micro_count, rows_ref, gate_ref, up_ref, down_ref, out_ref, act_ref):
+    @pl.when(busy(tick, micro_count))
+    def _():
+        product(rows_ref, gate_ref, up_ref, down_ref, out_ref, act_ref, lambda step: None)
 
 
 def first_kernel(info_ref, rows_ref, gate_hbm, up_hbm, down_hbm,
@@ -279,9 +300,9 @@
             name="first",
         )(info, rows, *map(outside, weights))
 
-    def experts(rows, held):
+    def experts(tick, rows, held):
         return pl.pallas_call(
-            expert_kernel,
+            functools.partial(expert_kernel, tick, micro_count),
             out_shape=part_shape,
             in_specs=[VM] * 4,
             out_specs=VM,
@@ -311,11 +332,13 @@
             send, mix, layer_input, unpack, info = pre(tick)
             part, relative, *held = first(exchange(send), info)
         else:
-            send, mix, layer_input = pre(tick, unpack, incoming)
-            part = experts(exchange(send), held)
+            send, mix, layer_input = pre(tick, unpack, incoming, *pace)
+            part = experts(tick, exchange(send), held)
         next_rows, *kept = post(tick, layer_input, exchange(part), mix, *kept)
         if tick < last:
             incoming = live_hop(next_rows, "section", tick, micro_count)
+            incoming, token = lax.optimization_barrier((incoming, mix))
+            pace = pacing(token, tick, micro_count)
     return (kept[0][None], relative[:, :1])
 
 

time: 489 us -> 465 us (0.951)
  the two profiles are of different devices: /device:TPU:16 before, /device:TPU:24 now
where the time goes in v4:
time: 465 us; the launch traced here: 456 us
  blocking collectives  359 us (77%)
  Pallas kernels  38.5 us (8%)
  waiting for transfers between devices  38 us (8%)
  starting transfers between devices  18.2 us (4%)
    all_to_all x22, blocking collectives, exchange(): return lax.all_to_all(block, 'ep', split_axis=0, concat_axis=0, tiled=True)  359 us
    ppermute x10, waiting for transfers between devices, live_hop(): return lax.ppermute(block, axis, route)  35 us
    pallas_call x10, Pallas kernels, experts(): pl.pallas_call(functools.partial(expert_kernel, tick, micro_count), out_s...  16.5 us
    ppermute x10, starting transfers between devices, live_hop(): return lax.ppermute(block, axis, route)  11.7 us
    pallas_call x11, Pallas kernels, pre(): pl.pallas_call(functools.partial(pre_kernel, tick), out_shape=out_shape,...  10.4 us
  transfers between devices with their start and end apart: 17, of which 6 were waited for; matrix products, arithmetic and copies ran while one was open for 0% of the time, Pallas kernels for 0%

profile of v4, /device:TPU:24, one launch (start us, length us, event | category | flops | bytes accessed | tf_op | source)
XLA Modules:
  0.0 456.5 jit_solution(10725866211583854149)
XLA Ops:
  1.3 2.0 pre.11
  3.3 23.8 %all_to_all.242 = bf16[16,8,3712]{2,1,0:T(8,128)(2,1)S(1)} all-to-all(bf16[16,8,3712]{2,1,0:T(8,128)(2,1)S(1)} %bitcast.99), channel_id=1, replica_groups=mesh['section'=8,'ep'=16] {'ep'}, dimensions={0} | all-to-all | bytes 1900544 | tf_op jit(solution)/shard_map/all_to_all | solution.py:326
  27.1 8.2 %first.1 = (bf16[128,3584]{1,0:T(8,128)(2,1)S(1)}, f32[1,128]{1,0:T(1,128)}, bf16[7168,512]{1,0:T(8,128)(2,1)S(1)}, bf16[7168,512]{1,0:T(8,128)(2,1)S(1)}, bf16[512,7168]{1,0:T(8,128)(2,1)S(1)}) custom-call(f32[2,128]{1,0:T(2,128)S(1)} %get-tuple-element.82.info_ref, bf16[128,3712]{1,0:T(8,128)(2,1)S(1)} %bitcast.67, bf16[7168,512]{1,0:T(8,128)(2,1)} %bitcast.122, ...), custom_call_target="tpu_custom_call" | custom-call | tf_op jit(solution)/shard_map/first/pallas_call | solution.py:292
  35.3 18.2 %all_to_all.243 = bf16[16,8,3584]{2,1,0:T(8,128)(2,1)S(1)} all-to-all(bf16[16,8,3584]{2,1,0:T(8,128)(2,1)S(1)} %bitcast.100), channel_id=1, replica_groups=mesh['section'=8,'ep'=16] {'ep'}, dimensions={0} | all-to-all | bytes 1835008 | tf_op jit(solution)/shard_map/all_to_all | solution.py:326
  55.2 0.9 pre.12
  56.0 16.8 %all_to_all.244 = bf16[16,8,3584]{2,1,0:T(8,128)(2,1)S(1)} all-to-all(bf16[16,8,3584]{2,1,0:T(8,128)(2,1)S(1)} %bitcast.102), channel_id=1, replica_groups=mesh['section'=8,'ep'=16] {'ep'}, dimensions={0} | all-to-all | bytes 1835008 | tf_op jit(solution)/shard_map/all_to_all | solution.py:326
  72.8 15.7 %all_to_all.245 = bf16[16,8,3584]{2,1,0:T(8,128)(2,1)S(1)} all-to-all(bf16[16,8,3584]{2,1,0:T(8,128)(2,1)S(1)} %bitcast.82), channel_id=1, replica_groups=mesh['section'=8,'ep'=16] {'ep'}, dimensions={0} | all-to-all | bytes 1835008 | tf_op jit(solution)/shard_map/all_to_all | solution.py:326
  90.1 0.9 pre.13
  91.0 15.0 %all_to_all.246 = bf16[16,8,3584]{2,1,0:T(8,128)(2,1)S(1)} all-to-all(bf16[16,8,3584]{2,1,0:T(8,128)(2,1)S(1)} %bitcast.103), channel_id=1, replica_groups=mesh['section'=8,'ep'=16] {'ep'}, dimensions={0} | all-to-all | bytes 1835008 | tf_op jit(solution)/shard_map/all_to_all | solution.py:326
  106.5 15.1 %all_to_all.247 = bf16[16,8,3584]{2,1,0:T(8,128)(2,1)S(1)} all-to-all(bf16[16,8,3584]{2,1,0:T(8,128)(2,1)S(1)} %bitcast.84), channel_id=1, replica_groups=mesh['section'=8,'ep'=16] {'ep'}, dimensions={0} | all-to-all | bytes 1835008 | tf_op jit(solution)/shard_map/all_to_all | solution.py:326
  123.2 0.9 pre.14
  124.1 15.4 %all_to_all.248 = bf16[16,8,3584]{2,1,0:T(8,128)(2,1)S(1)} all-to-all(bf16[16,8,3584]{2,1,0:T(8,128)(2,1)S(1)} %bitcast.104), channel_id=1, replica_groups=mesh['section'=8,'ep'=16] {'ep'}, dimensions={0} | all-to-all | bytes 1835008 | tf_op jit(solution)/shard_map/all_to_all | solution.py:326
  139.5 14.9 %all_to_all.249 = bf16[16,8,3584]{2,1,0:T(8,128)(2,1)S(1)} all-to-all(bf16[16,8,3584]{2,1,0:T(8,128)(2,1)S(1)} %bitcast.86), channel_id=1, replica_groups=mesh['section'=8,'ep'=16] {'ep'}, dimensions={0} | all-to-all | bytes 1835008 | tf_op jit(solution)/shard_map/all_to_all | solution.py:326
  156.0 0.8 pre.15
  156.8 16.2 %all_to_all.250 = bf16[16,8,3584]{2,1,0:T(8,128)(2,1)S(1)} all-to-all(bf16[16,8,3584]{2,1,0:T(8,128)(2,1)S(1)} %bitcast.105), channel_id=1, replica_groups=mesh['section'=8,'ep'=16] {'ep'}, dimensions={0} | all-to-all | bytes 1835008 | tf_op jit(solution)/shard_map/all_to_all | solution.py:326
  173.1 16.5 %all_to_all.251 = bf16[16,8,3584]{2,1,0:T(8,128)(2,1)S(1)} all-to-all(bf16[16,8,3584]{2,1,0:T(8,128)(2,1)S(1)} %bitcast.88), channel_id=1, replica_groups=mesh['section'=8,'ep'=16] {'ep'}, dimensions={0} | all-to-all | bytes 1835008 | tf_op jit(solution)/shard_map/all_to_all | solution.py:326
  191.3 19.9 %all_to_all.252 = bf16[16,8,3584]{2,1,0:T(8,128)(2,1)S(1)} all-to-all(bf16[16,8,3584]{2,1,0:T(8,128)(2,1)S(1)} %bitcast.108), channel_id=1, replica_groups=mesh['section'=8,'ep'=16] {'ep'}, dimensions={0} | all-to-all | bytes 1835008 | tf_op jit(solution)/shard_map/all_to_all | solution.py:326
  211.1 19.1 %all_to_all.253 = bf16[16,8,3584]{2,1,0:T(8,128)(2,1)S(1)} all-to-all(bf16[16,8,3584]{2,1,0:T(8,128)(2,1)S(1)} %bitcast.90), channel_id=1, replica_groups=mesh['section'=8,'ep'=16] {'ep'}, dimensions={0} | all-to-all | bytes 1835008 | tf_op jit(solution)/shard_map/all_to_all | solution.py:326
  230.5 1.3 collective-permute-start.9
  231.8 17.8 %collective-permute-done.9.refs_5_ = bf16[8,7168]{1,0:T(8,128)(2,1)S(1)} collective-permute-done((bf16[8,7168]{1,0:T(8,128)(2,1)S(1)}, bf16[8,7168]{1,0:T(8,128)(2,1)S(1)}, u32[]{:S(2)}, u32[]{:S(2)}) %collective-permute-start.9) | collective-permute-done | bytes 114720 | tf_op jit(solution)/shard_map/ppermute | solution.py:21
  250.3 0.8 pre.17
  251.1 15.2 %all_to_all.254 = bf16[16,8,3584]{2,1,0:T(8,128)(2,1)S(1)} all-to-all(bf16[16,8,3584]{2,1,0:T(8,128)(2,1)S(1)} %bitcast.106), channel_id=1, replica_groups=mesh['section'=8,'ep'=16] {'ep'}, dimensions={0} | all-to-all | bytes 1835008 | tf_op jit(solution)/shard_map/all_to_all | solution.py:326
  266.3 3.2 experts.15
  269.5 15.1 %all_to_all.255 = bf16[16,8,3584]{2,1,0:T(8,128)(2,1)S(1)} all-to-all(bf16[16,8,3584]{2,1,0:T(8,128)(2,1)S(1)} %bitcast.92), channel_id=1, replica_groups=mesh['section'=8,'ep'=16] {'ep'}, dimensions={0} | all-to-all | bytes 1835008 | tf_op jit(solution)/shard_map/all_to_all | solution.py:326
  284.9 1.9 collective-permute-start.11
  286.8 5.2 %collective-permute-done.11.refs_5_ = bf16[8,7168]{1,0:T(8,128)(2,1)S(1)} collective-permute-done((bf16[8,7168]{1,0:T(8,128)(2,1)S(1)}, bf16[8,7168]{1,0:T(8,128)(2,1)S(1)}, u32[]{:S(2)}, u32[]{:S(2)}) %collective-permute-start.11) | collective-permute-done | bytes 114720 | tf_op jit(solution)/shard_map/ppermute | solution.py:21
  292.8 15.2 %all_to_all.256 = bf16[16,8,3584]{2,1,0:T(8,128)(2,1)S(1)} all-to-all(bf16[16,8,3584]{2,1,0:T(8,128)(2,1)S(1)} %bitcast.109), channel_id=1, replica_groups=mesh['section'=8,'ep'=16] {'ep'}, dimensions={0} | all-to-all | bytes 1835008 | tf_op jit(solution)/shard_map/all_to_all | solution.py:326
  308.0 3.4 experts.16
  311.3 15.1 %all_to_all.257 = bf16[16,8,3584]{2,1,0:T(8,128)(2,1)S(1)} all-to-all(bf16[16,8,3584]{2,1,0:T(8,128)(2,1)S(1)} %bitcast.94), channel_id=1, replica_groups=mesh['section'=8,'ep'=16] {'ep'}, dimensions={0} | all-to-all | bytes 1835008 | tf_op jit(solution)/shard_map/all_to_all | solution.py:326
  326.7 1.9 collective-permute-start.12
  328.7 6.9 %collective-permute-done.12.refs_5_ = bf16[8,7168]{1,0:T(8,128)(2,1)S(1)} collective-permute-done((bf16[8,7168]{1,0:T(8,128)(2,1)S(1)}, bf16[8,7168]{1,0:T(8,128)(2,1)S(1)}, u32[]{:S(2)}, u32[]{:S(2)}) %collective-permute-start.12) | collective-permute-done | bytes 114720 | tf_op jit(solution)/shard_map/ppermute | solution.py:21
  336.2 0.8 pre.19
  337.0 14.9 %all_to_all.258 = bf16[16,8,3584]{2,1,0:T(8,128)(2,1)S(1)} all-to-all(bf16[16,8,3584]{2,1,0:T(8,128)(2,1)S(1)} %bitcast.107), channel_id=1, replica_groups=mesh['section'=8,'ep'=16] {'ep'}, dimensions={0} | all-to-all | bytes 1835008 | tf_op jit(solution)/shard_map/all_to_all | solution.py:326
  351.9 3.2 experts.17
  355.1 15.1 %all_to_all.259 = bf16[16,8,3584]{2,1,0:T(8,128)(2,1)S(1)} all-to-all(bf16[16,8,3584]{2,1,0:T(8,128)(2,1)S(1)} %bitcast.96), channel_id=1, replica_groups=mesh['section'=8,'ep'=16] {'ep'}, dimensions={0} | all-to-all | bytes 1835008 | tf_op jit(solution)/shard_map/all_to_all | solution.py:326
  370.5 1.9 collective-permute-start.14
  372.4 4.2 collective-permute-done.14.refs_5_
  377.4 16.0 %all_to_all.260 = bf16[16,8,3584]{2,1,0:T(8,128)(2,1)S(1)} all-to-all(bf16[16,8,3584]{2,1,0:T(8,128)(2,1)S(1)} %bitcast.110), channel_id=1, replica_groups=mesh['section'=8,'ep'=16] {'ep'}, dimensions={0} | all-to-all | bytes 1835008 | tf_op jit(solution)/shard_map/all_to_all | solution.py:326
  393.4 3.2 experts.18
  396.6 15.5 %all_to_all.261 = bf16[16,8,3584]{2,1,0:T(8,128)(2,1)S(1)} all-to-all(bf16[16,8,3584]{2,1,0:T(8,128)(2,1)S(1)} %bitcast.98), channel_id=1, replica_groups=mesh['section'=8,'ep'=16] {'ep'}, dimensions={0} | all-to-all | bytes 1835008 | tf_op jit(solution)/shard_map/all_to_all | solution.py:326
  412.4 1.3 collective-permute-start.15
  413.7 0.9 collective-permute-done.15.refs_5_
  414.6 2.5 collective-permute-start.16
  417.1 3.0 collective-permute-done.16.refs_6_
  421.0 15.1 %all_to_all.262 = bf16[16,8,3584]{2,1,0:T(8,128)(2,1)S(1)} all-to-all(bf16[16,8,3584]{2,1,0:T(8,128)(2,1)S(1)} %bitcast.101), channel_id=1, replica_groups=mesh['section'=8,'ep'=16] {'ep'}, dimensions={0} | all-to-all | bytes 1835008 | tf_op jit(solution)/shard_map/all_to_all | solution.py:326
  436.0 3.2 experts.19
  439.2 15.1 %all_to_all.263 = bf16[16,8,3584]{2,1,0:T(8,128)(2,1)S(1)} all-to-all(bf16[16,8,3584]{2,1,0:T(8,128)(2,1)S(1)} %bitcast.80), channel_id=1, replica_groups=mesh['section'=8,'ep'=16] {'ep'}, dimensions={0} | all-to-all | bytes 1835008 | tf_op jit(solution)/shard_map/all_to_all | solution.py:326
  454.4 0.9 post.21
  (50 shorter events, 14.3 us)
Async XLA Ops:
  27.1 28.0 %copy-start = (bf16[4,8,7168]{2,1,0:T(8,128)(2,1)S(1)}, bf16[4,8,7168]{2,1,0:T(8,128)(2,1)}, u32[]{:S(2)}) copy-start(bf16[4,8,7168]{2,1,0:T(8,128)(2,1)} %refs_0_.20) | copy-start | bytes 1376260
  27.1 28.0 %copy-start.1 = (bf16[1,7168,8]{1,2,0:T(8,128)(2,1)S(1)}, bf16[1,7168,8]{1,2,0:T(8,128)(2,1)}, u32[]{:S(2)}) copy-start(bf16[1,7168,8]{1,2,0:T(8,128)(2,1)} %param.12) | copy-start | bytes 344068
  27.1 28.0 %copy-start.2 = (f32[1,7168]{1,0:T(1,128)S(1)}, f32[1,7168]{1,0:T(1,128)}, u32[]{:S(2)}) copy-start(f32[1,7168]{1,0:T(1,128)} %refs_1_.21) | copy-start | bytes 86020
  27.1 28.0 %copy-start.3 = (s32[1,4,8,2]{2,3,1,0:T(2,128)S(1)}, s32[1,4,8,2]{2,3,1,0:T(2,128)}, u32[]{:S(2)}) copy-start(s32[1,4,8,2]{2,3,1,0:T(2,128)} %param.9) | copy-start | bytes 772
  53.7 0.7 collective-permute-start
  54.4 0.7 collective-permute-start.1
  88.8 0.7 collective-permute-start.2
  89.5 0.7 collective-permute-start.3
  121.8 0.7 collective-permute-start.4
  122.5 0.7 collective-permute-start.5
  154.6 0.7 collective-permute-start.6
  155.3 0.7 collective-permute-start.7
  189.8 0.7 collective-permute-start.8
  230.5 19.1 %collective-permute-start.9 = (bf16[8,7168]{1,0:T(8,128)(2,1)S(1)}, bf16[8,7168]{1,0:T(8,128)(2,1)S(1)}, u32[]{:S(2)}, u32[]{:S(2)}) collective-permute-start(bf16[8,7168]{1,0:T(8,128)(2,1)S(1)} %get-tuple-element.123), channel_id=1, source_target_pairs={{32,48},{48,64},{64,80},{80,96},{33,49},{49,65},{65,81},{81,97},{3... | collective-permute-start | bytes 344072 | tf_op jit(solution)/shard_map/ppermute | solution.py:21
  249.6 0.7 collective-permute-start.10
  284.9 7.1 %collective-permute-start.11 = (bf16[8,7168]{1,0:T(8,128)(2,1)S(1)}, bf16[8,7168]{1,0:T(8,128)(2,1)S(1)}, u32[]{:S(2)}, u32[]{:S(2)}) collective-permute-start(bf16[8,7168]{1,0:T(8,128)(2,1)S(1)} %get-tuple-element.130), channel_id=1, source_target_pairs={{48,64},{64,80},{80,96},{96,112},{49,65},{65,81},{81,97},{97,113},... | collective-permute-start | bytes 344072 | tf_op jit(solution)/shard_map/ppermute | solution.py:21
  326.7 8.8 %collective-permute-start.12 = (bf16[8,7168]{1,0:T(8,128)(2,1)S(1)}, bf16[8,7168]{1,0:T(8,128)(2,1)S(1)}, u32[]{:S(2)}, u32[]{:S(2)}) collective-permute-start(bf16[8,7168]{1,0:T(8,128)(2,1)S(1)} %get-tuple-element.136), channel_id=1, source_target_pairs={{64,80},{80,96},{96,112},{65,81},{81,97},{97,113},{66,82},{82,98},... | collective-permute-start | bytes 344072 | tf_op jit(solution)/shard_map/ppermute | solution.py:21
  335.5 0.7 collective-permute-start.13
  370.5 6.1 %collective-permute-start.14 = (bf16[8,7168]{1,0:T(8,128)(2,1)S(1)}, bf16[8,7168]{1,0:T(8,128)(2,1)S(1)}, u32[]{:S(2)}, u32[]{:S(2)}) collective-permute-start(bf16[8,7168]{1,0:T(8,128)(2,1)S(1)} %get-tuple-element.143), channel_id=1, source_target_pairs={{80,96},{96,112},{81,97},{97,113},{82,98},{98,114},{83,99},{99,115... | collective-permute-start | bytes 344072 | tf_op jit(solution)/shard_map/ppermute | solution.py:21
  412.4 2.2 collective-permute-start.15
  414.6 5.5 %collective-permute-start.16 = (bf16[32,128]{1,0:T(8,128)(2,1)S(1)}, bf16[32,128]{1,0:T(8,128)(2,1)S(1)}, u32[]{:S(2)}, u32[]{:S(2)}) collective-permute-start(bf16[32,128]{1,0:T(8,128)(2,1)S(1)} %get-tuple-element.151.mix_ref), channel_id=1, source_target_pairs={{96,97},{97,96},{98,99},{99,98},{100,101},{101,100},{102,103},{103... | collective-permute-start | bytes 24584 | tf_op jit(solution)/shard_map/ppermute | solution.py:34

commit v5 on v4

--- a/solution.py
+++ b/solution.py
@@ -33,6 +33,12 @@
     for _ in range(PACE if pairs else 0):
         token = lax.ppermute(token, ("section", "ep"), pairs)
     return (token,) if pairs else ()
+
+
+def busy(tick, micro_count):
+    section = lax.axis_index("section")
+    m = tick - section
+    return (m >= 0) & (m < micro_count + 1 - section % 2)
 
 
 def row_ids(rows, lanes, experts, capacity):
@@ -136,6 +142,16 @@
     mix_ref[mix.shape[0] :] = (mix - high.astype(F32)).astype(BF16)
 
 
+def pre_or_idle(tick, micro_count, *refs):
+    if tick == 0:
+        pre_kernel(tick, *refs)
+    else:
+
+        @pl.when(busy(tick, micro_count))
+        def _():
+            pre_kernel(tick, *refs)
+
+
 def product(rows_ref, gate_ref, up_ref, down_ref, out_ref, act_ref, arrived):
     count, half = out_ref.shape
     hidden = gate_ref.shape[1]
@@ -168,11 +184,6 @@
             second, down_ref[:, rest], preferred_element_type=F32
         )
         out_ref[:, cols] = out.astype(BF16)
-
-
-def busy(tick, micro_count):
-    m = tick - lax.axis_index("section")
-    return (m >= 0) & (m <= micro_count)
 
 
 def expert_kernel(tick, micro_count, rows_ref, gate_ref, up_ref, down_ref, out_ref, act_ref):
@@ -214,7 +225,16 @@
         for copy in copies[step]:
             copy.wait()
 
-    product(rows_ref, gate_ref, up_ref, down_ref, out_ref, act_ref, arrived)
+    live = lax.axis_index("section") == 0
+
+    @pl.when(live)
+    def _():
+        product(rows_ref, gate_ref, up_ref, down_ref, out_ref, act_ref, arrived)
+
+    @pl.when(jnp.logical_not(live))
+    def _():
+        for step in range(len(copies)):
+            arrived(step)
 
 
 def post_kernel(tick, x_ref, back_ref, mix_ref, *rest):
@@ -275,7 +295,7 @@
             specs = [VM] * len(values)
             scratch = []
         return pl.pallas_call(
-            functools.partial(pre_kernel, tick),
+            functools.partial(pre_or_idle, tick, micro_count),
             out_shape=out_shape,
             in_specs=specs,
             out_specs=[VM] * len(out_shape),

time: 465 us -> 464 us (level)
  no operation moved by 1% of the time
where the time goes in v5:
time: 464 us; the launch traced here: 456 us
  blocking collectives  361 us (78%)
  waiting for transfers between devices  40.4 us (9%)
  Pallas kernels  34.2 us (7%)
  starting transfers between devices  18.2 us (4%)
    all_to_all x22, blocking collectives, exchange(): return lax.all_to_all(block, 'ep', split_axis=0, concat_axis=0, tiled=True)  361 us
    ppermute x10, waiting for transfers between devices, live_hop(): return lax.ppermute(block, axis, route)  37.3 us
    pallas_call x10, Pallas kernels, experts(): pl.pallas_call(functools.partial(expert_kernel, tick, micro_count), out_s...  16.5 us
    ppermute x10, starting transfers between devices, live_hop(): return lax.ppermute(block, axis, route)  11.7 us
  transfers between devices with their start and end apart: 17, of which 6 were waited for; matrix products, arithmetic and copies ran while one was open for 0% of the time, Pallas kernels for 0%

profile of v5, /device:TPU:24, one launch (start us, length us, event | category | flops | bytes accessed | tf_op | source)
XLA Modules:
  0.0 456.2 jit_solution(10509685885848951578)
XLA Ops:
  1.3 2.0 pre.11
  3.3 23.8 %all_to_all.242 = bf16[16,8,3712]{2,1,0:T(8,128)(2,1)S(1)} all-to-all(bf16[16,8,3712]{2,1,0:T(8,128)(2,1)S(1)} %bitcast.99), channel_id=1, replica_groups=mesh['section'=8,'ep'=16] {'ep'}, dimensions={0} | all-to-all | bytes 1900544 | tf_op jit(solution)/shard_map/all_to_all | solution.py:346
  27.1 8.0 %first.1 = (bf16[128,3584]{1,0:T(8,128)(2,1)S(1)}, f32[1,128]{1,0:T(1,128)}, bf16[7168,512]{1,0:T(8,128)(2,1)S(1)}, bf16[7168,512]{1,0:T(8,128)(2,1)S(1)}, bf16[512,7168]{1,0:T(8,128)(2,1)S(1)}) custom-call(f32[2,128]{1,0:T(2,128)S(1)} %get-tuple-element.82.info_ref, bf16[128,3712]{1,0:T(8,128)(2,1)S(1)} %bitcast.67, bf16[7168,512]{1,0:T(8,128)(2,1)} %bitcast.122, ...), custom_call_target="tpu_custom_call" | custom-call | tf_op jit(solution)/shard_map/first/pallas_call | solution.py:312
  35.1 18.1 %all_to_all.243 = bf16[16,8,3584]{2,1,0:T(8,128)(2,1)S(1)} all-to-all(bf16[16,8,3584]{2,1,0:T(8,128)(2,1)S(1)} %bitcast.100), channel_id=1, replica_groups=mesh['section'=8,'ep'=16] {'ep'}, dimensions={0} | all-to-all | bytes 1835008 | tf_op jit(solution)/shard_map/all_to_all | solution.py:346
  54.9 16.8 %all_to_all.244 = bf16[16,8,3584]{2,1,0:T(8,128)(2,1)S(1)} all-to-all(bf16[16,8,3584]{2,1,0:T(8,128)(2,1)S(1)} %bitcast.102), channel_id=1, replica_groups=mesh['section'=8,'ep'=16] {'ep'}, dimensions={0} | all-to-all | bytes 1835008 | tf_op jit(solution)/shard_map/all_to_all | solution.py:346
  71.7 15.7 %all_to_all.245 = bf16[16,8,3584]{2,1,0:T(8,128)(2,1)S(1)} all-to-all(bf16[16,8,3584]{2,1,0:T(8,128)(2,1)S(1)} %bitcast.82), channel_id=1, replica_groups=mesh['section'=8,'ep'=16] {'ep'}, dimensions={0} | all-to-all | bytes 1835008 | tf_op jit(solution)/shard_map/all_to_all | solution.py:346
  89.0 15.0 %all_to_all.246 = bf16[16,8,3584]{2,1,0:T(8,128)(2,1)S(1)} all-to-all(bf16[16,8,3584]{2,1,0:T(8,128)(2,1)S(1)} %bitcast.103), channel_id=1, replica_groups=mesh['section'=8,'ep'=16] {'ep'}, dimensions={0} | all-to-all | bytes 1835008 | tf_op jit(solution)/shard_map/all_to_all | solution.py:346
  104.5 15.1 %all_to_all.247 = bf16[16,8,3584]{2,1,0:T(8,128)(2,1)S(1)} all-to-all(bf16[16,8,3584]{2,1,0:T(8,128)(2,1)S(1)} %bitcast.84), channel_id=1, replica_groups=mesh['section'=8,'ep'=16] {'ep'}, dimensions={0} | all-to-all | bytes 1835008 | tf_op jit(solution)/shard_map/all_to_all | solution.py:346
  121.3 15.4 %all_to_all.248 = bf16[16,8,3584]{2,1,0:T(8,128)(2,1)S(1)} all-to-all(bf16[16,8,3584]{2,1,0:T(8,128)(2,1)S(1)} %bitcast.104), channel_id=1, replica_groups=mesh['section'=8,'ep'=16] {'ep'}, dimensions={0} | all-to-all | bytes 1835008 | tf_op jit(solution)/shard_map/all_to_all | solution.py:346
  136.6 15.0 %all_to_all.249 = bf16[16,8,3584]{2,1,0:T(8,128)(2,1)S(1)} all-to-all(bf16[16,8,3584]{2,1,0:T(8,128)(2,1)S(1)} %bitcast.86), channel_id=1, replica_groups=mesh['section'=8,'ep'=16] {'ep'}, dimensions={0} | all-to-all | bytes 1835008 | tf_op jit(solution)/shard_map/all_to_all | solution.py:346
  153.3 16.1 %all_to_all.250 = bf16[16,8,3584]{2,1,0:T(8,128)(2,1)S(1)} all-to-all(bf16[16,8,3584]{2,1,0:T(8,128)(2,1)S(1)} %bitcast.105), channel_id=1, replica_groups=mesh['section'=8,'ep'=16] {'ep'}, dimensions={0} | all-to-all | bytes 1835008 | tf_op jit(solution)/shard_map/all_to_all | solution.py:346
  169.4 17.0 %all_to_all.251 = bf16[16,8,3584]{2,1,0:T(8,128)(2,1)S(1)} all-to-all(bf16[16,8,3584]{2,1,0:T(8,128)(2,1)S(1)} %bitcast.88), channel_id=1, replica_groups=mesh['section'=8,'ep'=16] {'ep'}, dimensions={0} | all-to-all | bytes 1835008 | tf_op jit(solution)/shard_map/all_to_all | solution.py:346
  187.4 20.1 %all_to_all.252 = bf16[16,8,3584]{2,1,0:T(8,128)(2,1)S(1)} all-to-all(bf16[16,8,3584]{2,1,0:T(8,128)(2,1)S(1)} %bitcast.108), channel_id=1, replica_groups=mesh['section'=8,'ep'=16] {'ep'}, dimensions={0} | all-to-all | bytes 1835008 | tf_op jit(solution)/shard_map/all_to_all | solution.py:346
  207.5 20.1 %all_to_all.253 = bf16[16,8,3584]{2,1,0:T(8,128)(2,1)S(1)} all-to-all(bf16[16,8,3584]{2,1,0:T(8,128)(2,1)S(1)} %bitcast.90), channel_id=1, replica_groups=mesh['section'=8,'ep'=16] {'ep'}, dimensions={0} | all-to-all | bytes 1835008 | tf_op jit(solution)/shard_map/all_to_all | solution.py:346
  227.9 1.3 collective-permute-start.9
  229.2 20.1 %collective-permute-done.9.refs_5_ = bf16[8,7168]{1,0:T(8,128)(2,1)S(1)} collective-permute-done((bf16[8,7168]{1,0:T(8,128)(2,1)S(1)}, bf16[8,7168]{1,0:T(8,128)(2,1)S(1)}, u32[]{:S(2)}, u32[]{:S(2)}) %collective-permute-start.9) | collective-permute-done | bytes 114720 | tf_op jit(solution)/shard_map/ppermute | solution.py:21
  249.9 0.8 pre.17
  250.8 15.2 %all_to_all.254 = bf16[16,8,3584]{2,1,0:T(8,128)(2,1)S(1)} all-to-all(bf16[16,8,3584]{2,1,0:T(8,128)(2,1)S(1)} %bitcast.106), channel_id=1, replica_groups=mesh['section'=8,'ep'=16] {'ep'}, dimensions={0} | all-to-all | bytes 1835008 | tf_op jit(solution)/shard_map/all_to_all | solution.py:346
  266.0 3.2 experts.15
  269.2 15.1 %all_to_all.255 = bf16[16,8,3584]{2,1,0:T(8,128)(2,1)S(1)} all-to-all(bf16[16,8,3584]{2,1,0:T(8,128)(2,1)S(1)} %bitcast.92), channel_id=1, replica_groups=mesh['section'=8,'ep'=16] {'ep'}, dimensions={0} | all-to-all | bytes 1835008 | tf_op jit(solution)/shard_map/all_to_all | solution.py:346
  284.5 1.9 collective-permute-start.11
  286.5 5.1 %collective-permute-done.11.refs_5_ = bf16[8,7168]{1,0:T(8,128)(2,1)S(1)} collective-permute-done((bf16[8,7168]{1,0:T(8,128)(2,1)S(1)}, bf16[8,7168]{1,0:T(8,128)(2,1)S(1)}, u32[]{:S(2)}, u32[]{:S(2)}) %collective-permute-start.11) | collective-permute-done | bytes 114720 | tf_op jit(solution)/shard_map/ppermute | solution.py:21
  291.6 0.8 pre.18
  292.4 15.2 %all_to_all.256 = bf16[16,8,3584]{2,1,0:T(8,128)(2,1)S(1)} all-to-all(bf16[16,8,3584]{2,1,0:T(8,128)(2,1)S(1)} %bitcast.109), channel_id=1, replica_groups=mesh['section'=8,'ep'=16] {'ep'}, dimensions={0} | all-to-all | bytes 1835008 | tf_op jit(solution)/shard_map/all_to_all | solution.py:346
  307.6 3.4 experts.16
  311.0 15.1 %all_to_all.257 = bf16[16,8,3584]{2,1,0:T(8,128)(2,1)S(1)} all-to-all(bf16[16,8,3584]{2,1,0:T(8,128)(2,1)S(1)} %bitcast.94), channel_id=1, replica_groups=mesh['section'=8,'ep'=16] {'ep'}, dimensions={0} | all-to-all | bytes 1835008 | tf_op jit(solution)/shard_map/all_to_all | solution.py:346
  326.3 1.9 collective-permute-start.12
  328.2 7.0 %collective-permute-done.12.refs_5_ = bf16[8,7168]{1,0:T(8,128)(2,1)S(1)} collective-permute-done((bf16[8,7168]{1,0:T(8,128)(2,1)S(1)}, bf16[8,7168]{1,0:T(8,128)(2,1)S(1)}, u32[]{:S(2)}, u32[]{:S(2)}) %collective-permute-start.12) | collective-permute-done | bytes 114720 | tf_op jit(solution)/shard_map/ppermute | solution.py:21
  335.9 0.9 pre.19
  336.7 14.9 %all_to_all.258 = bf16[16,8,3584]{2,1,0:T(8,128)(2,1)S(1)} all-to-all(bf16[16,8,3584]{2,1,0:T(8,128)(2,1)S(1)} %bitcast.107), channel_id=1, replica_groups=mesh['section'=8,'ep'=16] {'ep'}, dimensions={0} | all-to-all | bytes 1835008 | tf_op jit(solution)/shard_map/all_to_all | solution.py:346
  351.6 3.2 experts.17
  354.8 15.1 %all_to_all.259 = bf16[16,8,3584]{2,1,0:T(8,128)(2,1)S(1)} all-to-all(bf16[16,8,3584]{2,1,0:T(8,128)(2,1)S(1)} %bitcast.96), channel_id=1, replica_groups=mesh['section'=8,'ep'=16] {'ep'}, dimensions={0} | all-to-all | bytes 1835008 | tf_op jit(solution)/shard_map/all_to_all | solution.py:346
  370.2 1.9 collective-permute-start.14
  372.1 4.2 collective-permute-done.14.refs_5_
  376.3 0.8 pre.20
  377.1 16.0 %all_to_all.260 = bf16[16,8,3584]{2,1,0:T(8,128)(2,1)S(1)} all-to-all(bf16[16,8,3584]{2,1,0:T(8,128)(2,1)S(1)} %bitcast.110), channel_id=1, replica_groups=mesh['section'=8,'ep'=16] {'ep'}, dimensions={0} | all-to-all | bytes 1835008 | tf_op jit(solution)/shard_map/all_to_all | solution.py:346
  393.1 3.2 experts.18
  396.3 15.5 %all_to_all.261 = bf16[16,8,3584]{2,1,0:T(8,128)(2,1)S(1)} all-to-all(bf16[16,8,3584]{2,1,0:T(8,128)(2,1)S(1)} %bitcast.98), channel_id=1, replica_groups=mesh['section'=8,'ep'=16] {'ep'}, dimensions={0} | all-to-all | bytes 1835008 | tf_op jit(solution)/shard_map/all_to_all | solution.py:346
  412.1 1.3 collective-permute-start.15
  413.4 0.9 collective-permute-done.15.refs_5_
  414.4 2.5 collective-permute-start.16
  416.9 3.0 collective-permute-done.16.refs_6_
  419.9 0.8 pre.21
  420.7 15.1 %all_to_all.262 = bf16[16,8,3584]{2,1,0:T(8,128)(2,1)S(1)} all-to-all(bf16[16,8,3584]{2,1,0:T(8,128)(2,1)S(1)} %bitcast.101), channel_id=1, replica_groups=mesh['section'=8,'ep'=16] {'ep'}, dimensions={0} | all-to-all | bytes 1835008 | tf_op jit(solution)/shard_map/all_to_all | solution.py:346
  435.8 3.2 experts.19
  439.0 15.2 %all_to_all.263 = bf16[16,8,3584]{2,1,0:T(8,128)(2,1)S(1)} all-to-all(bf16[16,8,3584]{2,1,0:T(8,128)(2,1)S(1)} %bitcast.80), channel_id=1, replica_groups=mesh['section'=8,'ep'=16] {'ep'}, dimensions={0} | all-to-all | bytes 1835008 | tf_op jit(solution)/shard_map/all_to_all | solution.py:346
  454.1 0.9 post.21
  455.0 0.8 copy.33
  (50 shorter events, 10.4 us)
Async XLA Ops:
  27.1 27.7 %copy-start = (bf16[4,8,7168]{2,1,0:T(8,128)(2,1)S(1)}, bf16[4,8,7168]{2,1,0:T(8,128)(2,1)}, u32[]{:S(2)}) copy-start(bf16[4,8,7168]{2,1,0:T(8,128)(2,1)} %refs_0_.20) | copy-start | bytes 1376260
  27.1 27.7 %copy-start.1 = (bf16[1,7168,8]{1,2,0:T(8,128)(2,1)S(1)}, bf16[1,7168,8]{1,2,0:T(8,128)(2,1)}, u32[]{:S(2)}) copy-start(bf16[1,7168,8]{1,2,0:T(8,128)(2,1)} %param.12) | copy-start | bytes 344068
  27.1 27.8 %copy-start.2 = (f32[1,7168]{1,0:T(1,128)S(1)}, f32[1,7168]{1,0:T(1,128)}, u32[]{:S(2)}) copy-start(f32[1,7168]{1,0:T(1,128)} %refs_1_.21) | copy-start | bytes 86020
  27.1 27.8 %copy-start.3 = (s32[1,4,8,2]{2,3,1,0:T(2,128)S(1)}, s32[1,4,8,2]{2,3,1,0:T(2,128)}, u32[]{:S(2)}) copy-start(s32[1,4,8,2]{2,3,1,0:T(2,128)} %param.9) | copy-start | bytes 772
  53.5 0.7 collective-permute-start
  54.2 0.7 collective-permute-start.1
  87.6 0.7 collective-permute-start.2
  88.3 0.7 collective-permute-start.3
  119.9 0.7 collective-permute-start.4
  120.5 0.7 collective-permute-start.5
  151.9 0.7 collective-permute-start.6
  152.6 0.7 collective-permute-start.7
  186.7 0.7 collective-permute-start.8
  227.9 21.4 %collective-permute-start.9 = (bf16[8,7168]{1,0:T(8,128)(2,1)S(1)}, bf16[8,7168]{1,0:T(8,128)(2,1)S(1)}, u32[]{:S(2)}, u32[]{:S(2)}) collective-permute-start(bf16[8,7168]{1,0:T(8,128)(2,1)S(1)} %get-tuple-element.123), channel_id=1, source_target_pairs={{32,48},{48,64},{64,80},{80,96},{33,49},{49,65},{65,81},{81,97},{3... | collective-permute-start | bytes 344072 | tf_op jit(solution)/shard_map/ppermute | solution.py:21
  249.3 0.7 collective-permute-start.10
  284.5 7.1 %collective-permute-start.11 = (bf16[8,7168]{1,0:T(8,128)(2,1)S(1)}, bf16[8,7168]{1,0:T(8,128)(2,1)S(1)}, u32[]{:S(2)}, u32[]{:S(2)}) collective-permute-start(bf16[8,7168]{1,0:T(8,128)(2,1)S(1)} %get-tuple-element.130), channel_id=1, source_target_pairs={{48,64},{64,80},{80,96},{96,112},{49,65},{65,81},{81,97},{97,113},... | collective-permute-start | bytes 344072 | tf_op jit(solution)/shard_map/ppermute | solution.py:21
  326.3 8.9 %collective-permute-start.12 = (bf16[8,7168]{1,0:T(8,128)(2,1)S(1)}, bf16[8,7168]{1,0:T(8,128)(2,1)S(1)}, u32[]{:S(2)}, u32[]{:S(2)}) collective-permute-start(bf16[8,7168]{1,0:T(8,128)(2,1)S(1)} %get-tuple-element.136), channel_id=1, source_target_pairs={{64,80},{80,96},{96,112},{65,81},{81,97},{97,113},{66,82},{82,98},... | collective-permute-start | bytes 344072 | tf_op jit(solution)/shard_map/ppermute | solution.py:21
  335.2 0.7 collective-permute-start.13
  370.2 6.1 %collective-permute-start.14 = (bf16[8,7168]{1,0:T(8,128)(2,1)S(1)}, bf16[8,7168]{1,0:T(8,128)(2,1)S(1)}, u32[]{:S(2)}, u32[]{:S(2)}) collective-permute-start(bf16[8,7168]{1,0:T(8,128)(2,1)S(1)} %get-tuple-element.143), channel_id=1, source_target_pairs={{80,96},{96,112},{81,97},{97,113},{82,98},{98,114},{83,99},{99,115... | collective-permute-start | bytes 344072 | tf_op jit(solution)/shard_map/ppermute | solution.py:21
  412.1 2.2 collective-permute-start.15
  414.4 5.5 %collective-permute-start.16 = (bf16[32,128]{1,0:T(8,128)(2,1)S(1)}, bf16[32,128]{1,0:T(8,128)(2,1)S(1)}, u32[]{:S(2)}, u32[]{:S(2)}) collective-permute-start(bf16[32,128]{1,0:T(8,128)(2,1)S(1)} %get-tuple-element.151.mix_ref), channel_id=1, source_target_pairs={{96,97},{97,96},{98,99},{99,98},{100,101},{101,100},{102,103},{103... | collective-permute-start | bytes 24584 | tf_op jit(solution)/shard_map/ppermute | solution.py:34

commit v6 on v4

--- a/solution.py
+++ b/solution.py
@@ -11,6 +11,7 @@
 BLK = 256
 VM = pl.BlockSpec(memory_space=pltpu.VMEM)
 SM = pl.BlockSpec(memory_space=pltpu.SMEM)
+DOWN_PARTS = 7
 F32 = jnp.float32
 BF16 = jnp.bfloat16
 
@@ -159,8 +160,8 @@
         act_ref[:, n * 256 + hidden : n * 256 + hidden + 256] = pltpu.roll(act, 4, 0).astype(BF16)
     first = act_ref[:, :hidden]
     second = act_ref[:, hidden:]
-    wide = half // 2
-    for n in range(2):
+    wide = half // DOWN_PARTS
+    for n in range(DOWN_PARTS):
         cols = slice(n * wide, n * wide + wide)
         rest = slice(half + n * wide, half + n * wide + wide)
         arrived(hidden // 128 + n)
@@ -185,13 +186,13 @@
                  out_ref, load_ref, gate_ref, up_ref, down_ref, act_ref, sems):
     half = out_ref.shape[1]
     hidden = gate_ref.shape[1]
-    wide = half // 2
+    wide = half // DOWN_PARTS
     steps = []
     for n in range(hidden // 256):
         cols = slice(n * 256, n * 256 + 256)
         steps.append([(gate_hbm, gate_ref, cols)])
         steps.append([(up_hbm, up_ref, cols)])
-    for n in range(2):
+    for n in range(DOWN_PARTS):
         steps.append(
             [(down_hbm, down_ref, slice(c + n * wide, c + n * wide + wide)) for c in (0, half)]
         )
@@ -295,7 +296,7 @@
             + [pltpu.VMEM(w.shape, w.dtype) for w in weights],
             in_specs=[VM, VM] + [HB] * 3,
             out_specs=[VM] * 5,
-            scratch_shapes=[act_shape, pltpu.SemaphoreType.DMA((8,))],
+            scratch_shapes=[act_shape, pltpu.SemaphoreType.DMA((2 * hidden // 256 + 2 * DOWN_PARTS,))],
             compiler_params=params(12),
             name="first",
         )(info, rows, *map(outside, weights))

time: 465 us -> 465 us (level)
  no operation moved by 1% of the time
where the time goes in v6:
time: 465 us; the launch traced here: 457 us
  blocking collectives  359 us (77%)
  Pallas kernels  39 us (8%)
  waiting for transfers between devices  37.7 us (8%)
  starting transfers between devices  18.2 us (4%)
    all_to_all x22, blocking collectives, exchange(): return lax.all_to_all(block, 'ep', split_axis=0, concat_axis=0, tiled=True)  359 us
    ppermute x10, waiting for transfers between devices, live_hop(): return lax.ppermute(block, axis, route)  34.7 us
    pallas_call x10, Pallas kernels, experts(): pl.pallas_call(functools.partial(expert_kernel, tick, micro_count), out_s...  16.5 us
    ppermute x10, starting transfers between devices, live_hop(): return lax.ppermute(block, axis, route)  11.7 us
    pallas_call x11, Pallas kernels, pre(): pl.pallas_call(functools.partial(pre_kernel, tick), out_shape=out_shape,...  10.4 us
  transfers between devices with their start and end apart: 17, of which 6 were waited for; matrix products, arithmetic and copies ran while one was open for 0% of the time, Pallas kernels for 0%

profile of v6, /device:TPU:24, one launch (start us, length us, event | category | flops | bytes accessed | tf_op | source)
XLA Modules:
  0.0 457.1 jit_solution(8580004390403886384)
XLA Ops:
  1.3 2.0 pre.11
  3.3 23.8 %all_to_all.242 = bf16[16,8,3712]{2,1,0:T(8,128)(2,1)S(1)} all-to-all(bf16[16,8,3712]{2,1,0:T(8,128)(2,1)S(1)} %bitcast.99), channel_id=1, replica_groups=mesh['section'=8,'ep'=16] {'ep'}, dimensions={0} | all-to-all | bytes 1900544 | tf_op jit(solution)/shard_map/all_to_all | solution.py:327
  27.1 8.7 %first.1 = (bf16[128,3584]{1,0:T(8,128)(2,1)S(1)}, f32[1,128]{1,0:T(1,128)}, bf16[7168,512]{1,0:T(8,128)(2,1)S(1)}, bf16[7168,512]{1,0:T(8,128)(2,1)S(1)}, bf16[512,7168]{1,0:T(8,128)(2,1)S(1)}) custom-call(f32[2,128]{1,0:T(2,128)S(1)} %get-tuple-element.82.info_ref, bf16[128,3712]{1,0:T(8,128)(2,1)S(1)} %bitcast.67, bf16[7168,512]{1,0:T(8,128)(2,1)} %bitcast.122, ...), custom_call_target="tpu_custom_call" | custom-call | tf_op jit(solution)/shard_map/first/pallas_call | solution.py:293
  35.8 18.2 %all_to_all.243 = bf16[16,8,3584]{2,1,0:T(8,128)(2,1)S(1)} all-to-all(bf16[16,8,3584]{2,1,0:T(8,128)(2,1)S(1)} %bitcast.100), channel_id=1, replica_groups=mesh['section'=8,'ep'=16] {'ep'}, dimensions={0} | all-to-all | bytes 1835008 | tf_op jit(solution)/shard_map/all_to_all | solution.py:327
  55.7 0.9 pre.12
  56.5 16.8 %all_to_all.244 = bf16[16,8,3584]{2,1,0:T(8,128)(2,1)S(1)} all-to-all(bf16[16,8,3584]{2,1,0:T(8,128)(2,1)S(1)} %bitcast.102), channel_id=1, replica_groups=mesh['section'=8,'ep'=16] {'ep'}, dimensions={0} | all-to-all | bytes 1835008 | tf_op jit(solution)/shard_map/all_to_all | solution.py:327
  73.3 15.7 %all_to_all.245 = bf16[16,8,3584]{2,1,0:T(8,128)(2,1)S(1)} all-to-all(bf16[16,8,3584]{2,1,0:T(8,128)(2,1)S(1)} %bitcast.82), channel_id=1, replica_groups=mesh['section'=8,'ep'=16] {'ep'}, dimensions={0} | all-to-all | bytes 1835008 | tf_op jit(solution)/shard_map/all_to_all | solution.py:327
  90.6 0.9 pre.13
  91.5 15.0 %all_to_all.246 = bf16[16,8,3584]{2,1,0:T(8,128)(2,1)S(1)} all-to-all(bf16[16,8,3584]{2,1,0:T(8,128)(2,1)S(1)} %bitcast.103), channel_id=1, replica_groups=mesh['section'=8,'ep'=16] {'ep'}, dimensions={0} | all-to-all | bytes 1835008 | tf_op jit(solution)/shard_map/all_to_all | solution.py:327
  107.0 15.1 %all_to_all.247 = bf16[16,8,3584]{2,1,0:T(8,128)(2,1)S(1)} all-to-all(bf16[16,8,3584]{2,1,0:T(8,128)(2,1)S(1)} %bitcast.84), channel_id=1, replica_groups=mesh['section'=8,'ep'=16] {'ep'}, dimensions={0} | all-to-all | bytes 1835008 | tf_op jit(solution)/shard_map/all_to_all | solution.py:327
  123.7 0.9 pre.14
  124.6 15.4 %all_to_all.248 = bf16[16,8,3584]{2,1,0:T(8,128)(2,1)S(1)} all-to-all(bf16[16,8,3584]{2,1,0:T(8,128)(2,1)S(1)} %bitcast.104), channel_id=1, replica_groups=mesh['section'=8,'ep'=16] {'ep'}, dimensions={0} | all-to-all | bytes 1835008 | tf_op jit(solution)/shard_map/all_to_all | solution.py:327
  140.0 14.9 %all_to_all.249 = bf16[16,8,3584]{2,1,0:T(8,128)(2,1)S(1)} all-to-all(bf16[16,8,3584]{2,1,0:T(8,128)(2,1)S(1)} %bitcast.86), channel_id=1, replica_groups=mesh['section'=8,'ep'=16] {'ep'}, dimensions={0} | all-to-all | bytes 1835008 | tf_op jit(solution)/shard_map/all_to_all | solution.py:327
  156.5 0.8 pre.15
  157.3 16.2 %all_to_all.250 = bf16[16,8,3584]{2,1,0:T(8,128)(2,1)S(1)} all-to-all(bf16[16,8,3584]{2,1,0:T(8,128)(2,1)S(1)} %bitcast.105), channel_id=1, replica_groups=mesh['section'=8,'ep'=16] {'ep'}, dimensions={0} | all-to-all | bytes 1835008 | tf_op jit(solution)/shard_map/all_to_all | solution.py:327
  173.5 16.6 %all_to_all.251 = bf16[16,8,3584]{2,1,0:T(8,128)(2,1)S(1)} all-to-all(bf16[16,8,3584]{2,1,0:T(8,128)(2,1)S(1)} %bitcast.88), channel_id=1, replica_groups=mesh['section'=8,'ep'=16] {'ep'}, dimensions={0} | all-to-all | bytes 1835008 | tf_op jit(solution)/shard_map/all_to_all | solution.py:327
  191.0 0.8 pre.16
  191.9 20.2 %all_to_all.252 = bf16[16,8,3584]{2,1,0:T(8,128)(2,1)S(1)} all-to-all(bf16[16,8,3584]{2,1,0:T(8,128)(2,1)S(1)} %bitcast.108), channel_id=1, replica_groups=mesh['section'=8,'ep'=16] {'ep'}, dimensions={0} | all-to-all | bytes 1835008 | tf_op jit(solution)/shard_map/all_to_all | solution.py:327
  212.0 19.2 %all_to_all.253 = bf16[16,8,3584]{2,1,0:T(8,128)(2,1)S(1)} all-to-all(bf16[16,8,3584]{2,1,0:T(8,128)(2,1)S(1)} %bitcast.90), channel_id=1, replica_groups=mesh['section'=8,'ep'=16] {'ep'}, dimensions={0} | all-to-all | bytes 1835008 | tf_op jit(solution)/shard_map/all_to_all | solution.py:327
  231.5 1.3 collective-permute-start.9
  232.8 17.5 %collective-permute-done.9.refs_5_ = bf16[8,7168]{1,0:T(8,128)(2,1)S(1)} collective-permute-done((bf16[8,7168]{1,0:T(8,128)(2,1)S(1)}, bf16[8,7168]{1,0:T(8,128)(2,1)S(1)}, u32[]{:S(2)}, u32[]{:S(2)}) %collective-permute-start.9) | collective-permute-done | bytes 114720 | tf_op jit(solution)/shard_map/ppermute | solution.py:22
  251.8 15.2 %all_to_all.254 = bf16[16,8,3584]{2,1,0:T(8,128)(2,1)S(1)} all-to-all(bf16[16,8,3584]{2,1,0:T(8,128)(2,1)S(1)} %bitcast.106), channel_id=1, replica_groups=mesh['section'=8,'ep'=16] {'ep'}, dimensions={0} | all-to-all | bytes 1835008 | tf_op jit(solution)/shard_map/all_to_all | solution.py:327
  267.0 3.2 experts.15
  270.2 15.1 %all_to_all.255 = bf16[16,8,3584]{2,1,0:T(8,128)(2,1)S(1)} all-to-all(bf16[16,8,3584]{2,1,0:T(8,128)(2,1)S(1)} %bitcast.92), channel_id=1, replica_groups=mesh['section'=8,'ep'=16] {'ep'}, dimensions={0} | all-to-all | bytes 1835008 | tf_op jit(solution)/shard_map/all_to_all | solution.py:327
  285.5 1.9 collective-permute-start.11
  287.5 5.0 %collective-permute-done.11.refs_5_ = bf16[8,7168]{1,0:T(8,128)(2,1)S(1)} collective-permute-done((bf16[8,7168]{1,0:T(8,128)(2,1)S(1)}, bf16[8,7168]{1,0:T(8,128)(2,1)S(1)}, u32[]{:S(2)}, u32[]{:S(2)}) %collective-permute-start.11) | collective-permute-done | bytes 114720 | tf_op jit(solution)/shard_map/ppermute | solution.py:22
  293.3 15.2 %all_to_all.256 = bf16[16,8,3584]{2,1,0:T(8,128)(2,1)S(1)} all-to-all(bf16[16,8,3584]{2,1,0:T(8,128)(2,1)S(1)} %bitcast.109), channel_id=1, replica_groups=mesh['section'=8,'ep'=16] {'ep'}, dimensions={0} | all-to-all | bytes 1835008 | tf_op jit(solution)/shard_map/all_to_all | solution.py:327
  308.5 3.4 experts.16
  311.9 15.1 %all_to_all.257 = bf16[16,8,3584]{2,1,0:T(8,128)(2,1)S(1)} all-to-all(bf16[16,8,3584]{2,1,0:T(8,128)(2,1)S(1)} %bitcast.94), channel_id=1, replica_groups=mesh['section'=8,'ep'=16] {'ep'}, dimensions={0} | all-to-all | bytes 1835008 | tf_op jit(solution)/shard_map/all_to_all | solution.py:327
  327.2 1.9 collective-permute-start.12
  329.1 7.1 %collective-permute-done.12.refs_5_ = bf16[8,7168]{1,0:T(8,128)(2,1)S(1)} collective-permute-done((bf16[8,7168]{1,0:T(8,128)(2,1)S(1)}, bf16[8,7168]{1,0:T(8,128)(2,1)S(1)}, u32[]{:S(2)}, u32[]{:S(2)}) %collective-permute-start.12) | collective-permute-done | bytes 114720 | tf_op jit(solution)/shard_map/ppermute | solution.py:22
  336.8 0.8 pre.19
  337.7 14.9 %all_to_all.258 = bf16[16,8,3584]{2,1,0:T(8,128)(2,1)S(1)} all-to-all(bf16[16,8,3584]{2,1,0:T(8,128)(2,1)S(1)} %bitcast.107), channel_id=1, replica_groups=mesh['section'=8,'ep'=16] {'ep'}, dimensions={0} | all-to-all | bytes 1835008 | tf_op jit(solution)/shard_map/all_to_all | solution.py:327
  352.6 3.2 experts.17
  355.8 15.1 %all_to_all.259 = bf16[16,8,3584]{2,1,0:T(8,128)(2,1)S(1)} all-to-all(bf16[16,8,3584]{2,1,0:T(8,128)(2,1)S(1)} %bitcast.96), channel_id=1, replica_groups=mesh['section'=8,'ep'=16] {'ep'}, dimensions={0} | all-to-all | bytes 1835008 | tf_op jit(solution)/shard_map/all_to_all | solution.py:327
  371.1 1.9 collective-permute-start.14
  373.0 4.2 collective-permute-done.14.refs_5_
  378.1 16.0 %all_to_all.260 = bf16[16,8,3584]{2,1,0:T(8,128)(2,1)S(1)} all-to-all(bf16[16,8,3584]{2,1,0:T(8,128)(2,1)S(1)} %bitcast.110), channel_id=1, replica_groups=mesh['section'=8,'ep'=16] {'ep'}, dimensions={0} | all-to-all | bytes 1835008 | tf_op jit(solution)/shard_map/all_to_all | solution.py:327
  394.1 3.2 experts.18
  397.3 15.5 %all_to_all.261 = bf16[16,8,3584]{2,1,0:T(8,128)(2,1)S(1)} all-to-all(bf16[16,8,3584]{2,1,0:T(8,128)(2,1)S(1)} %bitcast.98), channel_id=1, replica_groups=mesh['section'=8,'ep'=16] {'ep'}, dimensions={0} | all-to-all | bytes 1835008 | tf_op jit(solution)/shard_map/all_to_all | solution.py:327
  413.0 1.3 collective-permute-start.15
  414.3 0.9 collective-permute-done.15.refs_5_
  415.3 2.5 collective-permute-start.16
  417.8 3.0 collective-permute-done.16.refs_6_
  421.6 15.1 %all_to_all.262 = bf16[16,8,3584]{2,1,0:T(8,128)(2,1)S(1)} all-to-all(bf16[16,8,3584]{2,1,0:T(8,128)(2,1)S(1)} %bitcast.101), channel_id=1, replica_groups=mesh['section'=8,'ep'=16] {'ep'}, dimensions={0} | all-to-all | bytes 1835008 | tf_op jit(solution)/shard_map/all_to_all | solution.py:327
  436.7 3.2 experts.19
  439.9 15.2 %all_to_all.263 = bf16[16,8,3584]{2,1,0:T(8,128)(2,1)S(1)} all-to-all(bf16[16,8,3584]{2,1,0:T(8,128)(2,1)S(1)} %bitcast.80), channel_id=1, replica_groups=mesh['section'=8,'ep'=16] {'ep'}, dimensions={0} | all-to-all | bytes 1835008 | tf_op jit(solution)/shard_map/all_to_all | solution.py:327
  455.0 0.9 post.21
  (50 shorter events, 14.3 us)
Async XLA Ops:
  27.1 28.5 %copy-start = (bf16[4,8,7168]{2,1,0:T(8,128)(2,1)S(1)}, bf16[4,8,7168]{2,1,0:T(8,128)(2,1)}, u32[]{:S(2)}) copy-start(bf16[4,8,7168]{2,1,0:T(8,128)(2,1)} %refs_0_.20) | copy-start | bytes 1376260
  27.1 28.5 %copy-start.1 = (bf16[1,7168,8]{1,2,0:T(8,128)(2,1)S(1)}, bf16[1,7168,8]{1,2,0:T(8,128)(2,1)}, u32[]{:S(2)}) copy-start(bf16[1,7168,8]{1,2,0:T(8,128)(2,1)} %param.12) | copy-start | bytes 344068
  27.1 28.5 %copy-start.2 = (f32[1,7168]{1,0:T(1,128)S(1)}, f32[1,7168]{1,0:T(1,128)}, u32[]{:S(2)}) copy-start(f32[1,7168]{1,0:T(1,128)} %refs_1_.21) | copy-start | bytes 86020
  27.1 28.5 %copy-start.3 = (s32[1,4,8,2]{2,3,1,0:T(2,128)S(1)}, s32[1,4,8,2]{2,3,1,0:T(2,128)}, u32[]{:S(2)}) copy-start(s32[1,4,8,2]{2,3,1,0:T(2,128)} %param.9) | copy-start | bytes 772
  54.2 0.7 collective-permute-start
  54.9 0.7 collective-permute-start.1
  89.3 0.7 collective-permute-start.2
  90.0 0.7 collective-permute-start.3
  122.3 0.7 collective-permute-start.4
  123.0 0.7 collective-permute-start.5
  155.1 0.7 collective-permute-start.6
  155.8 0.7 collective-permute-start.7
  190.3 0.7 collective-permute-start.8
  231.5 18.8 %collective-permute-start.9 = (bf16[8,7168]{1,0:T(8,128)(2,1)S(1)}, bf16[8,7168]{1,0:T(8,128)(2,1)S(1)}, u32[]{:S(2)}, u32[]{:S(2)}) collective-permute-start(bf16[8,7168]{1,0:T(8,128)(2,1)S(1)} %get-tuple-element.123), channel_id=1, source_target_pairs={{32,48},{48,64},{64,80},{80,96},{33,49},{49,65},{65,81},{81,97},{3... | collective-permute-start | bytes 344072 | tf_op jit(solution)/shard_map/ppermute | solution.py:22
  250.3 0.7 collective-permute-start.10
  285.5 6.9 %collective-permute-start.11 = (bf16[8,7168]{1,0:T(8,128)(2,1)S(1)}, bf16[8,7168]{1,0:T(8,128)(2,1)S(1)}, u32[]{:S(2)}, u32[]{:S(2)}) collective-permute-start(bf16[8,7168]{1,0:T(8,128)(2,1)S(1)} %get-tuple-element.130), channel_id=1, source_target_pairs={{48,64},{64,80},{80,96},{96,112},{49,65},{65,81},{81,97},{97,113},... | collective-permute-start | bytes 344072 | tf_op jit(solution)/shard_map/ppermute | solution.py:22
  327.2 9.0 %collective-permute-start.12 = (bf16[8,7168]{1,0:T(8,128)(2,1)S(1)}, bf16[8,7168]{1,0:T(8,128)(2,1)S(1)}, u32[]{:S(2)}, u32[]{:S(2)}) collective-permute-start(bf16[8,7168]{1,0:T(8,128)(2,1)S(1)} %get-tuple-element.136), channel_id=1, source_target_pairs={{64,80},{80,96},{96,112},{65,81},{81,97},{97,113},{66,82},{82,98},... | collective-permute-start | bytes 344072 | tf_op jit(solution)/shard_map/ppermute | solution.py:22
  336.2 0.7 collective-permute-start.13
  371.1 6.1 %collective-permute-start.14 = (bf16[8,7168]{1,0:T(8,128)(2,1)S(1)}, bf16[8,7168]{1,0:T(8,128)(2,1)S(1)}, u32[]{:S(2)}, u32[]{:S(2)}) collective-permute-start(bf16[8,7168]{1,0:T(8,128)(2,1)S(1)} %get-tuple-element.143), channel_id=1, source_target_pairs={{80,96},{96,112},{81,97},{97,113},{82,98},{98,114},{83,99},{99,115... | collective-permute-start | bytes 344072 | tf_op jit(solution)/shard_map/ppermute | solution.py:22
  413.0 2.2 collective-permute-start.15
  415.3 5.5 %collective-permute-start.16 = (bf16[32,128]{1,0:T(8,128)(2,1)S(1)}, bf16[32,128]{1,0:T(8,128)(2,1)S(1)}, u32[]{:S(2)}, u32[]{:S(2)}) collective-permute-start(bf16[32,128]{1,0:T(8,128)(2,1)S(1)} %get-tuple-element.151.mix_ref), channel_id=1, source_target_pairs={{96,97},{97,96},{98,99},{99,98},{100,101},{101,100},{102,103},{103... | collective-permute-start | bytes 24584 | tf_op jit(solution)/shard_map/ppermute | solution.py:35
